TPU v7x, 256 devices: a whole 4x4x8 slice. The times are simulated.
256 devices in a mesh: gx: 64 (over z, y, core), gy: 4 (over x).
Axes of the slice: x: 4, y: 4, z: 8, core: 2. Of those that a mesh axis runs over, the one named last changes fastest.
Arguments:
- latent: float32 [512, 32, 4, 256], P('gx', 'gy'), may hold values from -6 to 6
- active: int32 [128, 8, 1], P('gx', 'gy'), may hold values from 0 to 1, as said below
- parent_owner: int32 [64, 4, 4, 4], P('gx', 'gy'), may hold values from 0 to 63, all different within a row; in each aligned block of 4 rows (0 to 3, 4 to 7, ..., all dimensions but the last counted through in order) at most 2 rows name the same one
- parent_slot: int32 [64, 4, 4, 4], P('gx', 'gy'), may hold values from 0 to 3
- coarse_kv: bfloat16 [256, 128, 512], P('gx')
- norm_gain: float32 [256], replicated, may hold values from 0.5 to 1.5
- conv_weight: bfloat16 [27, 256, 256], replicated, may hold values from -0.078125 to 0.078125
- conv_bias: float32 [256], replicated, may hold values from -3 to 3
- attn_gain: float32 [256], replicated, may hold values from 0.1 to 1.9
- q_weight: bfloat16 [256, 256], replicated, may hold values from -0.375 to 0.375
- out_weight: bfloat16 [256, 256], replicated, may hold values from -1.5 to 1.5
Outputs:
- denoised: float32 [512, 32, 4, 256], P('gx', 'gy')
Inputs may be any that keep to these rules, and one draw needn't show every extreme that they name: `active`: active blocks of one device: at least one eighth of 4, and never fewer than one; at most 3, and some device has exactly 3. `parent_owner`: the 4 owners of one window are distinct; among the windows of one device no owner is named by more than 2 windows, and some device names some owner exactly 2 times.
All inputs are finite; a program needn't handle non-finite values.
Results may differ from a plain program's by a relative error of at most 0.03.
The roundings to bfloat16 on the way count: a program that leaves them out, or rounds other values in their place, can miss the bound.
Values may be sent and summed in bfloat16 or wider, within the bound.
No kernel may reach another device: no remote copies, remote signals or barrier semaphores. Data moves between devices by JAX's collectives and lax.ppermute only.
A program may use at most 128 MiB of HBM per device.

v0:
```python
import math

import jax
import jax.numpy as jnp
from jax import lax
from jax.sharding import PartitionSpec as P

HEADS = 8


def padded(block, sides, width):
    for axis, dim in sides:
        count = lax.axis_size(axis)
        forward = [(i, i + 1) for i in range(count - 1)]
        backward = [(target, source) for source, target in forward]
        low = lax.ppermute(
            lax.slice_in_dim(block, block.shape[dim] - width, None, axis=dim), axis, forward
        )
        high = lax.ppermute(lax.slice_in_dim(block, 0, width, axis=dim), axis, backward)
        block = jnp.concatenate([low, block, high], axis=dim)
    return block


def rms_scale(values):
    return lax.rsqrt(jnp.mean(values * values, axis=-1, keepdims=True) + 1e-06)


def attend_part(queries, kv_rows):
    members, per_window, channels = queries.shape
    head_dim = channels // HEADS
    q_heads = queries.reshape(members, per_window, HEADS, head_dim)
    k_heads = kv_rows[:, :, :channels].reshape(members, -1, HEADS, head_dim)
    v_heads = kv_rows[:, :, channels:].reshape(members, -1, HEADS, head_dim)
    scores = jnp.einsum(
        "nqhd,nkhd->nhqk", q_heads, k_heads, preferred_element_type=jnp.float32
    ) / math.sqrt(head_dim)
    peaks = jnp.max(scores, axis=-1)
    lifted = jnp.exp(scores - peaks[..., None])
    totals = jnp.sum(lifted, axis=-1)
    sums = jnp.einsum(
        "nhqk,nkhd->nqhd", lifted.astype(jnp.bfloat16), v_heads, preferred_element_type=jnp.float32
    )
    return (
        sums.reshape(members, per_window, channels),
        peaks.transpose(0, 2, 1),
        totals.transpose(0, 2, 1),
    )


def per_device(
    latent,
    active,
    parent_owner,
    parent_slot,
    coarse_kv,
    norm_gain,
    conv_weight,
    conv_bias,
    attn_gain,
    q_weight,
    out_weight,
):
    vox_x, vox_y, vox_z, channels = latent.shape
    blk_x, blk_y, blk_z = active.shape
    edge_len = vox_x // blk_x
    windows = blk_x * blk_y * blk_z
    per_window = edge_len**3
    fan_out = parent_owner.shape[-1]
    head_dim = channels // HEADS
    voxel_mask = jnp.repeat(
        jnp.repeat(jnp.repeat(active.astype(jnp.float32), edge_len, 0), edge_len, 1), edge_len, 2
    )[..., None]
    normed = (voxel_mask * latent * rms_scale(latent) * norm_gain).astype(jnp.bfloat16)
    framed = padded(normed, (("gx", 0), ("gy", 1)), 1)
    framed = jnp.pad(framed, ((0, 0), (0, 0), (1, 1), (0, 0)))
    conv_sum = jnp.zeros((vox_x * vox_y * vox_z, channels), jnp.float32)
    for offset in range(27):
        shift_x, shift_y, shift_z = (offset // 9, offset // 3 % 3, offset % 3)
        shifted = framed[
            shift_x : shift_x + vox_x, shift_y : shift_y + vox_y, shift_z : shift_z + vox_z
        ].reshape(-1, channels)
        conv_sum = conv_sum + jnp.dot(
            shifted, conv_weight[offset], preferred_element_type=jnp.float32
        )
    conv_sum = conv_sum.reshape(vox_x, vox_y, vox_z, channels)
    conv_sum = conv_sum + conv_bias
    hidden = latent + voxel_mask * jax.nn.silu(conv_sum)
    query_in = (hidden * rms_scale(hidden) * attn_gain).astype(jnp.bfloat16)
    queries = jnp.dot(
        query_in.reshape(-1, channels), q_weight, preferred_element_type=jnp.float32
    ).astype(jnp.bfloat16)
    shaped = queries.reshape(vox_x, vox_y, vox_z, channels).reshape(
        blk_x, edge_len, blk_y, edge_len, blk_z, edge_len, channels
    )
    window_queries = shaped.transpose(0, 2, 4, 1, 3, 5, 6).reshape(windows, per_window, channels)
    owners = parent_owner.reshape(-1)
    region_slots = parent_slot.reshape(-1)
    gx_count = lax.axis_size("gx")
    capacity = max(2, (windows * fan_out + gx_count - 1) // gx_count + 1)
    owner_hit = (owners[:, None] == jnp.arange(gx_count, dtype=jnp.int32)[None, :]).astype(
        jnp.int32
    )
    ranking = jnp.sum(owner_hit * jnp.cumsum(owner_hit, axis=0), axis=1) - 1
    cells = owners * capacity + ranking
    cell_hit = (cells[:, None] == jnp.arange(gx_count * capacity, dtype=jnp.int32)[None, :]).astype(
        jnp.int32
    )
    table = jnp.sum(cell_hit * region_slots[:, None], axis=0).reshape(gx_count, capacity)
    cell_grid = cells.reshape(windows, fan_out)
    picked = coarse_kv[lax.all_to_all(table, "gx", split_axis=0, concat_axis=0, tiled=True)]
    arrived = lax.all_to_all(picked, "gx", split_axis=0, concat_axis=0, tiled=True)
    arrived = arrived.reshape(gx_count * capacity, arrived.shape[2], arrived.shape[3])
    pieces = [
        attend_part(window_queries, arrived[cell_grid[:, parent]]) for parent in range(fan_out)
    ]
    peak_stack = jnp.stack([piece[1] for piece in pieces])
    highest = jnp.max(peak_stack, axis=0)
    factors = jnp.exp(peak_stack - highest[None])
    sums_all = jnp.zeros((windows, per_window, HEADS, head_dim), jnp.float32)
    totals_all = jnp.zeros((windows, per_window, HEADS), jnp.float32)
    for parent in range(fan_out):
        sums_all = (
            sums_all
            + pieces[parent][0].reshape(windows, per_window, HEADS, head_dim)
            * factors[parent][..., None]
        )
        totals_all = totals_all + pieces[parent][2] * factors[parent]
    mixed = (
        (sums_all / totals_all[..., None])
        .reshape(windows, per_window, channels)
        .astype(jnp.bfloat16)
    )
    shaped = mixed.reshape(blk_x, blk_y, blk_z, edge_len, edge_len, edge_len, channels)
    attended = (
        shaped.transpose(0, 3, 1, 4, 2, 5, 6)
        .reshape(vox_x, vox_y, vox_z, channels)
        .reshape(-1, channels)
    )
    projected = jnp.dot(attended, out_weight, preferred_element_type=jnp.float32).reshape(
        vox_x, vox_y, vox_z, channels
    )
    return voxel_mask * (hidden + projected)


def solution(mesh):
    placed = (
        P("gx", "gy", None, None),
        P("gx", "gy", None),
        P("gx", "gy", None, None),
        P("gx", "gy", None, None),
        P("gx", None, None),
        P(),
        P(),
        P(),
        P(),
        P(),
        P(),
    )
    return jax.shard_map(
        per_device, mesh=mesh, in_specs=placed, out_specs=P("gx", "gy", None, None), check_vma=False
    )
```

profile of v0, /device:TPU:31, one launch (start us, length us, event | category | flops | bytes accessed | tf_op | source)
XLA Modules:
  0.0 489.8 jit_solution(1866052863683023393)
XLA Ops:
  2.1 19.6 %all_to_all.17 = s32[64,1,2]{2,1,0:T(1,128)S(1)} all-to-all(s32[64,1,2]{2,1,0:T(1,128)S(1)} %bitcast.255), channel_id=1, replica_groups=mesh['gx'=64,'gy'=4] {'gx'}, dimensions={0} | all-to-all | bytes 1024 | tf_op jit(solution)/shard_map/all_to_all | solution.py:110
  22.1 7.8 %gather_fusion = bf16[128,128,512]{2,1,0:T(8,128)(2,1)} fusion(bf16[4,128,512]{2,1,0:T(8,128)(2,1)S(1)} %copy-done, s32[1024]{0:T(1024)S(1)} %pad_clamp_fusion.4), kind=kCustom, calls=%fused_computation | custom fusion | bytes 33554944 | tf_op jit(solution)/shard_map/gather | solution.py:110
  29.8 8.0 %all-to-all-start.1 = ((bf16[64,2,128,512]{3,2,1,0:T(8,128)(2,1)}), bf16[64,2,128,512]{3,2,1,0:T(8,128)(2,1)}, u32[]{:S(2)}, u32[]{:S(2)}) async-start(bf16[64,2,128,512]{3,2,1,0:T(8,128)(2,1)} %bitcast.239), calls=%async_computation.1 | async-start | bytes 33554432 | tf_op jit(solution)/shard_map/all_to_all | solution.py:111
  38.7 2.3 collective-permute-start.1
  40.9 5.4 %collective-permute-start = (bf16[1,8,4,256]{3,1,2,0:T(8,128)(2,1)S(1)}, bf16[1,8,4,256]{3,1,2,0:T(8,128)(2,1)S(1)}, u32[]{:S(2)}, u32[]{:S(2)}) collective-permute-start(bf16[1,8,4,256]{3,1,2,0:T(8,128)(2,1)S(1)} %get-tuple-element.49), channel_id=1, source_target_pairs={{0,4},{4,8},{8,12},{12,16},{16,20},{20,24},{24,28},{28,32},{32,36}... | collective-permute-start | bytes 49160 | tf_op jit(solution)/shard_map/ppermute | solution.py:16
  47.4 360.9 %collective-permute-done.1 = bf16[1,8,4,256]{3,1,2,0:T(8,128)(2,1)S(1)} collective-permute-done((bf16[1,8,4,256]{3,1,2,0:T(8,128)(2,1)S(1)}, bf16[1,8,4,256]{3,1,2,0:T(8,128)(2,1)S(1)}, u32[]{:S(2)}, u32[]{:S(2)}) %collective-permute-start.1) | collective-permute-done | bytes 16416 | tf_op jit(solution)/shard_map/ppermute | solution.py:19
  408.3 2.4 collective-permute-start.3
  410.7 1.5 collective-permute-start.2
  413.1 2.4 collective-permute-done.2
  427.8 1.2 fusion.59
  429.1 1.1 convolution_add_fusion.26
  430.2 1.1 convolution_add_fusion.25
  431.4 1.1 convolution_add_fusion.24
  432.5 1.1 convolution_add_fusion.23
  433.6 1.1 convolution_add_fusion.22
  434.7 1.1 convolution_add_fusion.21
  435.9 1.1 convolution_add_fusion.20
  437.0 1.1 convolution_add_fusion.19
  443.3 6.5 %gather_fusion.4 = bf16[4,128,512]{2,1,0:T(8,128)(2,1)S(1)} fusion(bf16[128,128,512]{2,1,0:T(8,128)(2,1)} %bitcast.32, s32[1024]{0:T(1024)} %get-tuple-element.68), kind=kCustom, calls=%fused_computation.4 | custom fusion | bytes 1048592 | tf_op jit(solution)/shard_map/gather | solution.py:114
  450.2 6.4 %gather_fusion.3 = bf16[4,128,512]{2,1,0:T(8,128)(2,1)S(1)} fusion(bf16[128,128,512]{2,1,0:T(8,128)(2,1)} %bitcast.32, s32[1024]{0:T(1024)S(1)} %get-tuple-element.69), kind=kCustom, calls=%fused_computation.3 | custom fusion | bytes 1048592 | tf_op jit(solution)/shard_map/gather | solution.py:114
  458.6 6.3 %gather_fusion.2 = bf16[4,128,512]{2,1,0:T(8,128)(2,1)S(1)} fusion(bf16[128,128,512]{2,1,0:T(8,128)(2,1)} %bitcast.32, s32[1024]{0:T(1024)S(1)} %get-tuple-element.70), kind=kCustom, calls=%fused_computation.2 | custom fusion | bytes 1048592 | tf_op jit(solution)/shard_map/gather | solution.py:114
  465.0 0.8 fusion.101
  465.8 1.1 copy.335
  466.9 1.3 fusion.110
  468.3 6.3 %gather_fusion.1 = bf16[4,128,512]{2,1,0:T(8,128)(2,1)S(1)} fusion(bf16[128,128,512]{2,1,0:T(8,128)(2,1)} %bitcast.32, s32[1024]{0:T(1024)S(1)} %get-tuple-element.71), kind=kCustom, calls=%fused_computation.1 | custom fusion | bytes 1048592 | tf_op jit(solution)/shard_map/gather | solution.py:114
  475.4 1.1 copy.333
  476.6 1.3 fusion.111
  478.5 1.1 copy.342
  479.7 1.1 copy.341
  480.8 1.1 copy.328
  483.3 1.9 fusion.13
  485.2 0.9 fusion.11
  (210 shorter events, 30.9 us)
Async XLA Ops:
  0.0 22.0 %copy-start = (bf16[4,128,512]{2,1,0:T(8,128)(2,1)S(1)}, bf16[4,128,512]{2,1,0:T(8,128)(2,1)}, u32[]{:S(2)}) copy-start(bf16[4,128,512]{2,1,0:T(8,128)(2,1)} %param.15) | copy-start | bytes 1572868
  29.8 8.0 %copy-start.5 = (f32[8,8,4,256]{3,2,1,0:T(4,128)S(1)}, f32[8,8,4,256]{3,2,1,0:T(4,128)}, u32[]{:S(2)}) copy-start(f32[8,8,4,256]{3,2,1,0:T(4,128)} %param.11) | copy-start | bytes 786436
  29.8 8.3 %copy-start.31 = (s32[2,2,1]{1,2,0:T(1,128)S(1)}, s32[2,2,1]{1,2,0:T(1,128)}, u32[]{:S(2)}) copy-start(s32[2,2,1]{1,2,0:T(1,128)} %param.12) | copy-start | bytes 52
  29.8 8.7 %copy-start.28 = (f32[256]{0:T(256)S(1)}, f32[256]{0:T(256)}, u32[]{:S(2)}) copy-start(f32[256]{0:T(256)} %param.16) | copy-start | bytes 3076
  29.8 16.6 %copy-start.27 = (s32[1,1,4,4]{3,2,1,0:T(4,128)S(1)}, s32[1,1,4,4]{3,2,1,0:T(4,128)}, u32[]{:S(2)}) copy-start(s32[1,1,4,4]{3,2,1,0:T(4,128)} %param.13) | copy-start | bytes 196
  29.8 413.5 %all-to-all-start.1 = ((bf16[64,2,128,512]{3,2,1,0:T(8,128)(2,1)}), bf16[64,2,128,512]{3,2,1,0:T(8,128)(2,1)}, u32[]{:S(2)}, u32[]{:S(2)}) async-start(bf16[64,2,128,512]{3,2,1,0:T(8,128)(2,1)} %bitcast.239), calls=%async_computation.1 | async-start | bytes 33554432 | tf_op jit(solution)/shard_map/all_to_all | solution.py:111
  38.7 369.6 %collective-permute-start.1 = (bf16[1,8,4,256]{3,1,2,0:T(8,128)(2,1)S(1)}, bf16[1,8,4,256]{3,1,2,0:T(8,128)(2,1)S(1)}, u32[]{:S(2)}, u32[]{:S(2)}) collective-permute-start(bf16[1,8,4,256]{3,1,2,0:T(8,128)(2,1)S(1)} %get-tuple-element.50), channel_id=1, source_target_pairs={{4,0},{8,4},{12,8},{16,12},{20,16},{24,20},{28,24},{32,28},{36,32}... | collective-permute-start | bytes 49160 | tf_op jit(solution)/shard_map/ppermute | solution.py:19
  40.9 367.3 %collective-permute-start = (bf16[1,8,4,256]{3,1,2,0:T(8,128)(2,1)S(1)}, bf16[1,8,4,256]{3,1,2,0:T(8,128)(2,1)S(1)}, u32[]{:S(2)}, u32[]{:S(2)}) collective-permute-start(bf16[1,8,4,256]{3,1,2,0:T(8,128)(2,1)S(1)} %get-tuple-element.49), channel_id=1, source_target_pairs={{0,4},{4,8},{8,12},{12,16},{16,20},{20,24},{24,28},{28,32},{32,36}... | collective-permute-start | bytes 49160 | tf_op jit(solution)/shard_map/ppermute | solution.py:16
  408.3 4.8 collective-permute-start.3
  410.7 4.7 collective-permute-start.2
  421.3 6.6 %copy-start.7 = (bf16[256,256]{1,0:T(8,128)(2,1)S(1)}, bf16[256,256]{1,0:T(8,128)(2,1)}, u32[]{:S(2)}) copy-start(bf16[256,256]{1,0:T(8,128)(2,1)} %reshape.236) | copy-start | bytes 393220
  422.0 7.0 %copy-start.8 = (bf16[256,256]{1,0:T(8,128)(2,1)S(1)}, bf16[256,256]{1,0:T(8,128)(2,1)}, u32[]{:S(2)}) copy-start(bf16[256,256]{1,0:T(8,128)(2,1)} %reshape.237) | copy-start | bytes 393220
  422.8 7.4 %copy-start.9 = (bf16[256,256]{1,0:T(8,128)(2,1)S(1)}, bf16[256,256]{1,0:T(8,128)(2,1)}, u32[]{:S(2)}) copy-start(bf16[256,256]{1,0:T(8,128)(2,1)} %reshape.238) | copy-start | bytes 393220
  424.4 8.1 %copy-start.6 = (bf16[256,256]{1,0:T(8,128)(2,1)S(1)}, bf16[256,256]{1,0:T(8,128)(2,1)}, u32[]{:S(2)}) copy-start(bf16[256,256]{1,0:T(8,128)(2,1)} %reshape.240) | copy-start | bytes 393220
  427.0 10.1 %copy-start.10 = (bf16[256,256]{1,0:T(8,128)(2,1)S(1)}, bf16[256,256]{1,0:T(8,128)(2,1)}, u32[]{:S(2)}) copy-start(bf16[256,256]{1,0:T(8,128)(2,1)} %reshape.244) | copy-start | bytes 393220
  427.1 11.0 %copy-start.11 = (bf16[256,256]{1,0:T(8,128)(2,1)S(1)}, bf16[256,256]{1,0:T(8,128)(2,1)}, u32[]{:S(2)}) copy-start(bf16[256,256]{1,0:T(8,128)(2,1)} %reshape.245) | copy-start | bytes 393220
  427.8 10.3 %copy-start.4 = (bf16[27,256,256]{2,1,0:T(8,128)(2,1)S(1)}, bf16[27,256,256]{2,1,0:T(8,128)(2,1)}, u32[]{:S(2)}) copy-start(bf16[27,256,256]{2,1,0:T(8,128)(2,1)} %param.17) | copy-start | bytes 10616836
  429.1 9.3 %copy-start.12 = (bf16[256,256]{1,0:T(8,128)(2,1)S(1)}, bf16[256,256]{1,0:T(8,128)(2,1)}, u32[]{:S(2)}) copy-start(bf16[256,256]{1,0:T(8,128)(2,1)} %reshape.246) | copy-start | bytes 393220
  430.2 8.3 %copy-start.13 = (bf16[256,256]{1,0:T(8,128)(2,1)S(1)}, bf16[256,256]{1,0:T(8,128)(2,1)}, u32[]{:S(2)}) copy-start(bf16[256,256]{1,0:T(8,128)(2,1)} %reshape.247) | copy-start | bytes 393220
  431.4 7.4 %copy-start.15 = (bf16[256,256]{1,0:T(8,128)(2,1)S(1)}, bf16[256,256]{1,0:T(8,128)(2,1)}, u32[]{:S(2)}) copy-start(bf16[256,256]{1,0:T(8,128)(2,1)} %reshape.248) | copy-start | bytes 393220
  434.7 4.7 copy-start.14
  435.9 3.7 copy-start.16
  438.2 1.8 copy-start.17
  438.6 1.8 copy-start.18
  438.8 1.8 copy-start.19
  481.9 3.2 copy-start.3
  481.9 4.1 copy-start.26
  481.9 4.6 copy-start.25
  482.6 4.4 copy-start.2
  482.6 4.4 copy-start.24
  485.2 2.4 copy-start.23
  487.0 2.8 copy-start.1
  (5 other events, 8.9 us)
where the time goes:
time: 491 us; the launch traced here: 490 us
  waiting for transfers between devices  363 us (74%)
  local copies, waits for them, and re-layouts  60.1 us (12%)
  blocking collectives  19.6 us (4%)
  starting transfers between devices  19.6 us (4%)
  matrix products  19.5 us (4%)
  other arithmetic  6.43 us (1%)
    ppermute x2, waiting for transfers between devices, padded(): lax.ppermute(lax.slice_in_dim(block, 0, width, axis=dim), axis, backward)  361 us
    gather x4, local copies, waits for them, and re-layouts, per_device(): arrived[cell_grid[:, parent]]  25.5 us
    all_to_all x1, blocking collectives, per_device(): lax.all_to_all(table, 'gx', split_axis=0, concat_axis=0, tiled=True)  19.6 us
    dot_general x27, matrix products, per_device(): jnp.dot(shifted, conv_weight[offset], preferred_element_type=jnp.float32)  13.5 us
    reshape x27, local copies, waits for them, and re-layouts, per_device(): shifted = framed[shift_x:shift_x + vox_x, shift_y:shift_y + vox_y, shift_...  10.7 us
  transfers between devices with their start and end apart: 5, of which 2 were waited for; matrix products, arithmetic and copies ran while one was open for 6% of the time, Pallas kernels for 0%

commit v1 on v0

v1 whole, which is shorter than its diff:
```python
import math

import jax
import jax.numpy as jnp
import numpy as np
from jax import lax
from jax.experimental import pallas as pl
from jax.experimental.pallas import tpu as pltpu
from jax.sharding import PartitionSpec as P

CH = 256
HEADS = 8
HEAD_DIM = 32
EDGE = 4
VX, VY, VZ = 8, 8, 4
ROWS = VX * VY * VZ
WINDOWS = 4
ACT_MAX = 3
PARENTS = 4
TOK = 128
LANES = 128
PACK = 144
SCALE = math.log2(math.e) / math.sqrt(HEAD_DIM)
LOWEST = -3e38
F32 = jnp.float32
BF16 = jnp.bfloat16
VMEM = pl.BlockSpec(memory_space=pltpu.VMEM)
SMEM = pl.BlockSpec(memory_space=pltpu.SMEM)
ANY = pl.BlockSpec(memory_space=pl.ANY)
NT = (((1,), (1,)), ((), ()))


def placement():
    row = np.arange(ROWS)
    z, x, y = row // 64, row // 8 % 8, row % 8
    window = (x // EDGE) * 2 + y // EDGE
    query = z * 16 + x % EDGE * 4 + y % EDGE
    lane = np.arange(LANES) % 64
    hit = (window[None, :, None] == np.arange(WINDOWS)[:, None, None]) & (
        query[None, :, None] == lane[None, None, :]
    )
    return hit.astype(np.float32)


def row_mask(act_ref):
    low = lax.broadcasted_iota(jnp.int32, (VY, CH), 0) < EDGE
    flags = [act_ref[w].astype(F32) for w in range(WINDOWS)]
    halves = [jnp.where(low, flags[2 * b], flags[2 * b + 1]) for b in range(2)]
    return jnp.concatenate(
        [jnp.broadcast_to(half[None], (EDGE, VY, CH)) for half in halves], axis=0
    )


def conv_kernel(
    act_ref, slot_ref, latent_ref, xlo_ref, xhi_ref, ylo_ref, yhi_ref, ngain_ref, bias_ref,
    again_ref, weight_ref, qw_ref, place_ref, extra_ref, hidden_ref, query_ref,
    frame, weights, sems,
):
    copies = [
        pltpu.make_async_copy(weight_ref.at[pl.ds(3 * ab, 3)], weights.at[pl.ds(3 * ab, 3)], sems.at[ab])
        for ab in range(9)
    ]
    for copy in copies:
        copy.start()
    latent = latent_ref[...]
    mask = row_mask(act_ref)[None]
    scale = lax.rsqrt(jnp.mean(latent * latent, axis=-1, keepdims=True) + 1e-06)
    normed = mask * latent * scale * ngain_ref[...].reshape(1, 1, 1, CH)
    frame[1, :, 1 : VX + 1] = normed
    frame[1, :, 0] = xlo_ref[...].astype(F32)
    frame[1, :, VX + 1] = xhi_ref[...].astype(F32)
    ylo = ylo_ref[...].astype(F32)
    yhi = yhi_ref[...].astype(F32)
    first = lax.broadcasted_iota(jnp.int32, (VY, CH), 0) == 0
    last = lax.broadcasted_iota(jnp.int32, (VY, CH), 0) == VY - 1
    for z in range(VZ):
        for x in range(VX + 2):
            r = z * (VX + 2) + x
            here = frame[1, z, x]
            frame[0, z, x] = jnp.where(first, ylo[r : r + 1, :], pltpu.roll(here, 1, 0))
            frame[2, z, x] = jnp.where(last, yhi[r : r + 1, :], pltpu.roll(here, VY - 1, 0))
    mid = jnp.zeros((ROWS, CH), F32)
    up = jnp.zeros((ROWS - 64, CH), F32)
    down = jnp.zeros((ROWS - 64, CH), F32)
    for ab in range(9):
        copies[ab].wait()
        a, b = ab // 3, ab % 3
        slab = frame[b, :, a : a + VX].reshape(ROWS, CH).astype(BF16)
        up = up + jnp.dot(slab[: ROWS - 64], weights[3 * ab], preferred_element_type=F32)
        mid = mid + jnp.dot(slab, weights[3 * ab + 1], preferred_element_type=F32)
        down = down + jnp.dot(slab[64:], weights[3 * ab + 2], preferred_element_type=F32)
    gap = jnp.zeros((64, CH), F32)
    conv = mid + jnp.concatenate([gap, up], 0) + jnp.concatenate([down, gap], 0) + bias_ref[...]
    flat_mask = jnp.broadcast_to(mask, (VZ, VX, VY, CH)).reshape(ROWS, CH)
    hidden = latent.reshape(ROWS, CH) + flat_mask * (conv / (1.0 + jnp.exp(-conv)))
    hidden_ref[...] = hidden
    scale = lax.rsqrt(jnp.mean(hidden * hidden, axis=-1, keepdims=True) + 1e-06)
    query_in = (hidden * scale * again_ref[...]).astype(BF16)
    queries = lax.dot_general(qw_ref[...], query_in, NT, preferred_element_type=F32).astype(BF16)
    left = lax.broadcasted_iota(jnp.int32, (LANES, LANES), 1) < 64
    query_ref[:, :LANES, :] = jnp.zeros((ACT_MAX, LANES, LANES), BF16)
    query_ref[:, LANES:, :] = extra_ref[...]
    for w in range(WINDOWS):
        @pl.when(act_ref[w] > 0)
        def _(w=w):
            both = jnp.dot(queries, place_ref[w], preferred_element_type=F32)
            query_ref[slot_ref[w], :LANES, :] = jnp.where(left, both[:LANES], both[LANES:]).astype(BF16)


def attend_kernel(code_ref, *refs):
    query_refs, kv_ref, out_refs = refs[:4], refs[4], refs[5:9]
    held, blocks, sums, peak, total, sems = refs[9:]

    def fetch(n):
        region = jnp.maximum(code_ref[n], 0)
        return pltpu.make_async_copy(kv_ref.at[region], held.at[n], sems.at[n])

    def begin(n, carry):
        @pl.when(code_ref[n] >= 0)
        def _():
            fetch(n).start()
        return carry

    lax.fori_loop(0, 4 * ACT_MAX * PARENTS, begin, 0)
    blocks[...] = jnp.zeros_like(blocks)
    left = lax.broadcasted_iota(jnp.int32, (HEAD_DIM, LANES), 1) < 64
    for source in range(4):
        query_ref, out_ref = query_refs[source], out_refs[source]

        def window(s, carry, source=source, query_ref=query_ref, out_ref=out_ref):
            base = (source * ACT_MAX + s) * PARENTS
            found = code_ref[base]
            for p in range(1, PARENTS):
                found = jnp.maximum(found, code_ref[base + p])

            @pl.when(found < 0)
            def _():
                out_ref[s, :LANES, :] = jnp.zeros((LANES, LANES), BF16)
                rows = lax.broadcasted_iota(jnp.int32, (PACK - LANES, LANES), 0)
                out_ref[s, LANES:, :] = jnp.where(rows < 4, LOWEST, 0.0).astype(BF16)

            @pl.when(found >= 0)
            def _():
                for j in range(4):
                    pair = query_ref[s, 32 * j : 32 * j + 32, :].astype(F32)
                    lanes = slice(LANES * j, LANES * j + LANES)
                    blocks[64 * j : 64 * j + 32, lanes] = jnp.where(left, pair, 0.0).astype(BF16)
                    blocks[64 * j + 32 : 64 * j + 64, lanes] = jnp.where(left, 0.0, pair).astype(BF16)
                sums[...] = jnp.zeros_like(sums)
                peak[...] = jnp.full_like(peak, LOWEST)
                total[...] = jnp.zeros_like(total)

                def parent(p, carry):
                    n = base + p

                    @pl.when(code_ref[n] >= 0)
                    def _():
                        fetch(n).wait()
                        for g in range(2):
                            half = slice(LANES * g, LANES * g + LANES)
                            wide = slice(256 * g, 256 * g + 256)
                            scores = jnp.dot(held[n, :, half], blocks[half, wide], preferred_element_type=F32)
                            old = peak[:, wide]
                            new = jnp.maximum(old, jnp.max(scores, axis=0, keepdims=True))
                            lifted = jnp.exp2((scores - new) * SCALE)
                            fade = jnp.exp2((old - new) * SCALE)
                            peak[:, wide] = new
                            total[:, wide] = total[:, wide] * fade + jnp.sum(lifted, axis=0, keepdims=True)
                            mixed = jnp.dot(
                                held[n, :, CH + LANES * g : CH + LANES * g + LANES],
                                lifted.astype(BF16), preferred_element_type=F32,
                            )
                            for jj in range(2):
                                rows = slice(64 * (2 * g + jj), 64 * (2 * g + jj) + 64)
                                cut = slice(LANES * jj, LANES * jj + LANES)
                                sums[rows, :] = sums[rows, :] * fade[:, cut] + mixed[64 * jj : 64 * jj + 64, cut]
                    return carry

                lax.fori_loop(0, PARENTS, parent, 0)
                levels = []
                for j in range(4):
                    lanes = slice(LANES * j, LANES * j + LANES)
                    kept = jnp.where(left, sums[64 * j : 64 * j + 32, :], sums[64 * j + 32 : 64 * j + 64, :])
                    out_ref[s, 32 * j : 32 * j + 32, :] = (kept / total[:, lanes]).astype(BF16)
                    levels.append(peak[:, lanes] * SCALE + jnp.log2(total[:, lanes]))
                level = jnp.concatenate(levels, axis=0)
                high = level.astype(BF16).astype(F32)
                middle = (level - high).astype(BF16).astype(F32)
                low = level - high - middle
                stats = jnp.concatenate([high, middle, low, jnp.zeros_like(low)], axis=0)
                out_ref[s, LANES:, :] = stats.astype(BF16)
            return carry

        lax.fori_loop(0, ACT_MAX, window, 0)


def merge_kernel(act_ref, slot_ref, *refs):
    part_refs = refs[:4]
    hidden_ref, ow_ref, place_ref, out_ref, mixed, attended = refs[4:]
    for s in range(ACT_MAX):
        stats = [ref[s, LANES:, :].astype(F32) for ref in part_refs]
        levels = [one[0:4] + one[4:8] + one[8:12] for one in stats]
        top = jnp.maximum(jnp.maximum(levels[0], levels[1]), jnp.maximum(levels[2], levels[3]))
        shares = [jnp.exp2(level - top) for level in levels]
        whole = shares[0] + shares[1] + shares[2] + shares[3]
        for j in range(4):
            rows = slice(32 * j, 32 * j + 32)
            value = jnp.zeros((HEAD_DIM, LANES), F32)
            for ref, share in zip(part_refs, shares):
                value = value + ref[s, rows, :].astype(F32) * (share / whole)[j : j + 1, :]
            mixed[s, rows, :] = value.astype(BF16)
    attended[...] = jnp.zeros_like(attended)
    left = lax.broadcasted_iota(jnp.int32, (ROWS, LANES), 1) < 64
    for w in range(WINDOWS):
        @pl.when(act_ref[w] > 0)
        def _(w=w):
            block = mixed[slot_ref[w]]
            place = place_ref[w].astype(F32)
            attended[0] += lax.dot_general(
                jnp.where(left, place, 0.0).astype(BF16), block, NT, preferred_element_type=F32
            )
            attended[1] += lax.dot_general(
                jnp.where(left, 0.0, place).astype(BF16), block, NT, preferred_element_type=F32
            )
    projected = jnp.dot(attended[0].astype(BF16), ow_ref[0], preferred_element_type=F32)
    projected = projected + jnp.dot(attended[1].astype(BF16), ow_ref[1], preferred_element_type=F32)
    mask = jnp.broadcast_to(row_mask(act_ref)[None], (VZ, VX, VY, CH)).reshape(ROWS, CH)
    out_ref[...] = mask * (hidden_ref[...] + projected)


def shift(block, axis, step):
    count = lax.axis_size(axis)
    return lax.ppermute(block, axis, [(i, i + step) for i in range(count) if 0 <= i + step < count])


def turn(block, axis, step):
    count = lax.axis_size(axis)
    return lax.ppermute(block, axis, [(i, (i + step) % count) for i in range(count)])


def per_device(
    latent, active, parent_owner, parent_slot, coarse_kv, norm_gain, conv_weight, conv_bias,
    attn_gain, q_weight, out_weight,
):
    plane = lax.axis_index("gy")
    mine = lax.dynamic_index_in_dim(coarse_kv, plane, 0, keepdims=False)
    mine = jnp.concatenate([mine[:, :CH], mine[:, CH : CH + 128].T, mine[:, CH + 128 :].T], axis=1)
    kv_all = lax.all_gather(mine, "gx")

    act = active.reshape(WINDOWS)
    slots = jnp.cumsum(act) - 1
    hit = (act[None, :] > 0) & (slots[None, :] == jnp.arange(ACT_MAX)[:, None])
    codes = (parent_owner * 4 + parent_slot).reshape(WINDOWS, PARENTS) + 1
    codes = jnp.sum(jnp.where(hit[:, :, None], codes[None], 0), axis=1) - 1
    extra = jnp.zeros((ACT_MAX, PACK - LANES, LANES), BF16).at[:, 0, :PARENTS].set(codes.astype(BF16))

    turned = latent.transpose(2, 0, 1, 3)
    mask = jnp.repeat(jnp.repeat(active[:, :, 0].astype(F32), EDGE, 0), EDGE, 1)

    def normed(values, flags):
        scale = lax.rsqrt(jnp.mean(values * values, axis=-1, keepdims=True) + 1e-06)
        return (flags[None, :, None] * values * scale * norm_gain).astype(BF16)

    x_first, x_last = normed(turned[:, 0], mask[0]), normed(turned[:, -1], mask[-1])
    y_first, y_last = normed(turned[:, :, 0], mask[:, 0]), normed(turned[:, :, -1], mask[:, -1])
    x_low, x_high = shift(x_last, "gx", 1), shift(x_first, "gx", -1)
    y_first = jnp.concatenate([x_low[:, :1], y_first, x_high[:, :1]], axis=1).reshape(-1, CH)
    y_last = jnp.concatenate([x_low[:, -1:], y_last, x_high[:, -1:]], axis=1).reshape(-1, CH)
    y_low, y_high = shift(y_last, "gy", 1), shift(y_first, "gy", -1)

    place = jnp.asarray(placement(), BF16)
    qw = q_weight.reshape(CH, 4, 2, HEAD_DIM).transpose(2, 1, 3, 0).reshape(CH, CH)
    ow = out_weight.reshape(4, 2, HEAD_DIM, CH).transpose(1, 0, 2, 3).reshape(2, LANES, CH)

    hidden, query = pl.pallas_call(
        conv_kernel,
        out_shape=(
            jax.ShapeDtypeStruct((ROWS, CH), F32),
            jax.ShapeDtypeStruct((ACT_MAX, PACK, LANES), BF16),
        ),
        in_specs=[SMEM, SMEM] + [VMEM] * 8 + [ANY] + [VMEM] * 3,
        out_specs=(VMEM, VMEM),
        scratch_shapes=[
            pltpu.VMEM((3, VZ, VX + 2, VY, CH), F32),
            pltpu.VMEM((27, CH, CH), BF16),
            pltpu.SemaphoreType.DMA((9,)),
        ],
        compiler_params=pltpu.CompilerParams(vmem_limit_bytes=24 << 20),
        cost_estimate=pl.CostEstimate(flops=2 * 27 * ROWS * CH * CH, bytes_accessed=5 << 20, transcendentals=ROWS * CH),
        name="conv",
    )(
        act, slots, turned, x_low, x_high, y_low, y_high, norm_gain.reshape(1, CH),
        conv_bias.reshape(1, CH), attn_gain.reshape(1, CH), conv_weight, qw, place, extra,
    )

    queries = [query] + [turn(query, "gy", d) for d in range(1, 4)]
    wanted = jnp.concatenate([one[:, LANES, :PARENTS] for one in queries]).astype(jnp.int32).reshape(-1)
    wanted = jnp.where((wanted >= 0) & (wanted % 4 == plane), wanted // 4, -1)

    parts = pl.pallas_call(
        attend_kernel,
        out_shape=[jax.ShapeDtypeStruct((ACT_MAX, PACK, LANES), BF16)] * 4,
        in_specs=[SMEM] + [VMEM] * 4 + [ANY],
        out_specs=[VMEM] * 4,
        scratch_shapes=[
            pltpu.VMEM((4 * ACT_MAX * PARENTS, TOK, 2 * CH), BF16),
            pltpu.VMEM((CH, 2 * CH), BF16),
            pltpu.VMEM((CH, LANES), F32),
            pltpu.VMEM((1, 2 * CH), F32),
            pltpu.VMEM((1, 2 * CH), F32),
            pltpu.SemaphoreType.DMA((4 * ACT_MAX * PARENTS,)),
        ],
        compiler_params=pltpu.CompilerParams(vmem_limit_bytes=24 << 20),
        name="attend",
    )(wanted, *queries, kv_all)

    merged = [parts[0]] + [turn(parts[d], "gy", -d) for d in range(1, 4)]
    out = pl.pallas_call(
        merge_kernel,
        out_shape=jax.ShapeDtypeStruct((ROWS, CH), F32),
        in_specs=[SMEM, SMEM] + [VMEM] * 7,
        out_specs=VMEM,
        scratch_shapes=[
            pltpu.VMEM((ACT_MAX, LANES, LANES), BF16),
            pltpu.VMEM((2, ROWS, LANES), F32),
        ],
        compiler_params=pltpu.CompilerParams(vmem_limit_bytes=16 << 20),
        name="merge",
    )(act, slots, *merged, hidden, ow, place)
    return out.reshape(VZ, VX, VY, CH).transpose(1, 2, 0, 3)


def solution(mesh):
    placed = (
        P("gx", "gy", None, None),
        P("gx", "gy", None),
        P("gx", "gy", None, None),
        P("gx", "gy", None, None),
        P("gx", None, None),
        P(),
        P(),
        P(),
        P(),
        P(),
        P(),
    )
    return jax.shard_map(
        per_device, mesh=mesh, in_specs=placed, out_specs=P("gx", "gy", None, None), check_vma=False
    )
```

time: 491 us -> 129 us (0.26)
  the two profiles are of different devices: /device:TPU:31 before, /device:TPU:49 now
where the time goes in v1:
time: 129 us; the launch traced here: 126 us
  waiting for transfers between devices  55.8 us (43%)
  starting transfers between devices  20.6 us (16%)
  local copies, waits for them, and re-layouts  16.5 us (13%)
  Pallas kernels  14.6 us (11%)
  between operations  13.7 us (11%)
  other arithmetic  5.05 us (4%)
    all_gather x1, waiting for transfers between devices, per_device(): kv_all = lax.all_gather(mine, 'gx')  46.5 us
    unnamed x21, local copies, waits for them, and re-layouts  12 us
    ppermute x4, starting transfers between devices, shift(): lax.ppermute(block, axis, [(i, i + step) for i in range(count) if 0 <= i...  10.7 us
    ppermute x6, starting transfers between devices, turn(): lax.ppermute(block, axis, [(i, (i + step) % count) for i in range(count)])  9.91 us
    ppermute x6, waiting for transfers between devices, turn(): lax.ppermute(block, axis, [(i, (i + step) % count) for i in range(count)])  8.73 us
    pallas_call x1, Pallas kernels, per_device(): pl.pallas_call(attend_kernel, out_shape=[jax.ShapeDtypeStruct((ACT_MAX, P...  7.6 us
    pallas_call x1, Pallas kernels, per_device(): pl.pallas_call(conv_kernel, out_shape=(jax.ShapeDtypeStruct((ROWS, CH), F...  5.51 us
  transfers between devices with their start and end apart: 11, of which 7 were waited for; matrix products, arithmetic and copies ran while one was open for 8% of the time, Pallas kernels for 4%

profile of v1, /device:TPU:49, one launch (start us, length us, event | category | flops | bytes accessed | tf_op | source)
XLA Modules:
  0.0 126.2 jit_solution(5009014150386115519)
XLA Ops:
  6.5 1.0 copy-done
  7.9 0.7 pad_maximum_fusion
  8.6 1.0 copy.137
  10.1 1.4 %fusion.12 = (f32[2,2,1]{1,2,0:T(1,128)S(1)}, s32[2,2]{1,0:T(2,128)S(1)}) fusion(s32[2,2,1]{1,2,0:T(1,128)} %param.15, s32[]{:T(128)} %broadcast.190), kind=kLoop, calls=%fused_computation.53 | loop fusion | flops 4 | bytes 52 | tf_op jit(solution)/shard_map/convert_element_type | solution.py:258
  12.7 0.8 multiply_convert_fusion
  13.4 3.5 %collective-permute-start = (bf16[4,8,256]{2,1,0:T(8,128)(2,1)S(1)}, bf16[4,8,256]{2,1,0:T(8,128)(2,1)S(1)}, u32[]{:S(2)}, u32[]{:S(2)}) collective-permute-start(bf16[4,8,256]{2,1,0:T(8,128)(2,1)S(1)} %get-tuple-element.34), channel_id=1, source_target_pairs={{0,4},{4,8},{8,12},{12,16},{16,20},{20,24},{24,28},{28,32},{32,36}... | collective-permute-start | bytes 49160 | tf_op jit(solution)/shard_map/ppermute | solution.py:233
  16.9 1.9 %collective-permute-start.1 = (bf16[4,8,256]{2,1,0:T(8,128)(2,1)S(1)}, bf16[4,8,256]{2,1,0:T(8,128)(2,1)S(1)}, u32[]{:S(2)}, u32[]{:S(2)}) collective-permute-start(bf16[4,8,256]{2,1,0:T(8,128)(2,1)S(1)} %get-tuple-element.33), channel_id=1, source_target_pairs={{4,0},{8,4},{12,8},{16,12},{20,16},{24,20},{28,24},{32,28},{36,32}... | collective-permute-start | bytes 49160 | tf_op jit(solution)/shard_map/ppermute | solution.py:233
  18.9 0.8 reshape.205
  19.9 0.7 add_bitcast_fusion
  20.6 0.8 fusion.4
  22.0 1.3 %collective-permute-start.3 = (bf16[40,256]{1,0:T(8,128)(2,1)S(1)}, bf16[40,256]{1,0:T(8,128)(2,1)S(1)}, u32[]{:S(2)}, u32[]{:S(2)}) collective-permute-start(bf16[40,256]{1,0:T(8,128)(2,1)S(1)} %reshape.209), channel_id=1, source_target_pairs={{1,0},{2,1},{3,2},{5,4},{6,5},{7,6},{9,8},{10,9},{11,10},{13,12},{... | collective-permute-start | bytes 61448 | tf_op jit(solution)/shard_map/ppermute | solution.py:233
  23.4 4.0 %collective-permute-start.2 = (bf16[40,256]{1,0:T(8,128)(2,1)S(1)}, bf16[40,256]{1,0:T(8,128)(2,1)S(1)}, u32[]{:S(2)}, u32[]{:S(2)}) collective-permute-start(bf16[40,256]{1,0:T(8,128)(2,1)S(1)} %reshape.208), channel_id=1, source_target_pairs={{0,1},{1,2},{2,3},{4,5},{5,6},{6,7},{8,9},{9,10},{10,11},{12,13},{... | collective-permute-start | bytes 61448 | tf_op jit(solution)/shard_map/ppermute | solution.py:233
  27.4 1.0 copy.135
  28.5 1.0 copy.102
  29.5 2.0 %copy-done.2 = bf16[27,256,256]{2,1,0:T(8,128)(2,1)S(1)} copy-done((bf16[27,256,256]{2,1,0:T(8,128)(2,1)S(1)}, bf16[27,256,256]{2,1,0:T(8,128)(2,1)}, u32[]{:S(2)}) %copy-start.2) | copy-done | bytes 3538968
  31.5 0.9 copy-done.3
  34.5 5.5 %conv.1 = (f32[256,256]{1,0:T(8,128)S(1)}, bf16[3,144,128]{2,1,0:T(8,128)(2,1)S(1)}) custom-call(s32[4]{0:T(128)S(1)} %reshape.204.act_ref, s32[4]{0:T(128)S(1)} %add_bitcast_fusion.1.slot_ref, f32[4,8,8,256]{3,2,1,0:T(8,128)S(1)} %bitcast.79, bf16[4,8,256]{2,1,0:T(8,128)(2,1)S(1)} %collective-permute-done.xlo_ref, ...), custom_call_target="tpu_custom_call" | custom-call | flops 905969664 | bytes 5242880 | tf_op jit(solution)/shard_map/conv/pallas_call | solution.py:275
  40.0 1.1 collective-permute-start.4
  41.1 2.0 %collective-permute-start.5 = (bf16[3,144,128]{2,1,0:T(8,128)(2,1)S(1)}, bf16[3,144,128]{2,1,0:T(8,128)(2,1)S(1)}, u32[]{:S(2)}, u32[]{:S(2)}) collective-permute-start(bf16[3,144,128]{2,1,0:T(8,128)(2,1)S(1)} %get-tuple-element.23.refs_0_), channel_id=1, source_target_pairs={{0,2},{1,3},{2,0},{3,1},{4,6},{5,7},{6,4},{7,5},{8,10},{9,11},{10,... | collective-permute-start | bytes 331784 | tf_op jit(solution)/shard_map/ppermute | solution.py:238
  43.2 1.6 %collective-permute-start.6 = (bf16[3,144,128]{2,1,0:T(8,128)(2,1)S(1)}, bf16[3,144,128]{2,1,0:T(8,128)(2,1)S(1)}, u32[]{:S(2)}, u32[]{:S(2)}) collective-permute-start(bf16[3,144,128]{2,1,0:T(8,128)(2,1)S(1)} %get-tuple-element.23.refs_0_), channel_id=1, source_target_pairs={{0,3},{1,0},{2,1},{3,2},{4,7},{5,4},{6,5},{7,6},{8,11},{9,8},{10,9... | collective-permute-start | bytes 331784 | tf_op jit(solution)/shard_map/ppermute | solution.py:238
  45.0 1.6 %collective-permute-done.5.refs_2_ = bf16[3,144,128]{2,1,0:T(8,128)(2,1)S(1)} collective-permute-done((bf16[3,144,128]{2,1,0:T(8,128)(2,1)S(1)}, bf16[3,144,128]{2,1,0:T(8,128)(2,1)S(1)}, u32[]{:S(2)}, u32[]{:S(2)}) %collective-permute-start.5) | collective-permute-done | bytes 110624 | tf_op jit(solution)/shard_map/ppermute | solution.py:238
  46.7 1.0 collective-permute-done.6.refs_3_
  48.2 46.5 %all-gather.3.cloned.1.call-done = bf16[8192,512]{1,0:T(8,128)(2,1)} async-done(((bf16[128,512]{1,0:T(8,128)(2,1)}), bf16[8192,512]{1,0:T(8,128)(2,1)}) %all-gather.3.cloned.1.call-update) | async-done | bytes 8388624 | tf_op jit(solution)/shard_map/all_gather | solution.py:248
  94.7 3.4 %copy-done.1 = bf16[8192,512]{1,0:T(8,128)(2,1)S(1)} copy-done((bf16[8192,512]{1,0:T(8,128)(2,1)S(1)}, bf16[8192,512]{1,0:T(8,128)(2,1)}, u32[]{:S(2)}) %copy-start.1) | copy-done | bytes 8388632
  98.1 7.6 %attend.1 = (bf16[3,144,128]{2,1,0:T(8,128)(2,1)S(1)}, bf16[3,144,128]{2,1,0:T(8,128)(2,1)S(1)}, bf16[3,144,128]{2,1,0:T(8,128)(2,1)S(1)}, bf16[3,144,128]{2,1,0:T(8,128)(2,1)S(1)}) custom-call(s32[48]{0:T(128)S(1)} %and_select_fusion.1.code_ref, bf16[3,144,128]{2,1,0:T(8,128)(2,1)S(1)} %get-tuple-element.23.refs_0_, ...), custom_call_target="tpu_custom_call" | custom-call | tf_op jit(solution)/shard_map/attend/pallas_call | solution.py:300
  105.7 2.5 %collective-permute-start.7 = (bf16[3,144,128]{2,1,0:T(8,128)(2,1)S(1)}, bf16[3,144,128]{2,1,0:T(8,128)(2,1)S(1)}, u32[]{:S(2)}, u32[]{:S(2)}) collective-permute-start(bf16[3,144,128]{2,1,0:T(8,128)(2,1)S(1)} %get-tuple-element.25), channel_id=1, source_target_pairs={{0,3},{1,0},{2,1},{3,2},{4,7},{5,4},{6,5},{7,6},{8,11},{9,8},{10,9... | collective-permute-start | bytes 331784 | tf_op jit(solution)/shard_map/ppermute | solution.py:238
  108.1 2.7 %collective-permute-start.8 = (bf16[3,144,128]{2,1,0:T(8,128)(2,1)S(1)}, bf16[3,144,128]{2,1,0:T(8,128)(2,1)S(1)}, u32[]{:S(2)}, u32[]{:S(2)}) collective-permute-start(bf16[3,144,128]{2,1,0:T(8,128)(2,1)S(1)} %get-tuple-element.26), channel_id=1, source_target_pairs={{0,2},{1,3},{2,0},{3,1},{4,6},{5,7},{6,4},{7,5},{8,10},{9,11},{10,... | collective-permute-start | bytes 331784 | tf_op jit(solution)/shard_map/ppermute | solution.py:238
  110.9 1.8 %collective-permute-done.7.refs_1_ = bf16[3,144,128]{2,1,0:T(8,128)(2,1)S(1)} collective-permute-done((bf16[3,144,128]{2,1,0:T(8,128)(2,1)S(1)}, bf16[3,144,128]{2,1,0:T(8,128)(2,1)S(1)}, u32[]{:S(2)}, u32[]{:S(2)}) %collective-permute-start.7) | collective-permute-done | bytes 110624 | tf_op jit(solution)/shard_map/ppermute | solution.py:238
  112.7 0.9 collective-permute-done.8.refs_2_
  113.6 3.4 %collective-permute-done.9.refs_3_ = bf16[3,144,128]{2,1,0:T(8,128)(2,1)S(1)} collective-permute-done((bf16[3,144,128]{2,1,0:T(8,128)(2,1)S(1)}, bf16[3,144,128]{2,1,0:T(8,128)(2,1)S(1)}, u32[]{:S(2)}, u32[]{:S(2)}) %collective-permute-start.9) | collective-permute-done | bytes 110624 | tf_op jit(solution)/shard_map/ppermute | solution.py:238
  117.0 1.5 %merge.1 = f32[256,256]{1,0:T(8,128)S(1)} custom-call(s32[4]{0:T(128)S(1)} %reshape.204.act_ref, s32[4]{0:T(128)S(1)} %add_bitcast_fusion.1.slot_ref, bf16[3,144,128]{2,1,0:T(8,128)(2,1)S(1)} %get-tuple-element.24.refs_0_, bf16[3,144,128]{2,1,0:T(8,128)(2,1)S(1)} %collective-permute-done.7.refs_1_, bf16[3,144,128]{2,1,0:T(8,128)(2,1)S(1)} %collective-permute-done.8.refs_2_, ...), custom_call_target="tpu_custom_call" | custom-call | tf_op jit(solution)/shard_map/merge/pallas_call | solution.py:318
  118.4 0.9 copy.136
  (77 shorter events, 5.8 us)
Async XLA Ops:
  6.5 1.0 copy-start
  6.5 88.2 %all-gather.3.cloned.1.call-start = ((), (), s32[]{:S(2)}) async-start(), calls=%async_computation | async-start | bytes 8519680 | tf_op jit(solution)/shard_map/all_gather | solution.py:248
  7.6 103.3 %copy-start.8 = (bf16[256,256]{1,0:T(8,128)(2,1)S(1)}, bf16[256,256]{1,0:T(8,128)(2,1)}, u32[]{:S(2)}) copy-start(bf16[256,256]{1,0:T(8,128)(2,1)} %param.24) | copy-start | bytes 393220
  7.6 109.4 %copy-start.4 = (bf16[4,256,128]{2,1,0:T(8,128)(2,1)S(1)}, bf16[4,256,128]{2,1,0:T(8,128)(2,1)}, u32[]{:S(2)}) copy-start(bf16[4,256,128]{2,1,0:T(8,128)(2,1)} %constant.91.clone.place_ref.refs_6_) | copy-start | bytes 786436
  13.4 8.0 %collective-permute-start = (bf16[4,8,256]{2,1,0:T(8,128)(2,1)S(1)}, bf16[4,8,256]{2,1,0:T(8,128)(2,1)S(1)}, u32[]{:S(2)}, u32[]{:S(2)}) collective-permute-start(bf16[4,8,256]{2,1,0:T(8,128)(2,1)S(1)} %get-tuple-element.34), channel_id=1, source_target_pairs={{0,4},{4,8},{8,12},{12,16},{16,20},{20,24},{24,28},{28,32},{32,36}... | collective-permute-start | bytes 49160 | tf_op jit(solution)/shard_map/ppermute | solution.py:233
  16.9 5.1 %collective-permute-start.1 = (bf16[4,8,256]{2,1,0:T(8,128)(2,1)S(1)}, bf16[4,8,256]{2,1,0:T(8,128)(2,1)S(1)}, u32[]{:S(2)}, u32[]{:S(2)}) collective-permute-start(bf16[4,8,256]{2,1,0:T(8,128)(2,1)S(1)} %get-tuple-element.33), channel_id=1, source_target_pairs={{4,0},{8,4},{12,8},{16,12},{20,16},{24,20},{28,24},{32,28},{36,32}... | collective-permute-start | bytes 49160 | tf_op jit(solution)/shard_map/ppermute | solution.py:233
  22.0 7.5 %collective-permute-start.3 = (bf16[40,256]{1,0:T(8,128)(2,1)S(1)}, bf16[40,256]{1,0:T(8,128)(2,1)S(1)}, u32[]{:S(2)}, u32[]{:S(2)}) collective-permute-start(bf16[40,256]{1,0:T(8,128)(2,1)S(1)} %reshape.209), channel_id=1, source_target_pairs={{1,0},{2,1},{3,2},{5,4},{6,5},{7,6},{9,8},{10,9},{11,10},{13,12},{... | collective-permute-start | bytes 61448 | tf_op jit(solution)/shard_map/ppermute | solution.py:233
  23.4 6.1 %collective-permute-start.2 = (bf16[40,256]{1,0:T(8,128)(2,1)S(1)}, bf16[40,256]{1,0:T(8,128)(2,1)S(1)}, u32[]{:S(2)}, u32[]{:S(2)}) collective-permute-start(bf16[40,256]{1,0:T(8,128)(2,1)S(1)} %reshape.208), channel_id=1, source_target_pairs={{0,1},{1,2},{2,3},{4,5},{5,6},{6,7},{8,9},{9,10},{10,11},{12,13},{... | collective-permute-start | bytes 61448 | tf_op jit(solution)/shard_map/ppermute | solution.py:233
  29.5 2.0 %copy-start.2 = (bf16[27,256,256]{2,1,0:T(8,128)(2,1)S(1)}, bf16[27,256,256]{2,1,0:T(8,128)(2,1)}, u32[]{:S(2)}) copy-start(bf16[27,256,256]{2,1,0:T(8,128)(2,1)} %weight_ref.1) | copy-start | bytes 10616836
  31.5 0.9 copy-start.3
  32.5 0.7 copy-start.5
  33.2 0.7 copy-start.6
  33.8 0.7 copy-start.7
  40.0 4.9 %collective-permute-start.4 = (bf16[3,144,128]{2,1,0:T(8,128)(2,1)S(1)}, bf16[3,144,128]{2,1,0:T(8,128)(2,1)S(1)}, u32[]{:S(2)}, u32[]{:S(2)}) collective-permute-start(bf16[3,144,128]{2,1,0:T(8,128)(2,1)S(1)} %get-tuple-element.23.refs_0_), channel_id=1, source_target_pairs={{0,1},{1,2},{2,3},{3,0},{4,5},{5,6},{6,7},{7,4},{8,9},{9,10},{10,1... | collective-permute-start | bytes 331784 | tf_op jit(solution)/shard_map/ppermute | solution.py:238
  41.1 5.5 %collective-permute-start.5 = (bf16[3,144,128]{2,1,0:T(8,128)(2,1)S(1)}, bf16[3,144,128]{2,1,0:T(8,128)(2,1)S(1)}, u32[]{:S(2)}, u32[]{:S(2)}) collective-permute-start(bf16[3,144,128]{2,1,0:T(8,128)(2,1)S(1)} %get-tuple-element.23.refs_0_), channel_id=1, source_target_pairs={{0,2},{1,3},{2,0},{3,1},{4,6},{5,7},{6,4},{7,5},{8,10},{9,11},{10,... | collective-permute-start | bytes 331784 | tf_op jit(solution)/shard_map/ppermute | solution.py:238
  43.2 4.6 %collective-permute-start.6 = (bf16[3,144,128]{2,1,0:T(8,128)(2,1)S(1)}, bf16[3,144,128]{2,1,0:T(8,128)(2,1)S(1)}, u32[]{:S(2)}, u32[]{:S(2)}) collective-permute-start(bf16[3,144,128]{2,1,0:T(8,128)(2,1)S(1)} %get-tuple-element.23.refs_0_), channel_id=1, source_target_pairs={{0,3},{1,0},{2,1},{3,2},{4,7},{5,4},{6,5},{7,6},{8,11},{9,8},{10,9... | collective-permute-start | bytes 331784 | tf_op jit(solution)/shard_map/ppermute | solution.py:238
  94.7 3.4 %copy-start.1 = (bf16[8192,512]{1,0:T(8,128)(2,1)S(1)}, bf16[8192,512]{1,0:T(8,128)(2,1)}, u32[]{:S(2)}) copy-start(bf16[8192,512]{1,0:T(8,128)(2,1)} %all-gather.3.cloned.1.call-done) | copy-start | bytes 25165828
  105.7 7.0 %collective-permute-start.7 = (bf16[3,144,128]{2,1,0:T(8,128)(2,1)S(1)}, bf16[3,144,128]{2,1,0:T(8,128)(2,1)S(1)}, u32[]{:S(2)}, u32[]{:S(2)}) collective-permute-start(bf16[3,144,128]{2,1,0:T(8,128)(2,1)S(1)} %get-tuple-element.25), channel_id=1, source_target_pairs={{0,3},{1,0},{2,1},{3,2},{4,7},{5,4},{6,5},{7,6},{8,11},{9,8},{10,9... | collective-permute-start | bytes 331784 | tf_op jit(solution)/shard_map/ppermute | solution.py:238
  108.1 5.4 %collective-permute-start.8 = (bf16[3,144,128]{2,1,0:T(8,128)(2,1)S(1)}, bf16[3,144,128]{2,1,0:T(8,128)(2,1)S(1)}, u32[]{:S(2)}, u32[]{:S(2)}) collective-permute-start(bf16[3,144,128]{2,1,0:T(8,128)(2,1)S(1)} %get-tuple-element.26), channel_id=1, source_target_pairs={{0,2},{1,3},{2,0},{3,1},{4,6},{5,7},{6,4},{7,5},{8,10},{9,11},{10,... | collective-permute-start | bytes 331784 | tf_op jit(solution)/shard_map/ppermute | solution.py:238
  110.9 6.1 %collective-permute-start.9 = (bf16[3,144,128]{2,1,0:T(8,128)(2,1)S(1)}, bf16[3,144,128]{2,1,0:T(8,128)(2,1)S(1)}, u32[]{:S(2)}, u32[]{:S(2)}) collective-permute-start(bf16[3,144,128]{2,1,0:T(8,128)(2,1)S(1)} %get-tuple-element.27), channel_id=1, source_target_pairs={{0,1},{1,2},{2,3},{3,0},{4,5},{5,6},{6,7},{7,4},{8,9},{9,10},{10,1... | collective-permute-start | bytes 331784 | tf_op jit(solution)/shard_map/ppermute | solution.py:238
Sparse Core Ops, SparseCore 0:
  10.1 84.5 all-gather.2

commit v2 on v1

v2 whole, which is shorter than its diff:
```python
import math

import jax
import jax.numpy as jnp
from jax import lax
from jax.experimental import pallas as pl
from jax.experimental.pallas import tpu as pltpu
from jax.sharding import PartitionSpec as P

CH = 256
HEADS = 8
HEAD_DIM = 32
EDGE = 4
VX, VY, VZ = 8, 8, 4
ROWS = VX * VY * VZ
WINDOWS = 4
ACT_MAX = 3
PARENTS = 4
TOK = 128
LANES = 128
PACK = 144
SLOTS = 4
CHIP = 2 * SLOTS
RING, LINE, CORES = 8, 4, 2
PAIRS = LINE * ACT_MAX * PARENTS
SCALE = math.log2(math.e) / math.sqrt(HEAD_DIM)
LOWEST = -3e38
F32 = jnp.float32
BF16 = jnp.bfloat16
VMEM = pl.BlockSpec(memory_space=pltpu.VMEM)
SMEM = pl.BlockSpec(memory_space=pltpu.SMEM)
ANY = pl.BlockSpec(memory_space=pl.ANY)
HBM = pl.BlockSpec(memory_space=pltpu.HBM)
NT = (((1,), (1,)), ((), ()))


def row_mask(act_ref):
    low = lax.broadcasted_iota(jnp.int32, (VY, CH), 0) < EDGE
    flags = [act_ref[w].astype(F32) for w in range(WINDOWS)]
    halves = [jnp.where(low, flags[2 * b], flags[2 * b + 1]) for b in range(2)]
    return jnp.concatenate(
        [jnp.broadcast_to(half[None], (EDGE, VY, CH)) for half in halves], axis=0
    )


def rank(act_ref, w):
    place = jnp.int32(0)
    for before in range(w):
        place = place + act_ref[before]
    return place


def placement():
    row = lax.broadcasted_iota(jnp.int32, (ROWS, LANES), 0)
    lane = lax.broadcasted_iota(jnp.int32, (ROWS, LANES), 1)
    query = (row >> 6) * 16 + ((row >> 3) & 3) * 4 + (row & 3)
    return query == (lane & 63), ((row >> 5) & 1) * 2 + ((row >> 2) & 1), lane


def face_kernel(act_ref, owner_ref, slot_ref, latent_ref, gain_ref, xa_ref, xb_ref, ya_ref, yb_ref, extra_ref):
    mask = row_mask(act_ref)
    gain = gain_ref[...].reshape(1, 1, CH)

    def normed(values, flags):
        scale = lax.rsqrt(jnp.mean(values * values, axis=-1, keepdims=True) + 1e-06)
        return (flags * values * scale * gain).astype(BF16)

    for side, ref in ((0, xa_ref), (VX - 1, xb_ref)):
        ref[...] = normed(latent_ref[:, side], mask[side][None])
    for side, ref in ((0, ya_ref), (VY - 1, yb_ref)):
        ref[...] = normed(latent_ref[:, :, side, :], mask[:, side, :][None])
    row = lax.broadcasted_iota(jnp.int32, (16, LANES), 0)
    lane = lax.broadcasted_iota(jnp.int32, (16, LANES), 1)
    for s in range(ACT_MAX):
        extra = jnp.full((16, LANES), -1.0, F32)
        for w in range(WINDOWS):
            here = (act_ref[w] > 0) & (rank(act_ref, w) == s)
            for p in range(PARENTS):
                code = owner_ref[w * PARENTS + p] * SLOTS + slot_ref[w * PARENTS + p]
                code = jnp.where(here, code, -1).astype(F32)
                extra = jnp.where((row == 0) & (lane == p), jnp.maximum(extra, code), extra)
        extra_ref[s] = extra.astype(BF16)


def conv_kernel(
    act_ref, latent_ref, xlo_ref, xhi_ref, ylo_ref, yhi_ref, ngain_ref, bias_ref,
    again_ref, weight_ref, qw_ref, extra_ref, hidden_ref, query_ref,
    frame, weights, sems,
):
    copies = [
        pltpu.make_async_copy(weight_ref.at[pl.ds(3 * ab, 3)], weights.at[pl.ds(3 * ab, 3)], sems.at[ab])
        for ab in range(9)
    ]
    for copy in copies:
        copy.start()
    latent = latent_ref[...]
    mask = row_mask(act_ref)[None]
    scale = lax.rsqrt(jnp.mean(latent * latent, axis=-1, keepdims=True) + 1e-06)
    normed = mask * latent * scale * ngain_ref[...].reshape(1, 1, 1, CH)
    frame[1, :, 1 : VX + 1] = normed
    frame[1, :, 0] = xlo_ref[...].astype(F32)
    frame[1, :, VX + 1] = xhi_ref[...].astype(F32)
    ylo = ylo_ref[...].astype(F32)
    yhi = yhi_ref[...].astype(F32)
    first = lax.broadcasted_iota(jnp.int32, (VY, CH), 0) == 0
    last = lax.broadcasted_iota(jnp.int32, (VY, CH), 0) == VY - 1
    for z in range(VZ):
        for x in range(VX + 2):
            r = z * (VX + 2) + x
            here = frame[1, z, x]
            frame[0, z, x] = jnp.where(first, ylo[r : r + 1, :], pltpu.roll(here, 1, 0))
            frame[2, z, x] = jnp.where(last, yhi[r : r + 1, :], pltpu.roll(here, VY - 1, 0))
    mid = jnp.zeros((ROWS, CH), F32)
    up = jnp.zeros((ROWS - 64, CH), F32)
    down = jnp.zeros((ROWS - 64, CH), F32)
    for ab in range(9):
        copies[ab].wait()
        a, b = ab // 3, ab % 3
        slab = frame[b, :, a : a + VX].reshape(ROWS, CH).astype(BF16)
        up = up + jnp.dot(slab[: ROWS - 64], weights[3 * ab], preferred_element_type=F32)
        mid = mid + jnp.dot(slab, weights[3 * ab + 1], preferred_element_type=F32)
        down = down + jnp.dot(slab[64:], weights[3 * ab + 2], preferred_element_type=F32)
    gap = jnp.zeros((64, CH), F32)
    conv = mid + jnp.concatenate([gap, up], 0) + jnp.concatenate([down, gap], 0) + bias_ref[...]
    flat_mask = jnp.broadcast_to(mask, (VZ, VX, VY, CH)).reshape(ROWS, CH)
    hidden = latent.reshape(ROWS, CH) + flat_mask * (conv / (1.0 + jnp.exp(-conv)))
    hidden_ref[...] = hidden
    scale = lax.rsqrt(jnp.mean(hidden * hidden, axis=-1, keepdims=True) + 1e-06)
    query_in = (hidden * scale * again_ref[...]).astype(BF16)
    queries = jnp.dot(query_in, qw_ref[...], preferred_element_type=F32).T.astype(BF16)
    left = lax.broadcasted_iota(jnp.int32, (HEAD_DIM, LANES), 1) < 64
    query_ref[:, :LANES, :] = jnp.zeros((ACT_MAX, LANES, LANES), BF16)
    query_ref[:, LANES:, :] = extra_ref[...]
    fits, window, _ = placement()
    for w in range(WINDOWS):
        @pl.when(act_ref[w] > 0)
        def _(w=w):
            place = jnp.where(fits & (window == w), 1.0, 0.0).astype(BF16)
            both = jnp.dot(queries, place, preferred_element_type=F32)
            packed = [
                jnp.where(left, both[64 * j : 64 * j + 32], both[64 * j + 32 : 64 * j + 64]) for j in range(4)
            ]
            query_ref[rank(act_ref, w), :LANES, :] = jnp.concatenate(packed, axis=0).astype(BF16)


def attend_kernel(here_ref, *refs):
    query_refs, kv_refs, out_refs = refs[:LINE], refs[LINE : LINE + RING], refs[LINE + RING : 2 * LINE + RING]
    codes, code_ref, held, blocks, sums, peak, total, sems, code_sem = refs[2 * LINE + RING :]
    ring, line, core = here_ref[0], here_ref[1], here_ref[2]
    for source in range(LINE):
        for s in range(ACT_MAX):
            codes[source * ACT_MAX + s] = query_refs[source][s, LANES:, :].astype(F32).astype(jnp.int32)
    listing = pltpu.make_async_copy(codes, code_ref, code_sem)
    listing.start()
    blocks[...] = jnp.zeros_like(blocks)
    listing.wait()

    def owned(n):
        code = code_ref[n // PARENTS, 0, n % PARENTS]
        owner = code >> 2
        return (code >= 0) & (((owner >> 1) & 3) == line), ((owner >> 3) - ring) & 7, owner & 1, code & 3

    def arrival(n):
        return pltpu.make_async_copy(kv_refs[0].at[0], held.at[n], sems.at[n])

    def begin(n, carry):
        mine, ahead, owner_core, slot = owned(n)
        steps = jnp.where((ahead > 4) | ((ahead == 4) & (core == 0)), RING - ahead, ahead)
        bearer = jnp.where(ahead == 0, core, jnp.where((ahead > 4) | ((ahead == 4) & (core == 0)), 0, 1))
        array = jnp.where((ahead == 0) | (bearer == core), steps, 4 + steps)
        index = jnp.where(owner_core == bearer, 0, SLOTS) + slot
        for k in range(RING):
            @pl.when(mine & (array == k))
            def _(k=k):
                pltpu.make_async_copy(kv_refs[k].at[index], held.at[n], sems.at[n]).start()
        return carry

    lax.fori_loop(0, PAIRS, begin, 0)
    left = lax.broadcasted_iota(jnp.int32, (HEAD_DIM, LANES), 1) < 64
    for source in range(LINE):
        query_ref, out_ref = query_refs[source], out_refs[source]

        def window(s, carry, source=source, query_ref=query_ref, out_ref=out_ref):
            base = (source * ACT_MAX + s) * PARENTS
            found = owned(base)[0]
            for p in range(1, PARENTS):
                found = found | owned(base + p)[0]

            @pl.when(jnp.logical_not(found))
            def _():
                out_ref[s, :LANES, :] = jnp.zeros((LANES, LANES), BF16)
                rows = lax.broadcasted_iota(jnp.int32, (PACK - LANES, LANES), 0)
                out_ref[s, LANES:, :] = jnp.where(rows < 4, LOWEST, 0.0).astype(BF16)

            @pl.when(found)
            def _():
                for j in range(4):
                    pair = query_ref[s, 32 * j : 32 * j + 32, :].astype(F32)
                    lanes = slice(LANES * j, LANES * j + LANES)
                    blocks[64 * j : 64 * j + 32, lanes] = jnp.where(left, pair, 0.0).astype(BF16)
                    blocks[64 * j + 32 : 64 * j + 64, lanes] = jnp.where(left, 0.0, pair).astype(BF16)
                sums[...] = jnp.zeros_like(sums)
                peak[...] = jnp.full_like(peak, LOWEST)
                total[...] = jnp.zeros_like(total)

                def parent(p, carry):
                    n = base + p

                    @pl.when(owned(n)[0])
                    def _():
                        arrival(n).wait()
                        for g in range(2):
                            half = slice(LANES * g, LANES * g + LANES)
                            wide = slice(256 * g, 256 * g + 256)
                            scores = jnp.dot(held[n, :, half], blocks[half, wide], preferred_element_type=F32)
                            old = peak[:, wide]
                            new = jnp.maximum(old, jnp.max(scores, axis=0, keepdims=True))
                            lifted = jnp.exp2((scores - new) * SCALE)
                            fade = jnp.exp2((old - new) * SCALE)
                            peak[:, wide] = new
                            total[:, wide] = total[:, wide] * fade + jnp.sum(lifted, axis=0, keepdims=True)
                            mixed = jnp.dot(
                                held[n, :, CH + LANES * g : CH + LANES * g + LANES].T,
                                lifted.astype(BF16), preferred_element_type=F32,
                            )
                            for jj in range(2):
                                rows = slice(64 * (2 * g + jj), 64 * (2 * g + jj) + 64)
                                cut = slice(LANES * jj, LANES * jj + LANES)
                                sums[rows, :] = sums[rows, :] * fade[:, cut] + mixed[64 * jj : 64 * jj + 64, cut]
                    return carry

                lax.fori_loop(0, PARENTS, parent, 0)
                levels = []
                for j in range(4):
                    lanes = slice(LANES * j, LANES * j + LANES)
                    kept = jnp.where(left, sums[64 * j : 64 * j + 32, :], sums[64 * j + 32 : 64 * j + 64, :])
                    out_ref[s, 32 * j : 32 * j + 32, :] = (kept / total[:, lanes]).astype(BF16)
                    levels.append(peak[:, lanes] * SCALE + jnp.log2(total[:, lanes]))
                level = jnp.concatenate(levels, axis=0)
                high = level.astype(BF16).astype(F32)
                middle = (level - high).astype(BF16).astype(F32)
                low = level - high - middle
                stats = jnp.concatenate([high, middle, low, jnp.zeros_like(low)], axis=0)
                out_ref[s, LANES:, :] = stats.astype(BF16)
            return carry

        lax.fori_loop(0, ACT_MAX, window, 0)


def merge_kernel(act_ref, *refs):
    part_refs = refs[:LINE]
    hidden_ref, ow_ref, out_ref, mixed, attended = refs[LINE:]
    for s in range(ACT_MAX):
        stats = [ref[s, LANES:, :].astype(F32) for ref in part_refs]
        levels = [one[0:4] + one[4:8] + one[8:12] for one in stats]
        top = jnp.maximum(jnp.maximum(levels[0], levels[1]), jnp.maximum(levels[2], levels[3]))
        shares = [jnp.exp2(level - top) for level in levels]
        whole = shares[0] + shares[1] + shares[2] + shares[3]
        for j in range(4):
            rows = slice(32 * j, 32 * j + 32)
            value = jnp.zeros((HEAD_DIM, LANES), F32)
            for ref, share in zip(part_refs, shares):
                value = value + ref[s, rows, :].astype(F32) * (share / whole)[j : j + 1, :]
            mixed[s, rows, :] = value.astype(BF16)
    attended[...] = jnp.zeros_like(attended)
    fits, window, lane = placement()
    for w in range(WINDOWS):
        @pl.when(act_ref[w] > 0)
        def _(w=w):
            block = mixed[rank(act_ref, w)]
            for side in range(2):
                place = jnp.where(fits & (window == w) & ((lane >> 6) == side), 1.0, 0.0).astype(BF16)
                attended[side] += lax.dot_general(place, block, NT, preferred_element_type=F32)
    projected = jnp.zeros((ROWS, CH), F32)
    for side in range(2):
        weight = jnp.concatenate([ow_ref[64 * j + 32 * side : 64 * j + 32 * side + 32, :] for j in range(4)], axis=0)
        projected = projected + jnp.dot(attended[side].astype(BF16), weight, preferred_element_type=F32)
    mask = jnp.broadcast_to(row_mask(act_ref)[None], (VZ, VX, VY, CH)).reshape(ROWS, CH)
    out_ref[...] = mask * (hidden_ref[...] + projected)


def shift(block, axis, step):
    count = lax.axis_size(axis)
    return lax.ppermute(block, axis, [(i, i + step) for i in range(count) if 0 <= i + step < count])


def after(block, *others):
    return lax.optimization_barrier((block, *others))[0]


def move(block, rule):
    pairs = []
    for i in range(RING * LINE * CORES):
        ring, line, core = rule(i // (LINE * CORES), i // CORES % LINE, i % CORES)
        pairs.append((i, (ring % RING * LINE + line % LINE) * CORES + core))
    return lax.ppermute(block, "gx", pairs)


def per_device(
    latent, active, parent_owner, parent_slot, coarse_kv, norm_gain, conv_weight, conv_bias,
    attn_gain, q_weight, out_weight,
):
    def swapped(block):
        return move(block, lambda ring, line, core: (ring, line, 1 - core))

    def ringed(block):
        return move(block, lambda ring, line, core: (ring + 1 - 2 * core, line, core))

    chip = jnp.concatenate([coarse_kv, swapped(coarse_kv)], axis=0)
    first = ringed(chip)

    act = active.reshape(WINDOWS)
    turned = latent.transpose(2, 0, 1, 3)
    face = jax.ShapeDtypeStruct((VZ, VX, CH), BF16)
    x_first, x_last, y_first, y_last, extra = pl.pallas_call(
        face_kernel,
        out_shape=[face] * 4 + [jax.ShapeDtypeStruct((ACT_MAX, PACK - LANES, LANES), BF16)],
        in_specs=[SMEM] * 3 + [VMEM] * 2,
        out_specs=[VMEM] * 5,
        name="faces",
    )(act, parent_owner.reshape(-1), parent_slot.reshape(-1), turned, norm_gain.reshape(1, CH))
    x_last = after(x_last, chip)
    x_low, x_high = shift(x_last, "gx", 1), shift(x_first, "gx", -1)
    y_first = jnp.concatenate([x_low[:, :1], y_first, x_high[:, :1]], axis=1).reshape(-1, CH)
    y_last = jnp.concatenate([x_low[:, -1:], y_last, x_high[:, -1:]], axis=1).reshape(-1, CH)
    y_low, y_high = shift(y_last, "gy", 1), shift(y_first, "gy", -1)

    second = ringed(after(first, y_low, y_high))
    hidden, query = pl.pallas_call(
        conv_kernel,
        out_shape=(
            jax.ShapeDtypeStruct((ROWS, CH), F32),
            jax.ShapeDtypeStruct((ACT_MAX, PACK, LANES), BF16),
        ),
        in_specs=[SMEM] + [VMEM] * 8 + [HBM] + [VMEM] * 2,
        out_specs=(VMEM, VMEM),
        scratch_shapes=[
            pltpu.VMEM((3, VZ, VX + 2, VY, CH), F32),
            pltpu.VMEM((27, CH, CH), BF16),
            pltpu.SemaphoreType.DMA((9,)),
        ],
        compiler_params=pltpu.CompilerParams(vmem_limit_bytes=20 << 20),
        cost_estimate=pl.CostEstimate(flops=2 * 27 * ROWS * CH * CH, bytes_accessed=5 << 20, transcendentals=ROWS * CH),
        name="conv",
    )(
        act, turned, x_low, x_high, y_low, y_high, norm_gain.reshape(1, CH),
        conv_bias.reshape(1, CH), attn_gain.reshape(1, CH), conv_weight, q_weight, extra,
    )

    def along(block, step):
        return move(block, lambda ring, line, core: (ring, line + step, core))

    index = lax.axis_index("gx")
    here = jnp.stack([index // (LINE * CORES), index // CORES % LINE, index % CORES]).astype(jnp.int32)
    queries = [query] + [along(query, d) for d in range(1, LINE)]
    third = ringed(after(second, *queries))
    fourth = ringed(third)
    kv_all = [chip, first, second, third, fourth]
    kv_all = kv_all + [swapped(after(first, *queries)), swapped(after(second, *queries)), swapped(third)]
    parts = pl.pallas_call(
        attend_kernel,
        out_shape=[jax.ShapeDtypeStruct((ACT_MAX, PACK, LANES), BF16)] * LINE,
        in_specs=[SMEM] + [VMEM] * LINE + [ANY] * RING,
        out_specs=[VMEM] * LINE,
        scratch_shapes=[
            pltpu.VMEM((LINE * ACT_MAX, PACK - LANES, LANES), jnp.int32),
            pltpu.SMEM((LINE * ACT_MAX, PACK - LANES, LANES), jnp.int32),
            pltpu.VMEM((PAIRS, TOK, 2 * CH), BF16),
            pltpu.VMEM((CH, 2 * CH), BF16),
            pltpu.VMEM((CH, LANES), F32),
            pltpu.VMEM((1, 2 * CH), F32),
            pltpu.VMEM((1, 2 * CH), F32),
            pltpu.SemaphoreType.DMA((PAIRS,)),
            pltpu.SemaphoreType.DMA,
        ],
        compiler_params=pltpu.CompilerParams(vmem_limit_bytes=16 << 20),
        name="attend",
    )(here, *queries, *kv_all)

    merged = [parts[0]] + [along(parts[d], -d) for d in range(1, LINE)]
    out = pl.pallas_call(
        merge_kernel,
        out_shape=jax.ShapeDtypeStruct((ROWS, CH), F32),
        in_specs=[SMEM] + [VMEM] * (LINE + 2),
        out_specs=VMEM,
        scratch_shapes=[
            pltpu.VMEM((ACT_MAX, LANES, LANES), BF16),
            pltpu.VMEM((2, ROWS, LANES), F32),
        ],
        compiler_params=pltpu.CompilerParams(vmem_limit_bytes=16 << 20),
        name="merge",
    )(act, *merged, hidden, out_weight)
    return out.reshape(VZ, VX, VY, CH).transpose(1, 2, 0, 3)


def solution(mesh):
    placed = (
        P("gx", "gy", None, None),
        P("gx", "gy", None),
        P("gx", "gy", None, None),
        P("gx", "gy", None, None),
        P("gx", None, None),
        P(),
        P(),
        P(),
        P(),
        P(),
        P(),
    )
    return jax.shard_map(
        per_device, mesh=mesh, in_specs=placed, out_specs=P("gx", "gy", None, None), check_vma=False
    )
```

time: 129 us -> 122 us (0.946)
  the two profiles are of different devices: /device:TPU:49 before, /device:TPU:2 now
where the time goes in v2:
time: 122 us
  waiting for transfers between devices  47.2 us (39%)
  starting transfers between devices  31.8 us (26%)
  Pallas kernels  20.1 us (16%)
  local copies, waits for them, and re-layouts  19.4 us (16%)
  other arithmetic  2.89 us (2%)
    ppermute x14, waiting for transfers between devices, move(): return lax.ppermute(block, 'gx', pairs)  43 us
    ppermute x14, starting transfers between devices, move(): return lax.ppermute(block, 'gx', pairs)  18.3 us
    unnamed x35, local copies, waits for them, and re-layouts  15.2 us
    ppermute x4, starting transfers between devices, shift(): lax.ppermute(block, axis, [(i, i + step) for i in range(count) if 0 <= i...  13.4 us
    pallas_call x1, Pallas kernels, per_device(): pl.pallas_call(attend_kernel, out_shape=[jax.ShapeDtypeStruct((ACT_MAX, P...  11.2 us
    pallas_call x1, Pallas kernels, per_device(): pl.pallas_call(conv_kernel, out_shape=(jax.ShapeDtypeStruct((ROWS, CH), F...  5.56 us
    ppermute x4, waiting for transfers between devices, shift(): lax.ppermute(block, axis, [(i, i + step) for i in range(count) if 0 <= i...  4.23 us
  transfers between devices with their start and end apart: 18, of which 12 were waited for; matrix products, arithmetic and copies ran while one was open for 8% of the time, Pallas kernels for 6%

profile of v2, /device:TPU:2, one launch (start us, length us, event | category | flops | bytes accessed | tf_op | source)
XLA Modules:
  0.0 121.5 jit_solution(15687719153185271510)
XLA Ops:
  0.0 1.1 constant_dynamic-update-slice_fusion.1
  1.1 1.0 collective-permute-done
  2.2 2.0 %collective-permute-start.8 = (bf16[8,128,512]{2,1,0:T(8,128)(2,1)S(1)}, bf16[8,128,512]{2,1,0:T(8,128)(2,1)S(1)}, u32[]{:S(2)}, u32[]{:S(2)}) collective-permute-start(bf16[8,128,512]{2,1,0:T(8,128)(2,1)S(1)} %constant_dynamic-update-slice_fusion.refs_4_), channel_id=1, source_target_pairs={{0,32},{4,228},{8,40},{12,236},{16,48},{20,244},{24,56},{28,252},{... | collective-permute-start | bytes 3145736 | tf_op jit(solution)/shard_map/ppermute | solution.py:296
  4.7 1.3 %reduce.3 = s32[2,2]{1,0:T(2,128)S(1)} reduce(s32[2,2,1]{1,2,0:T(1,128)} %param.12, s32[]{:T(128)} %broadcast.7), dimensions={2}, to_apply=%param.12.reduce_sub_computation.3 | reduce | bytes 36 | tf_op args[1]
  6.7 1.3 %reshape.29.owner_ref = s32[16]{0:T(128)} reshape(s32[1,1,4,4]{3,2,1,0:T(4,128)} %param.13) | data formatting | bytes 128 | tf_op jit(solution)/shard_map/reshape | solution.py:321
  8.0 1.3 %reshape.30.slot_ref = s32[16]{0:T(128)} reshape(s32[1,1,4,4]{3,2,1,0:T(4,128)} %param.14) | data formatting | bytes 128 | tf_op jit(solution)/shard_map/reshape | solution.py:321
  9.3 1.7 %copy.19 = f32[8,8,4,256]{3,1,0,2:T(8,128)} copy(f32[8,8,4,256]{3,2,1,0:T(4,128)} %param.11) | data formatting | bytes 524288 | tf_op args[0]
  11.0 1.7 %faces.1 = (bf16[4,8,256]{2,1,0:T(8,128)(2,1)}, bf16[4,8,256]{2,1,0:T(8,128)(2,1)}, bf16[4,8,256]{2,1,0:T(8,128)(2,1)}, bf16[4,8,256]{2,1,0:T(8,128)(2,1)}, bf16[3,16,128]{2,1,0:T(8,128)(2,1)}) custom-call(s32[4]{0:T(128)} %reshape.28.act_ref, s32[16]{0:T(128)} %reshape.29.owner_ref, s32[16]{0:T(128)} %reshape.30.slot_ref, f32[4,8,8,256]{3,2,1,0:T(8,128)} %bitcast.14, ...), custom_call_target="tpu_custom_call" | custom-call | tf_op jit(solution)/shard_map/faces/pallas_call | solution.py:315
  12.7 1.3 %collective-permute-start.2 = (bf16[4,8,256]{2,1,0:T(8,128)(2,1)}, bf16[4,8,256]{2,1,0:T(8,128)(2,1)S(1)}, u32[]{:S(2)}, u32[]{:S(2)}) collective-permute-start(bf16[4,8,256]{2,1,0:T(8,128)(2,1)} %get-tuple-element.22), channel_id=1, source_target_pairs={{4,0},{8,4},{12,8},{16,12},{20,16},{24,20},{28,24},{32,28},{36,32}... | collective-permute-start | bytes 49160 | tf_op jit(solution)/shard_map/ppermute | solution.py:284
  14.0 6.3 %collective-permute-start.1 = (bf16[4,8,256]{2,1,0:T(8,128)(2,1)}, bf16[4,8,256]{2,1,0:T(8,128)(2,1)S(1)}, u32[]{:S(2)}, u32[]{:S(2)}) collective-permute-start(bf16[4,8,256]{2,1,0:T(8,128)(2,1)} %get-tuple-element.21), channel_id=1, source_target_pairs={{0,4},{4,8},{8,12},{12,16},{16,20},{20,24},{24,28},{28,32},{32,36}... | collective-permute-start | bytes 49160 | tf_op jit(solution)/shard_map/ppermute | solution.py:284
  20.3 1.0 collective-permute-done.1.xlo_ref
  22.9 3.4 %collective-permute-start.3 = (bf16[40,256]{1,0:T(8,128)(2,1)S(1)}, bf16[40,256]{1,0:T(8,128)(2,1)S(1)}, u32[]{:S(2)}, u32[]{:S(2)}) collective-permute-start(bf16[40,256]{1,0:T(8,128)(2,1)S(1)} %reshape.32), channel_id=1, source_target_pairs={{0,1},{1,2},{2,3},{4,5},{5,6},{6,7},{8,9},{9,10},{10,11},{12,13},{... | collective-permute-start | bytes 61448 | tf_op jit(solution)/shard_map/ppermute | solution.py:284
  26.3 2.4 %collective-permute-start.4 = (bf16[40,256]{1,0:T(8,128)(2,1)S(1)}, bf16[40,256]{1,0:T(8,128)(2,1)S(1)}, u32[]{:S(2)}, u32[]{:S(2)}) collective-permute-start(bf16[40,256]{1,0:T(8,128)(2,1)S(1)} %reshape.33), channel_id=1, source_target_pairs={{1,0},{2,1},{3,2},{5,4},{6,5},{7,6},{9,8},{10,9},{11,10},{13,12},{... | collective-permute-start | bytes 61448 | tf_op jit(solution)/shard_map/ppermute | solution.py:284
  28.8 3.2 %collective-permute-done.4.yhi_ref = bf16[40,256]{1,0:T(8,128)(2,1)S(1)} collective-permute-done((bf16[40,256]{1,0:T(8,128)(2,1)S(1)}, bf16[40,256]{1,0:T(8,128)(2,1)S(1)}, u32[]{:S(2)}, u32[]{:S(2)}) %collective-permute-start.4) | collective-permute-done | bytes 20512 | tf_op jit(solution)/shard_map/ppermute | solution.py:284
  32.0 8.5 %collective-permute-start.9 = (bf16[8,128,512]{2,1,0:T(8,128)(2,1)S(1)}, bf16[8,128,512]{2,1,0:T(8,128)(2,1)S(1)}, u32[]{:S(2)}, u32[]{:S(2)}) collective-permute-start(bf16[8,128,512]{2,1,0:T(8,128)(2,1)S(1)} %collective-permute-done.8.refs_5_), channel_id=1, source_target_pairs={{0,32},{4,228},{8,40},{12,236},{16,48},{20,244},{24,56},{28,252},{... | collective-permute-start | bytes 3145736 | tf_op jit(solution)/shard_map/ppermute | solution.py:296
  40.5 2.0 %copy-done = bf16[27,256,256]{2,1,0:T(8,128)(2,1)S(1)} copy-done((bf16[27,256,256]{2,1,0:T(8,128)(2,1)S(1)}, bf16[27,256,256]{2,1,0:T(8,128)(2,1)}, u32[]{:S(2)}) %copy-start) | copy-done | bytes 3538968
  42.5 0.9 copy-done.1
  43.4 0.9 copy-done.2
  47.8 5.6 %conv.1 = (f32[256,256]{1,0:T(8,128)S(1)}, bf16[3,144,128]{2,1,0:T(8,128)(2,1)S(1)}) custom-call(s32[4]{0:T(128)S(1)} %copy-done.11, f32[4,8,8,256]{3,2,1,0:T(8,128)S(1)} %bitcast.15, bf16[4,8,256]{2,1,0:T(8,128)(2,1)S(1)} %collective-permute-done.1.xlo_ref, bf16[4,8,256]{2,1,0:T(8,128)(2,1)S(1)} %collective-permute-done.2.xhi_ref, ...), custom_call_target="tpu_custom_call" | custom-call | flops 905969664 | bytes 5242880 | tf_op jit(solution)/shard_map/conv/pallas_call | solution.py:329
  53.5 1.9 %collective-permute-start.5 = (bf16[3,144,128]{2,1,0:T(8,128)(2,1)S(1)}, bf16[3,144,128]{2,1,0:T(8,128)(2,1)S(1)}, u32[]{:S(2)}, u32[]{:S(2)}) collective-permute-start(bf16[3,144,128]{2,1,0:T(8,128)(2,1)S(1)} %get-tuple-element.26.refs_0_), channel_id=1, source_target_pairs={{0,8},{4,12},{8,16},{12,20},{16,24},{20,28},{24,0},{28,4},{32,40},... | collective-permute-start | bytes 331784 | tf_op jit(solution)/shard_map/ppermute | solution.py:296
  55.4 2.7 %collective-permute-done.7.refs_3_ = bf16[3,144,128]{2,1,0:T(8,128)(2,1)S(1)} collective-permute-done((bf16[3,144,128]{2,1,0:T(8,128)(2,1)S(1)}, bf16[3,144,128]{2,1,0:T(8,128)(2,1)S(1)}, u32[]{:S(2)}, u32[]{:S(2)}) %collective-permute-start.7) | collective-permute-done | bytes 110624 | tf_op jit(solution)/shard_map/ppermute | solution.py:296
  58.8 1.0 collective-permute-done.6.refs_2_
  62.2 15.5 %collective-permute-done.10.refs_7_ = bf16[8,128,512]{2,1,0:T(8,128)(2,1)} collective-permute-done((bf16[8,128,512]{2,1,0:T(8,128)(2,1)S(1)}, bf16[8,128,512]{2,1,0:T(8,128)(2,1)}, u32[]{:S(2)}, u32[]{:S(2)}) %collective-permute-start.10) | collective-permute-done | bytes 1048608 | tf_op jit(solution)/shard_map/ppermute | solution.py:296
  77.8 2.9 %collective-permute-done.14.refs_11_ = bf16[8,128,512]{2,1,0:T(8,128)(2,1)} collective-permute-done((bf16[8,128,512]{2,1,0:T(8,128)(2,1)}, bf16[8,128,512]{2,1,0:T(8,128)(2,1)}, u32[]{:S(2)}, u32[]{:S(2)}) %collective-permute-start.14) | collective-permute-done | bytes 1048608 | tf_op jit(solution)/shard_map/ppermute | solution.py:296
  80.7 13.3 %collective-permute-done.11.refs_8_ = bf16[8,128,512]{2,1,0:T(8,128)(2,1)} collective-permute-done((bf16[8,128,512]{2,1,0:T(8,128)(2,1)}, bf16[8,128,512]{2,1,0:T(8,128)(2,1)}, u32[]{:S(2)}, u32[]{:S(2)}) %collective-permute-start.11) | collective-permute-done | bytes 1048608 | tf_op jit(solution)/shard_map/ppermute | solution.py:296
  94.0 0.9 copy-done.5
  96.7 11.2 %attend.1 = (bf16[3,144,128]{2,1,0:T(8,128)(2,1)S(1)}, bf16[3,144,128]{2,1,0:T(8,128)(2,1)S(1)}, bf16[3,144,128]{2,1,0:T(8,128)(2,1)S(1)}, bf16[3,144,128]{2,1,0:T(8,128)(2,1)S(1)}) custom-call(s32[3]{0:T(128)S(1)} %pad_add_fusion.here_ref, bf16[3,144,128]{2,1,0:T(8,128)(2,1)S(1)} %get-tuple-element.26.refs_0_, bf16[3,144,128]{2,1,0:T(8,128)(2,1)S(1)} %copy-done.9, ...), custom_call_target="tpu_custom_call" | custom-call | tf_op jit(solution)/shard_map/attend/pallas_call | solution.py:360
  108.0 2.6 %collective-permute-start.15 = (bf16[3,144,128]{2,1,0:T(8,128)(2,1)S(1)}, bf16[3,144,128]{2,1,0:T(8,128)(2,1)S(1)}, u32[]{:S(2)}, u32[]{:S(2)}) collective-permute-start(bf16[3,144,128]{2,1,0:T(8,128)(2,1)S(1)} %get-tuple-element.31), channel_id=1, source_target_pairs={{0,24},{4,28},{8,0},{12,4},{16,8},{20,12},{24,16},{28,20},{32,56},... | collective-permute-start | bytes 331784 | tf_op jit(solution)/shard_map/ppermute | solution.py:296
  110.6 2.5 %collective-permute-start.16 = (bf16[3,144,128]{2,1,0:T(8,128)(2,1)S(1)}, bf16[3,144,128]{2,1,0:T(8,128)(2,1)S(1)}, u32[]{:S(2)}, u32[]{:S(2)}) collective-permute-start(bf16[3,144,128]{2,1,0:T(8,128)(2,1)S(1)} %get-tuple-element.32), channel_id=1, source_target_pairs={{0,16},{4,20},{8,24},{12,28},{16,0},{20,4},{24,8},{28,12},{32,48},... | collective-permute-start | bytes 331784 | tf_op jit(solution)/shard_map/ppermute | solution.py:296
  113.8 3.1 %collective-permute-done.16.refs_2_ = bf16[3,144,128]{2,1,0:T(8,128)(2,1)S(1)} collective-permute-done((bf16[3,144,128]{2,1,0:T(8,128)(2,1)S(1)}, bf16[3,144,128]{2,1,0:T(8,128)(2,1)S(1)}, u32[]{:S(2)}, u32[]{:S(2)}) %collective-permute-start.16) | collective-permute-done | bytes 110624 | tf_op jit(solution)/shard_map/ppermute | solution.py:296
  116.8 2.2 %collective-permute-done.17.refs_3_ = bf16[3,144,128]{2,1,0:T(8,128)(2,1)S(1)} collective-permute-done((bf16[3,144,128]{2,1,0:T(8,128)(2,1)S(1)}, bf16[3,144,128]{2,1,0:T(8,128)(2,1)S(1)}, u32[]{:S(2)}, u32[]{:S(2)}) %collective-permute-start.17) | collective-permute-done | bytes 110624 | tf_op jit(solution)/shard_map/ppermute | solution.py:296
  119.1 1.6 %merge.1 = f32[256,256]{1,0:T(8,128)S(1)} custom-call(s32[4]{0:T(128)S(1)} %copy-done.12, bf16[3,144,128]{2,1,0:T(8,128)(2,1)S(1)} %get-tuple-element.30.refs_0_, bf16[3,144,128]{2,1,0:T(8,128)(2,1)S(1)} %collective-permute-done.15.refs_1_, bf16[3,144,128]{2,1,0:T(8,128)(2,1)S(1)} %collective-permute-done.16.refs_2_, ...), custom_call_target="tpu_custom_call" | custom-call | tf_op jit(solution)/shard_map/merge/pallas_call | solution.py:381
  (56 shorter events, 12.8 us)
Async XLA Ops:
  0.0 2.1 %collective-permute-start = (bf16[4,128,512]{2,1,0:T(8,128)(2,1)}, bf16[4,128,512]{2,1,0:T(8,128)(2,1)S(1)}, u32[]{:S(2)}, u32[]{:S(2)}) collective-permute-start(bf16[4,128,512]{2,1,0:T(8,128)(2,1)} %param.15), channel_id=1, source_target_pairs={{0,4},{4,0},{8,12},{12,8},{16,20},{20,16},{24,28},{28,24},{32,36},... | collective-permute-start | bytes 1572872 | tf_op jit(solution)/shard_map/ppermute | solution.py:296
  2.2 29.8 %collective-permute-start.8 = (bf16[8,128,512]{2,1,0:T(8,128)(2,1)S(1)}, bf16[8,128,512]{2,1,0:T(8,128)(2,1)S(1)}, u32[]{:S(2)}, u32[]{:S(2)}) collective-permute-start(bf16[8,128,512]{2,1,0:T(8,128)(2,1)S(1)} %constant_dynamic-update-slice_fusion.refs_4_), channel_id=1, source_target_pairs={{0,32},{4,228},{8,40},{12,236},{16,48},{20,244},{24,56},{28,252},{... | collective-permute-start | bytes 3145736 | tf_op jit(solution)/shard_map/ppermute | solution.py:296
  12.7 7.6 %collective-permute-start.2 = (bf16[4,8,256]{2,1,0:T(8,128)(2,1)}, bf16[4,8,256]{2,1,0:T(8,128)(2,1)S(1)}, u32[]{:S(2)}, u32[]{:S(2)}) collective-permute-start(bf16[4,8,256]{2,1,0:T(8,128)(2,1)} %get-tuple-element.22), channel_id=1, source_target_pairs={{4,0},{8,4},{12,8},{16,12},{20,16},{24,20},{28,24},{32,28},{36,32}... | collective-permute-start | bytes 49160 | tf_op jit(solution)/shard_map/ppermute | solution.py:284
  14.0 7.4 %collective-permute-start.1 = (bf16[4,8,256]{2,1,0:T(8,128)(2,1)}, bf16[4,8,256]{2,1,0:T(8,128)(2,1)S(1)}, u32[]{:S(2)}, u32[]{:S(2)}) collective-permute-start(bf16[4,8,256]{2,1,0:T(8,128)(2,1)} %get-tuple-element.21), channel_id=1, source_target_pairs={{0,4},{4,8},{8,12},{12,16},{16,20},{20,24},{24,28},{28,32},{32,36}... | collective-permute-start | bytes 49160 | tf_op jit(solution)/shard_map/ppermute | solution.py:284
  22.9 5.9 %collective-permute-start.3 = (bf16[40,256]{1,0:T(8,128)(2,1)S(1)}, bf16[40,256]{1,0:T(8,128)(2,1)S(1)}, u32[]{:S(2)}, u32[]{:S(2)}) collective-permute-start(bf16[40,256]{1,0:T(8,128)(2,1)S(1)} %reshape.32), channel_id=1, source_target_pairs={{0,1},{1,2},{2,3},{4,5},{5,6},{6,7},{8,9},{9,10},{10,11},{12,13},{... | collective-permute-start | bytes 61448 | tf_op jit(solution)/shard_map/ppermute | solution.py:284
  26.3 5.7 %collective-permute-start.4 = (bf16[40,256]{1,0:T(8,128)(2,1)S(1)}, bf16[40,256]{1,0:T(8,128)(2,1)S(1)}, u32[]{:S(2)}, u32[]{:S(2)}) collective-permute-start(bf16[40,256]{1,0:T(8,128)(2,1)S(1)} %reshape.33), channel_id=1, source_target_pairs={{1,0},{2,1},{3,2},{5,4},{6,5},{7,6},{9,8},{10,9},{11,10},{13,12},{... | collective-permute-start | bytes 61448 | tf_op jit(solution)/shard_map/ppermute | solution.py:284
  32.0 29.6 %collective-permute-start.9 = (bf16[8,128,512]{2,1,0:T(8,128)(2,1)S(1)}, bf16[8,128,512]{2,1,0:T(8,128)(2,1)S(1)}, u32[]{:S(2)}, u32[]{:S(2)}) collective-permute-start(bf16[8,128,512]{2,1,0:T(8,128)(2,1)S(1)} %collective-permute-done.8.refs_5_), channel_id=1, source_target_pairs={{0,32},{4,228},{8,40},{12,236},{16,48},{20,244},{24,56},{28,252},{... | collective-permute-start | bytes 3145736 | tf_op jit(solution)/shard_map/ppermute | solution.py:296
  40.5 2.0 %copy-start = (bf16[27,256,256]{2,1,0:T(8,128)(2,1)S(1)}, bf16[27,256,256]{2,1,0:T(8,128)(2,1)}, u32[]{:S(2)}) copy-start(bf16[27,256,256]{2,1,0:T(8,128)(2,1)} %weight_ref.1) | copy-start | bytes 10616836
  42.5 0.9 copy-start.1
  43.4 0.9 copy-start.2
  44.3 0.7 copy-start.10
  45.0 0.7 copy-start.11
  45.7 0.7 copy-start.13
  46.4 0.7 copy-start.14
  47.1 0.7 copy-start.15
  53.3 4.8 %collective-permute-start.7 = (bf16[3,144,128]{2,1,0:T(8,128)(2,1)S(1)}, bf16[3,144,128]{2,1,0:T(8,128)(2,1)S(1)}, u32[]{:S(2)}, u32[]{:S(2)}) collective-permute-start(bf16[3,144,128]{2,1,0:T(8,128)(2,1)S(1)} %get-tuple-element.26.refs_0_), channel_id=1, source_target_pairs={{0,24},{4,28},{8,0},{12,4},{16,8},{20,12},{24,16},{28,20},{32,56},... | collective-permute-start | bytes 331784 | tf_op jit(solution)/shard_map/ppermute | solution.py:296
  53.4 6.4 %collective-permute-start.6 = (bf16[3,144,128]{2,1,0:T(8,128)(2,1)S(1)}, bf16[3,144,128]{2,1,0:T(8,128)(2,1)S(1)}, u32[]{:S(2)}, u32[]{:S(2)}) collective-permute-start(bf16[3,144,128]{2,1,0:T(8,128)(2,1)S(1)} %get-tuple-element.26.refs_0_), channel_id=1, source_target_pairs={{0,16},{4,20},{8,24},{12,28},{16,0},{20,4},{24,8},{28,12},{32,48},... | collective-permute-start | bytes 331784 | tf_op jit(solution)/shard_map/ppermute | solution.py:296
  53.5 7.4 %collective-permute-start.5 = (bf16[3,144,128]{2,1,0:T(8,128)(2,1)S(1)}, bf16[3,144,128]{2,1,0:T(8,128)(2,1)S(1)}, u32[]{:S(2)}, u32[]{:S(2)}) collective-permute-start(bf16[3,144,128]{2,1,0:T(8,128)(2,1)S(1)} %get-tuple-element.26.refs_0_), channel_id=1, source_target_pairs={{0,8},{4,12},{8,16},{12,20},{16,24},{20,28},{24,0},{28,4},{32,40},... | collective-permute-start | bytes 331784 | tf_op jit(solution)/shard_map/ppermute | solution.py:296
  59.8 0.7 copy-start.6
  61.6 16.1 %collective-permute-start.10 = (bf16[8,128,512]{2,1,0:T(8,128)(2,1)S(1)}, bf16[8,128,512]{2,1,0:T(8,128)(2,1)}, u32[]{:S(2)}, u32[]{:S(2)}) collective-permute-start(bf16[8,128,512]{2,1,0:T(8,128)(2,1)S(1)} %collective-permute-done.9.refs_6_), channel_id=1, source_target_pairs={{0,32},{4,228},{8,40},{12,236},{16,48},{20,244},{24,56},{28,252},{... | collective-permute-start | bytes 3145736 | tf_op jit(solution)/shard_map/ppermute | solution.py:296
  61.7 16.1 %collective-permute-start.12 = (bf16[8,128,512]{2,1,0:T(8,128)(2,1)S(1)}, bf16[8,128,512]{2,1,0:T(8,128)(2,1)}, u32[]{:S(2)}, u32[]{:S(2)}) collective-permute-start(bf16[8,128,512]{2,1,0:T(8,128)(2,1)S(1)} %collective-permute-done.8.refs_5_), channel_id=1, source_target_pairs={{0,4},{4,0},{8,12},{12,8},{16,20},{20,16},{24,28},{28,24},{32,36},... | collective-permute-start | bytes 3145736 | tf_op jit(solution)/shard_map/ppermute | solution.py:296
  61.7 16.1 %collective-permute-start.13 = (bf16[8,128,512]{2,1,0:T(8,128)(2,1)S(1)}, bf16[8,128,512]{2,1,0:T(8,128)(2,1)}, u32[]{:S(2)}, u32[]{:S(2)}) collective-permute-start(bf16[8,128,512]{2,1,0:T(8,128)(2,1)S(1)} %collective-permute-done.9.refs_6_), channel_id=1, source_target_pairs={{0,4},{4,0},{8,12},{12,8},{16,20},{20,16},{24,28},{28,24},{32,36},... | collective-permute-start | bytes 3145736 | tf_op jit(solution)/shard_map/ppermute | solution.py:296
  77.7 3.0 %collective-permute-start.14 = (bf16[8,128,512]{2,1,0:T(8,128)(2,1)}, bf16[8,128,512]{2,1,0:T(8,128)(2,1)}, u32[]{:S(2)}, u32[]{:S(2)}) collective-permute-start(bf16[8,128,512]{2,1,0:T(8,128)(2,1)} %collective-permute-done.10.refs_7_), channel_id=1, source_target_pairs={{0,4},{4,0},{8,12},{12,8},{16,20},{20,16},{24,28},{28,24},{32,36},... | collective-permute-start | bytes 3145736 | tf_op jit(solution)/shard_map/ppermute | solution.py:296
  77.7 16.3 %collective-permute-start.11 = (bf16[8,128,512]{2,1,0:T(8,128)(2,1)}, bf16[8,128,512]{2,1,0:T(8,128)(2,1)}, u32[]{:S(2)}, u32[]{:S(2)}) collective-permute-start(bf16[8,128,512]{2,1,0:T(8,128)(2,1)} %collective-permute-done.10.refs_7_), channel_id=1, source_target_pairs={{0,32},{4,228},{8,40},{12,236},{16,48},{20,244},{24,56},{28,252},{... | collective-permute-start | bytes 3145736 | tf_op jit(solution)/shard_map/ppermute | solution.py:296
  77.7 41.4 %copy-start.12 = (s32[4]{0:T(128)S(1)}, s32[4]{0:T(128)}, u32[]{:S(2)}) copy-start(s32[4]{0:T(128)} %reshape.28.act_ref) | copy-start | bytes 52
  77.8 41.3 %copy-start.3 = (bf16[256,256]{1,0:T(8,128)(2,1)S(1)}, bf16[256,256]{1,0:T(8,128)(2,1)}, u32[]{:S(2)}) copy-start(bf16[256,256]{1,0:T(8,128)(2,1)} %refs_5_.1) | copy-start | bytes 393220
  94.0 0.9 copy-start.5
  94.9 0.9 copy-start.7
  95.8 0.9 copy-start.9
  108.0 5.8 %collective-permute-start.15 = (bf16[3,144,128]{2,1,0:T(8,128)(2,1)S(1)}, bf16[3,144,128]{2,1,0:T(8,128)(2,1)S(1)}, u32[]{:S(2)}, u32[]{:S(2)}) collective-permute-start(bf16[3,144,128]{2,1,0:T(8,128)(2,1)S(1)} %get-tuple-element.31), channel_id=1, source_target_pairs={{0,24},{4,28},{8,0},{12,4},{16,8},{20,12},{24,16},{28,20},{32,56},... | collective-permute-start | bytes 331784 | tf_op jit(solution)/shard_map/ppermute | solution.py:296
  110.6 6.3 %collective-permute-start.16 = (bf16[3,144,128]{2,1,0:T(8,128)(2,1)S(1)}, bf16[3,144,128]{2,1,0:T(8,128)(2,1)S(1)}, u32[]{:S(2)}, u32[]{:S(2)}) collective-permute-start(bf16[3,144,128]{2,1,0:T(8,128)(2,1)S(1)} %get-tuple-element.32), channel_id=1, source_target_pairs={{0,16},{4,20},{8,24},{12,28},{16,0},{20,4},{24,8},{28,12},{32,48},... | collective-permute-start | bytes 331784 | tf_op jit(solution)/shard_map/ppermute | solution.py:296
  113.1 6.0 %collective-permute-start.17 = (bf16[3,144,128]{2,1,0:T(8,128)(2,1)S(1)}, bf16[3,144,128]{2,1,0:T(8,128)(2,1)S(1)}, u32[]{:S(2)}, u32[]{:S(2)}) collective-permute-start(bf16[3,144,128]{2,1,0:T(8,128)(2,1)S(1)} %get-tuple-element.33), channel_id=1, source_target_pairs={{0,8},{4,12},{8,16},{12,20},{16,24},{20,28},{24,0},{28,4},{32,40},... | collective-permute-start | bytes 331784 | tf_op jit(solution)/shard_map/ppermute | solution.py:296
  (2 other events, 1.3 us)

commit v3 on v2

--- a/solution.py
+++ b/solution.py
@@ -23,6 +23,7 @@
 CHIP = 2 * SLOTS
 RING, LINE, CORES = 8, 4, 2
 PAIRS = LINE * ACT_MAX * PARENTS
+GROUP = 4
 SCALE = math.log2(math.e) / math.sqrt(HEAD_DIM)
 LOWEST = -3e38
 F32 = jnp.float32
@@ -36,7 +37,7 @@
 
 def row_mask(act_ref):
     low = lax.broadcasted_iota(jnp.int32, (VY, CH), 0) < EDGE
-    flags = [act_ref[w].astype(F32) for w in range(WINDOWS)]
+    flags = [act_ref[w // 2, w % 2, 0].astype(F32) for w in range(WINDOWS)]
     halves = [jnp.where(low, flags[2 * b], flags[2 * b + 1]) for b in range(2)]
     return jnp.concatenate(
         [jnp.broadcast_to(half[None], (EDGE, VY, CH)) for half in halves], axis=0
@@ -46,7 +47,7 @@
 def rank(act_ref, w):
     place = jnp.int32(0)
     for before in range(w):
-        place = place + act_ref[before]
+        place = place + act_ref[before // 2, before % 2, 0]
     return place
 
 
@@ -57,7 +58,12 @@
     return query == (lane & 63), ((row >> 5) & 1) * 2 + ((row >> 2) & 1), lane
 
 
-def face_kernel(act_ref, owner_ref, slot_ref, latent_ref, gain_ref, xa_ref, xb_ref, ya_ref, yb_ref, extra_ref):
+def face_kernel(
+    act_ref, owner_ref, slot_ref, latent_ref, gain_ref, xa_ref, xb_ref, ya_ref, yb_ref, extra_ref, turned_ref
+):
+    for z in range(VZ):
+        for x in range(VX):
+            turned_ref[z, x] = latent_ref[x, :, z, :]
     mask = row_mask(act_ref)
     gain = gain_ref[...].reshape(1, 1, CH)
 
@@ -66,17 +72,17 @@
         return (flags * values * scale * gain).astype(BF16)
 
     for side, ref in ((0, xa_ref), (VX - 1, xb_ref)):
-        ref[...] = normed(latent_ref[:, side], mask[side][None])
+        ref[...] = normed(turned_ref[:, side], mask[side][None])
     for side, ref in ((0, ya_ref), (VY - 1, yb_ref)):
-        ref[...] = normed(latent_ref[:, :, side, :], mask[:, side, :][None])
+        ref[...] = normed(turned_ref[:, :, side, :], mask[:, side, :][None])
     row = lax.broadcasted_iota(jnp.int32, (16, LANES), 0)
     lane = lax.broadcasted_iota(jnp.int32, (16, LANES), 1)
     for s in range(ACT_MAX):
         extra = jnp.full((16, LANES), -1.0, F32)
         for w in range(WINDOWS):
-            here = (act_ref[w] > 0) & (rank(act_ref, w) == s)
+            here = (act_ref[w // 2, w % 2, 0] > 0) & (rank(act_ref, w) == s)
             for p in range(PARENTS):
-                code = owner_ref[w * PARENTS + p] * SLOTS + slot_ref[w * PARENTS + p]
+                code = owner_ref[0, 0, w, p] * SLOTS + slot_ref[0, 0, w, p]
                 code = jnp.where(here, code, -1).astype(F32)
                 extra = jnp.where((row == 0) & (lane == p), jnp.maximum(extra, code), extra)
         extra_ref[s] = extra.astype(BF16)
@@ -133,7 +139,7 @@
     query_ref[:, LANES:, :] = extra_ref[...]
     fits, window, _ = placement()
     for w in range(WINDOWS):
-        @pl.when(act_ref[w] > 0)
+        @pl.when(act_ref[w // 2, w % 2, 0] > 0)
         def _(w=w):
             place = jnp.where(fits & (window == w), 1.0, 0.0).astype(BF16)
             both = jnp.dot(queries, place, preferred_element_type=F32)
@@ -145,14 +151,26 @@
 
 def attend_kernel(here_ref, *refs):
     query_refs, kv_refs, out_refs = refs[:LINE], refs[LINE : LINE + RING], refs[LINE + RING : 2 * LINE + RING]
-    codes, code_ref, held, blocks, sums, peak, total, sems, code_sem = refs[2 * LINE + RING :]
-    ring, line, core = here_ref[0], here_ref[1], here_ref[2]
+    codes, code_ref, list_ref, held, blocks, values, levels, sems, code_sem = refs[2 * LINE + RING :]
+    here = here_ref[0]
+    ring, line, core = here >> 3, (here >> 1) & 3, here & 1
     for source in range(LINE):
         for s in range(ACT_MAX):
             codes[source * ACT_MAX + s] = query_refs[source][s, LANES:, :].astype(F32).astype(jnp.int32)
     listing = pltpu.make_async_copy(codes, code_ref, code_sem)
     listing.start()
-    blocks[...] = jnp.zeros_like(blocks)
+    left = lax.broadcasted_iota(jnp.int32, (HEAD_DIM, LANES), 1) < 64
+    none = jnp.zeros((64, LANES), BF16)
+    for source in range(LINE):
+        for s in range(ACT_MAX):
+            w = source * ACT_MAX + s
+            for j in range(4):
+                pair = query_refs[source][s, 32 * j : 32 * j + 32, :].astype(F32)
+                lanes = slice(LANES * (j % 2), LANES * (j % 2) + LANES)
+                beside = slice(LANES * (1 - j % 2), LANES * (1 - j % 2) + LANES)
+                blocks[w, 64 * j : 64 * j + 32, lanes] = jnp.where(left, pair, 0.0).astype(BF16)
+                blocks[w, 64 * j + 32 : 64 * j + 64, lanes] = jnp.where(left, 0.0, pair).astype(BF16)
+                blocks[w, 64 * j : 64 * j + 64, beside] = none
     listing.wait()
 
     def owned(n):
@@ -160,91 +178,101 @@
         owner = code >> 2
         return (code >= 0) & (((owner >> 1) & 3) == line), ((owner >> 3) - ring) & 7, owner & 1, code & 3
 
-    def arrival(n):
-        return pltpu.make_async_copy(kv_refs[0].at[0], held.at[n], sems.at[n])
-
-    def begin(n, carry):
+    def begin(n, count):
         mine, ahead, owner_core, slot = owned(n)
-        steps = jnp.where((ahead > 4) | ((ahead == 4) & (core == 0)), RING - ahead, ahead)
-        bearer = jnp.where(ahead == 0, core, jnp.where((ahead > 4) | ((ahead == 4) & (core == 0)), 0, 1))
+        below = (ahead > 4) | ((ahead == 4) & (core == 0))
+        steps = jnp.where(below, RING - ahead, ahead)
+        bearer = jnp.where(ahead == 0, core, jnp.where(below, 0, 1))
         array = jnp.where((ahead == 0) | (bearer == core), steps, 4 + steps)
         index = jnp.where(owner_core == bearer, 0, SLOTS) + slot
-        for k in range(RING):
-            @pl.when(mine & (array == k))
-            def _(k=k):
-                pltpu.make_async_copy(kv_refs[k].at[index], held.at[n], sems.at[n]).start()
+
+        @pl.when(mine)
+        def _():
+            list_ref[count] = n
+            for k in range(RING):
+                @pl.when(array == k)
+                def _(k=k):
+                    pltpu.make_async_copy(kv_refs[k].at[index], held.at[count], sems.at[count]).start()
+        return count + mine.astype(jnp.int32)
+
+    count = lax.fori_loop(0, PAIRS, begin, jnp.int32(0))
+
+    def attend(at, w):
+        for g in range(2):
+            half = slice(LANES * g, LANES * g + LANES)
+            scores = jnp.dot(held[at, :, half], blocks[w, half, :], preferred_element_type=F32)
+            peak = jnp.max(scores, axis=0, keepdims=True)
+            lifted = jnp.exp2((scores - peak) * SCALE)
+            total = jnp.sum(lifted, axis=0, keepdims=True)
+            turned = held[at, :, CH + LANES * g : CH + LANES * g + LANES].T
+            mixed = jnp.dot(turned, lifted.astype(BF16), preferred_element_type=F32)
+            for jj in range(2):
+                cut = slice(LANES * jj, LANES * jj + LANES)
+                row = 64 * jj
+                kept = jnp.where(left, mixed[row : row + 32, cut], mixed[row + 32 : row + 64, cut])
+                j = 2 * g + jj
+                values[at, 32 * j : 32 * j + 32, :] = kept
+                levels[at, j : j + 1, :] = peak[:, cut] * SCALE
+                levels[at, 4 + j : 5 + j, :] = total[:, cut]
+
+    def group(i, carry):
+        for u in range(GROUP):
+            at = i * GROUP + u
+
+            @pl.when(at < count)
+            def _(at=at):
+                pltpu.make_async_copy(kv_refs[0].at[0], held.at[at], sems.at[at]).wait()
+        window = [list_ref[jnp.minimum(i * GROUP + u, count - 1)] // PARENTS for u in range(GROUP)]
+        for u in range(GROUP):
+            attend(i * GROUP + u, window[u])
         return carry
 
-    lax.fori_loop(0, PAIRS, begin, 0)
-    left = lax.broadcasted_iota(jnp.int32, (HEAD_DIM, LANES), 1) < 64
+    lax.fori_loop(0, (count + GROUP - 1) // GROUP, group, 0)
+    rows = lax.broadcasted_iota(jnp.int32, (PACK - LANES, LANES), 0)
+    done = jnp.int32(0)
     for source in range(LINE):
-        query_ref, out_ref = query_refs[source], out_refs[source]
-
-        def window(s, carry, source=source, query_ref=query_ref, out_ref=out_ref):
-            base = (source * ACT_MAX + s) * PARENTS
-            found = owned(base)[0]
-            for p in range(1, PARENTS):
-                found = found | owned(base + p)[0]
-
-            @pl.when(jnp.logical_not(found))
-            def _():
+        out_ref = out_refs[source]
+        for s in range(ACT_MAX):
+            w = source * ACT_MAX + s
+            matches = jnp.int32(0)
+            for p in range(PARENTS):
+                matches = matches + owned(w * PARENTS + p)[0].astype(jnp.int32)
+
+            @pl.when(matches == 0)
+            def _(s=s, out_ref=out_ref):
                 out_ref[s, :LANES, :] = jnp.zeros((LANES, LANES), BF16)
-                rows = lax.broadcasted_iota(jnp.int32, (PACK - LANES, LANES), 0)
                 out_ref[s, LANES:, :] = jnp.where(rows < 4, LOWEST, 0.0).astype(BF16)
 
-            @pl.when(found)
-            def _():
+            @pl.when(matches > 0)
+            def _(s=s, out_ref=out_ref, done=done, matches=matches):
+                def join(k, state):
+                    peak, total, value = state
+                    new = jnp.maximum(peak, levels[done + k, 0:4, :])
+                    fade, gain = jnp.exp2(peak - new), jnp.exp2(levels[done + k, 0:4, :] - new)
+                    total = total * fade + levels[done + k, 4:8, :] * gain
+                    value = jnp.concatenate(
+                        [
+                            value[32 * j : 32 * j + 32] * fade[j : j + 1]
+                            + values[done + k, 32 * j : 32 * j + 32, :] * gain[j : j + 1]
+                            for j in range(4)
+                        ],
+                        axis=0,
+                    )
+                    return new, total, value
+
+                first = (levels[done, 0:4, :], levels[done, 4:8, :], values[done])
+                peak, total, value = lax.fori_loop(1, matches, join, first)
                 for j in range(4):
-                    pair = query_ref[s, 32 * j : 32 * j + 32, :].astype(F32)
-                    lanes = slice(LANES * j, LANES * j + LANES)
-                    blocks[64 * j : 64 * j + 32, lanes] = jnp.where(left, pair, 0.0).astype(BF16)
-                    blocks[64 * j + 32 : 64 * j + 64, lanes] = jnp.where(left, 0.0, pair).astype(BF16)
-                sums[...] = jnp.zeros_like(sums)
-                peak[...] = jnp.full_like(peak, LOWEST)
-                total[...] = jnp.zeros_like(total)
-
-                def parent(p, carry):
-                    n = base + p
-
-                    @pl.when(owned(n)[0])
-                    def _():
-                        arrival(n).wait()
-                        for g in range(2):
-                            half = slice(LANES * g, LANES * g + LANES)
-                            wide = slice(256 * g, 256 * g + 256)
-                            scores = jnp.dot(held[n, :, half], blocks[half, wide], preferred_element_type=F32)
-                            old = peak[:, wide]
-                            new = jnp.maximum(old, jnp.max(scores, axis=0, keepdims=True))
-                            lifted = jnp.exp2((scores - new) * SCALE)
-                            fade = jnp.exp2((old - new) * SCALE)
-                            peak[:, wide] = new
-                            total[:, wide] = total[:, wide] * fade + jnp.sum(lifted, axis=0, keepdims=True)
-                            mixed = jnp.dot(
-                                held[n, :, CH + LANES * g : CH + LANES * g + LANES].T,
-                                lifted.astype(BF16), preferred_element_type=F32,
-                            )
-                            for jj in range(2):
-                                rows = slice(64 * (2 * g + jj), 64 * (2 * g + jj) + 64)
-                                cut = slice(LANES * jj, LANES * jj + LANES)
-                                sums[rows, :] = sums[rows, :] * fade[:, cut] + mixed[64 * jj : 64 * jj + 64, cut]
-                    return carry
-
-                lax.fori_loop(0, PARENTS, parent, 0)
-                levels = []
-                for j in range(4):
-                    lanes = slice(LANES * j, LANES * j + LANES)
-                    kept = jnp.where(left, sums[64 * j : 64 * j + 32, :], sums[64 * j + 32 : 64 * j + 64, :])
-                    out_ref[s, 32 * j : 32 * j + 32, :] = (kept / total[:, lanes]).astype(BF16)
-                    levels.append(peak[:, lanes] * SCALE + jnp.log2(total[:, lanes]))
-                level = jnp.concatenate(levels, axis=0)
+                    cut = slice(32 * j, 32 * j + 32)
+                    out_ref[s, cut, :] = (value[cut] / total[j : j + 1]).astype(BF16)
+                level = peak + jnp.log2(total)
                 high = level.astype(BF16).astype(F32)
                 middle = (level - high).astype(BF16).astype(F32)
                 low = level - high - middle
                 stats = jnp.concatenate([high, middle, low, jnp.zeros_like(low)], axis=0)
                 out_ref[s, LANES:, :] = stats.astype(BF16)
-            return carry
-
-        lax.fori_loop(0, ACT_MAX, window, 0)
+
+            done = done + matches
 
 
 def merge_kernel(act_ref, *refs):
@@ -265,7 +293,7 @@
     attended[...] = jnp.zeros_like(attended)
     fits, window, lane = placement()
     for w in range(WINDOWS):
-        @pl.when(act_ref[w] > 0)
+        @pl.when(act_ref[w // 2, w % 2, 0] > 0)
         def _(w=w):
             block = mixed[rank(act_ref, w)]
             for side in range(2):
@@ -309,23 +337,26 @@
     chip = jnp.concatenate([coarse_kv, swapped(coarse_kv)], axis=0)
     first = ringed(chip)
 
-    act = active.reshape(WINDOWS)
-    turned = latent.transpose(2, 0, 1, 3)
     face = jax.ShapeDtypeStruct((VZ, VX, CH), BF16)
-    x_first, x_last, y_first, y_last, extra = pl.pallas_call(
+    x_first, x_last, y_first, y_last, extra, turned = pl.pallas_call(
         face_kernel,
-        out_shape=[face] * 4 + [jax.ShapeDtypeStruct((ACT_MAX, PACK - LANES, LANES), BF16)],
+        out_shape=[face] * 4 + [
+            jax.ShapeDtypeStruct((ACT_MAX, PACK - LANES, LANES), BF16),
+            jax.ShapeDtypeStruct((VZ, VX, VY, CH), F32),
+        ],
         in_specs=[SMEM] * 3 + [VMEM] * 2,
-        out_specs=[VMEM] * 5,
+        out_specs=[VMEM] * 6,
+        compiler_params=pltpu.CompilerParams(vmem_limit_bytes=6 << 20),
         name="faces",
-    )(act, parent_owner.reshape(-1), parent_slot.reshape(-1), turned, norm_gain.reshape(1, CH))
+    )(active, parent_owner, parent_slot, latent, norm_gain.reshape(1, CH))
     x_last = after(x_last, chip)
     x_low, x_high = shift(x_last, "gx", 1), shift(x_first, "gx", -1)
+    second = ringed(after(first, x_low, x_high))
+    y_first, y_last = after(y_first, first), after(y_last, first)
     y_first = jnp.concatenate([x_low[:, :1], y_first, x_high[:, :1]], axis=1).reshape(-1, CH)
     y_last = jnp.concatenate([x_low[:, -1:], y_last, x_high[:, -1:]], axis=1).reshape(-1, CH)
     y_low, y_high = shift(y_last, "gy", 1), shift(y_first, "gy", -1)
 
-    second = ringed(after(first, y_low, y_high))
     hidden, query = pl.pallas_call(
         conv_kernel,
         out_shape=(
@@ -339,22 +370,22 @@
             pltpu.VMEM((27, CH, CH), BF16),
             pltpu.SemaphoreType.DMA((9,)),
         ],
-        compiler_params=pltpu.CompilerParams(vmem_limit_bytes=20 << 20),
+        compiler_params=pltpu.CompilerParams(vmem_limit_bytes=56 << 20),
         cost_estimate=pl.CostEstimate(flops=2 * 27 * ROWS * CH * CH, bytes_accessed=5 << 20, transcendentals=ROWS * CH),
         name="conv",
     )(
-        act, turned, x_low, x_high, y_low, y_high, norm_gain.reshape(1, CH),
+        active, turned, x_low, x_high, y_low, y_high, norm_gain.reshape(1, CH),
         conv_bias.reshape(1, CH), attn_gain.reshape(1, CH), conv_weight, q_weight, extra,
     )
 
     def along(block, step):
         return move(block, lambda ring, line, core: (ring, line + step, core))
 
-    index = lax.axis_index("gx")
-    here = jnp.stack([index // (LINE * CORES), index // CORES % LINE, index % CORES]).astype(jnp.int32)
+    here = lax.axis_index("gx").astype(jnp.int32).reshape(1)
+    third = ringed(after(second, query))
+    query = after(query, second)
     queries = [query] + [along(query, d) for d in range(1, LINE)]
-    third = ringed(after(second, *queries))
-    fourth = ringed(third)
+    fourth = ringed(after(third, *queries))
     kv_all = [chip, first, second, third, fourth]
     kv_all = kv_all + [swapped(after(first, *queries)), swapped(after(second, *queries)), swapped(third)]
     parts = pl.pallas_call(
@@ -365,15 +396,15 @@
         scratch_shapes=[
             pltpu.VMEM((LINE * ACT_MAX, PACK - LANES, LANES), jnp.int32),
             pltpu.SMEM((LINE * ACT_MAX, PACK - LANES, LANES), jnp.int32),
+            pltpu.SMEM((PAIRS,), jnp.int32),
             pltpu.VMEM((PAIRS, TOK, 2 * CH), BF16),
-            pltpu.VMEM((CH, 2 * CH), BF16),
-            pltpu.VMEM((CH, LANES), F32),
-            pltpu.VMEM((1, 2 * CH), F32),
-            pltpu.VMEM((1, 2 * CH), F32),
+            pltpu.VMEM((LINE * ACT_MAX, CH, CH), BF16),
+            pltpu.VMEM((PAIRS, LANES, LANES), F32),
+            pltpu.VMEM((PAIRS, 8, LANES), F32),
             pltpu.SemaphoreType.DMA((PAIRS,)),
             pltpu.SemaphoreType.DMA,
         ],
-        compiler_params=pltpu.CompilerParams(vmem_limit_bytes=16 << 20),
+        compiler_params=pltpu.CompilerParams(vmem_limit_bytes=18 << 20),
         name="attend",
     )(here, *queries, *kv_all)
 
@@ -387,9 +418,9 @@
             pltpu.VMEM((ACT_MAX, LANES, LANES), BF16),
             pltpu.VMEM((2, ROWS, LANES), F32),
         ],
-        compiler_params=pltpu.CompilerParams(vmem_limit_bytes=16 << 20),
+        compiler_params=pltpu.CompilerParams(vmem_limit_bytes=8 << 20),
         name="merge",
-    )(act, *merged, hidden, out_weight)
+    )(active, *merged, hidden, out_weight)
     return out.reshape(VZ, VX, VY, CH).transpose(1, 2, 0, 3)
 
 

time: 122 us -> 93.6 us (0.77)
  local copies, waits for them, and re-layouts: 19.4 us -> 8.59 us
  waiting for transfers between devices: 47.2 us -> 41.5 us
  Pallas kernels: 20.1 us -> 15.1 us
  starting transfers between devices: 31.8 us -> 26.9 us
  other arithmetic: 2.89 us -> 0.04 us
    unnamed x35 -> x32, local copies, waits for them, and re-layouts: 15.2 us -> 7.63 us
    ppermute x14, starting transfers between devices: 18.3 us -> 13.4 us  [move(): return lax.ppermute(block, 'gx', pairs)]
    ppermute x14, waiting for transfers between devices: 43 us -> 38.4 us  [move(): return lax.ppermute(block, 'gx', pairs)]
    pallas_call x1, Pallas kernels: 11.2 us -> 7.27 us  [per_device(): pl.pallas_call(attend_kernel, out_shape=[jax.ShapeDtypeStruct((ACT_MAX, P...]
    reshape x3 -> x0, local copies, waits for them, and re-layouts: 3.26 us -> none  [the longest x1 1.3 us: per_device(): parent_owner.reshape(-1)]
    unnamed x1 -> x0, other arithmetic: 1.34 us -> none
  transfers between devices with their start and end apart: 18 -> 18, of which waited for: 12 -> 12; matrix products, arithmetic and copies ran while one was open for 8% -> 2% of each run, Pallas kernels for 6% -> 7%
where the time goes in v3:
time: 93.6 us; the launch traced here: 92.3 us
  waiting for transfers between devices  41.5 us (44%)
  starting transfers between devices  26.9 us (29%)
  Pallas kernels  15.1 us (16%)
  local copies, waits for them, and re-layouts  8.59 us (9%)
    ppermute x14, waiting for transfers between devices, move(): return lax.ppermute(block, 'gx', pairs)  38.4 us
    ppermute x4, starting transfers between devices, shift(): lax.ppermute(block, axis, [(i, i + step) for i in range(count) if 0 <= i...  13.5 us
    ppermute x14, starting transfers between devices, move(): return lax.ppermute(block, 'gx', pairs)  13.4 us
    unnamed x32, local copies, waits for them, and re-layouts  7.63 us
    pallas_call x1, Pallas kernels, per_device(): pl.pallas_call(attend_kernel, out_shape=[jax.ShapeDtypeStruct((ACT_MAX, P...  7.27 us
    pallas_call x1, Pallas kernels, per_device(): pl.pallas_call(conv_kernel, out_shape=(jax.ShapeDtypeStruct((ROWS, CH), F...  5.76 us
    ppermute x4, waiting for transfers between devices, shift(): lax.ppermute(block, axis, [(i, i + step) for i in range(count) if 0 <= i...  3.05 us
  transfers between devices with their start and end apart: 18, of which 12 were waited for; matrix products, arithmetic and copies ran while one was open for 2% of the time, Pallas kernels for 7%

profile of v3, /device:TPU:2, one launch (start us, length us, event | category | flops | bytes accessed | tf_op | source)
XLA Modules:
  0.0 92.3 jit_solution(17490961033851517799)
XLA Ops:
  0.0 1.1 %constant_dynamic-update-slice_fusion.1 = bf16[8,128,512]{2,1,0:T(8,128)(2,1)S(1)} fusion(bf16[4,128,512]{2,1,0:T(8,128)(2,1)} %param.15), kind=kLoop, calls=%fused_computation.4 | loop fusion | bytes 1048576
  1.1 1.0 %collective-permute-done = bf16[4,128,512]{2,1,0:T(8,128)(2,1)S(1)} collective-permute-done((bf16[4,128,512]{2,1,0:T(8,128)(2,1)}, bf16[4,128,512]{2,1,0:T(8,128)(2,1)S(1)}, u32[]{:S(2)}, u32[]{:S(2)}) %collective-permute-start) | collective-permute-done | bytes 524320 | tf_op jit(solution)/shard_map/ppermute | solution.py:324
  2.2 2.0 %collective-permute-start.3 = (bf16[8,128,512]{2,1,0:T(8,128)(2,1)S(1)}, bf16[8,128,512]{2,1,0:T(8,128)(2,1)S(1)}, u32[]{:S(2)}, u32[]{:S(2)}) collective-permute-start(bf16[8,128,512]{2,1,0:T(8,128)(2,1)S(1)} %constant_dynamic-update-slice_fusion.refs_4_), channel_id=1, source_target_pairs={{0,32},{4,228},{8,40},{12,236},{16,48},{20,244},{24,56},{28,252},{... | collective-permute-start | bytes 3145736 | tf_op jit(solution)/shard_map/ppermute | solution.py:324
  4.2 0.8 copy.18.act_ref
  4.9 1.0 %copy-done.1 = f32[8,8,4,256]{3,2,1,0:T(4,128)S(1)} copy-done((f32[8,8,4,256]{3,2,1,0:T(4,128)S(1)}, f32[8,8,4,256]{3,2,1,0:T(4,128)}, u32[]{:S(2)}) %copy-start.1) | copy-done | bytes 262168
  6.6 0.7 copy-done.9
  7.2 0.7 copy-done.10
  7.9 0.9 faces.1
  8.8 0.7 copy-done
  10.1 1.3 %collective-permute-start.2 = (bf16[4,8,256]{2,1,0:T(8,128)(2,1)S(1)}, bf16[4,8,256]{2,1,0:T(8,128)(2,1)S(1)}, u32[]{:S(2)}, u32[]{:S(2)}) collective-permute-start(bf16[4,8,256]{2,1,0:T(8,128)(2,1)S(1)} %get-tuple-element.29), channel_id=1, source_target_pairs={{4,0},{8,4},{12,8},{16,12},{20,16},{24,20},{28,24},{32,28},{36,32}... | collective-permute-start | bytes 49160 | tf_op jit(solution)/shard_map/ppermute | solution.py:312
  11.4 6.3 %collective-permute-start.1 = (bf16[4,8,256]{2,1,0:T(8,128)(2,1)S(1)}, bf16[4,8,256]{2,1,0:T(8,128)(2,1)S(1)}, u32[]{:S(2)}, u32[]{:S(2)}) collective-permute-start(bf16[4,8,256]{2,1,0:T(8,128)(2,1)S(1)} %get-tuple-element.28), channel_id=1, source_target_pairs={{0,4},{4,8},{8,12},{12,16},{16,20},{20,24},{24,28},{28,32},{32,36}... | collective-permute-start | bytes 49160 | tf_op jit(solution)/shard_map/ppermute | solution.py:312
  17.7 0.8 collective-permute-done.1.xlo_ref
  18.5 2.3 %collective-permute-done.3.refs_5_ = bf16[8,128,512]{2,1,0:T(8,128)(2,1)S(1)} collective-permute-done((bf16[8,128,512]{2,1,0:T(8,128)(2,1)S(1)}, bf16[8,128,512]{2,1,0:T(8,128)(2,1)S(1)}, u32[]{:S(2)}, u32[]{:S(2)}) %collective-permute-start.3) | collective-permute-done | bytes 1048608 | tf_op jit(solution)/shard_map/ppermute | solution.py:324
  20.9 6.2 %collective-permute-start.6 = (bf16[8,128,512]{2,1,0:T(8,128)(2,1)S(1)}, bf16[8,128,512]{2,1,0:T(8,128)(2,1)S(1)}, u32[]{:S(2)}, u32[]{:S(2)}) collective-permute-start(bf16[8,128,512]{2,1,0:T(8,128)(2,1)S(1)} %collective-permute-done.3.refs_5_), channel_id=1, source_target_pairs={{0,32},{4,228},{8,40},{12,236},{16,48},{20,244},{24,56},{28,252},{... | collective-permute-start | bytes 3145736 | tf_op jit(solution)/shard_map/ppermute | solution.py:324
  27.2 2.4 %collective-permute-start.5 = (bf16[40,256]{1,0:T(8,128)(2,1)S(1)}, bf16[40,256]{1,0:T(8,128)(2,1)S(1)}, u32[]{:S(2)}, u32[]{:S(2)}) collective-permute-start(bf16[40,256]{1,0:T(8,128)(2,1)S(1)} %reshape.25), channel_id=1, source_target_pairs={{1,0},{2,1},{3,2},{5,4},{6,5},{7,6},{9,8},{10,9},{11,10},{13,12},{... | collective-permute-start | bytes 61448 | tf_op jit(solution)/shard_map/ppermute | solution.py:312
  29.6 3.4 %collective-permute-start.4 = (bf16[40,256]{1,0:T(8,128)(2,1)S(1)}, bf16[40,256]{1,0:T(8,128)(2,1)S(1)}, u32[]{:S(2)}, u32[]{:S(2)}) collective-permute-start(bf16[40,256]{1,0:T(8,128)(2,1)S(1)} %reshape.24), channel_id=1, source_target_pairs={{0,1},{1,2},{2,3},{4,5},{5,6},{6,7},{8,9},{9,10},{10,11},{12,13},{... | collective-permute-start | bytes 61448 | tf_op jit(solution)/shard_map/ppermute | solution.py:312
  33.0 2.2 %collective-permute-done.4.ylo_ref = bf16[40,256]{1,0:T(8,128)(2,1)S(1)} collective-permute-done((bf16[40,256]{1,0:T(8,128)(2,1)S(1)}, bf16[40,256]{1,0:T(8,128)(2,1)S(1)}, u32[]{:S(2)}, u32[]{:S(2)}) %collective-permute-start.4) | collective-permute-done | bytes 20512 | tf_op jit(solution)/shard_map/ppermute | solution.py:312
  35.9 5.8 %conv.1 = (f32[256,256]{1,0:T(8,128)}, bf16[3,144,128]{2,1,0:T(8,128)(2,1)}) custom-call(s32[2,2,1]{2,1,0:T(2,128)} %copy-done.5, f32[4,8,8,256]{3,2,1,0:T(8,128)} %copy-done, bf16[4,8,256]{2,1,0:T(8,128)(2,1)} %copy-done.12, bf16[4,8,256]{2,1,0:T(8,128)(2,1)} %copy-done.11, bf16[40,256]{1,0:T(8,128)(2,1)} %copy-done.14, bf16[40,256]{1,0:T(8,128)(2,1)} %copy-done.13, ...), custom_call_target="tpu_custom_call" | custom-call | flops 905969664 | bytes 5242880 | tf_op jit(solution)/shard_map/conv/pallas_call | solution.py:360
  42.1 2.0 %collective-permute-start.7 = (bf16[3,144,128]{2,1,0:T(8,128)(2,1)}, bf16[3,144,128]{2,1,0:T(8,128)(2,1)S(1)}, u32[]{:S(2)}, u32[]{:S(2)}) collective-permute-start(bf16[3,144,128]{2,1,0:T(8,128)(2,1)} %get-tuple-element.37.refs_0_), channel_id=1, source_target_pairs={{0,8},{4,12},{8,16},{12,20},{16,24},{20,28},{24,0},{28,4},{32,40},... | collective-permute-start | bytes 331784 | tf_op jit(solution)/shard_map/ppermute | solution.py:324
  44.1 2.9 %collective-permute-done.9.refs_3_ = bf16[3,144,128]{2,1,0:T(8,128)(2,1)S(1)} collective-permute-done((bf16[3,144,128]{2,1,0:T(8,128)(2,1)}, bf16[3,144,128]{2,1,0:T(8,128)(2,1)S(1)}, u32[]{:S(2)}, u32[]{:S(2)}) %collective-permute-start.9) | collective-permute-done | bytes 110624 | tf_op jit(solution)/shard_map/ppermute | solution.py:324
  47.1 1.5 %collective-permute-done.8.refs_2_ = bf16[3,144,128]{2,1,0:T(8,128)(2,1)S(1)} collective-permute-done((bf16[3,144,128]{2,1,0:T(8,128)(2,1)}, bf16[3,144,128]{2,1,0:T(8,128)(2,1)S(1)}, u32[]{:S(2)}, u32[]{:S(2)}) %collective-permute-start.8) | collective-permute-done | bytes 110624 | tf_op jit(solution)/shard_map/ppermute | solution.py:324
  48.6 1.2 %collective-permute-done.7.refs_1_ = bf16[3,144,128]{2,1,0:T(8,128)(2,1)S(1)} collective-permute-done((bf16[3,144,128]{2,1,0:T(8,128)(2,1)}, bf16[3,144,128]{2,1,0:T(8,128)(2,1)S(1)}, u32[]{:S(2)}, u32[]{:S(2)}) %collective-permute-start.7) | collective-permute-done | bytes 110624 | tf_op jit(solution)/shard_map/ppermute | solution.py:324
  50.3 7.6 %collective-permute-done.10.refs_7_ = bf16[8,128,512]{2,1,0:T(8,128)(2,1)} collective-permute-done((bf16[8,128,512]{2,1,0:T(8,128)(2,1)S(1)}, bf16[8,128,512]{2,1,0:T(8,128)(2,1)}, u32[]{:S(2)}, u32[]{:S(2)}) %collective-permute-start.10) | collective-permute-done | bytes 1048608 | tf_op jit(solution)/shard_map/ppermute | solution.py:324
  57.9 16.3 %collective-permute-done.11.refs_8_ = bf16[8,128,512]{2,1,0:T(8,128)(2,1)} collective-permute-done((bf16[8,128,512]{2,1,0:T(8,128)(2,1)}, bf16[8,128,512]{2,1,0:T(8,128)(2,1)}, u32[]{:S(2)}, u32[]{:S(2)}) %collective-permute-start.11) | collective-permute-done | bytes 1048608 | tf_op jit(solution)/shard_map/ppermute | solution.py:324
  74.2 0.9 copy-done.4
  75.1 7.3 %attend.1 = (bf16[3,144,128]{2,1,0:T(8,128)(2,1)S(1)}, bf16[3,144,128]{2,1,0:T(8,128)(2,1)S(1)}, bf16[3,144,128]{2,1,0:T(8,128)(2,1)S(1)}, bf16[3,144,128]{2,1,0:T(8,128)(2,1)S(1)}) custom-call(s32[1]{0:T(128)} %bitcast.here_ref, bf16[3,144,128]{2,1,0:T(8,128)(2,1)S(1)} %copy-done.4, bf16[3,144,128]{2,1,0:T(8,128)(2,1)S(1)} %collective-permute-done.7.refs_1_, ...), custom_call_target="tpu_custom_call" | custom-call | tf_op jit(solution)/shard_map/attend/pallas_call | solution.py:391
  82.8 1.9 %collective-permute-start.17 = (bf16[3,144,128]{2,1,0:T(8,128)(2,1)S(1)}, bf16[3,144,128]{2,1,0:T(8,128)(2,1)S(1)}, u32[]{:S(2)}, u32[]{:S(2)}) collective-permute-start(bf16[3,144,128]{2,1,0:T(8,128)(2,1)S(1)} %get-tuple-element.45), channel_id=1, source_target_pairs={{0,8},{4,12},{8,16},{12,20},{16,24},{20,28},{24,0},{28,4},{32,40},... | collective-permute-start | bytes 331784 | tf_op jit(solution)/shard_map/ppermute | solution.py:324
  84.7 2.7 %collective-permute-done.15.refs_1_ = bf16[3,144,128]{2,1,0:T(8,128)(2,1)S(1)} collective-permute-done((bf16[3,144,128]{2,1,0:T(8,128)(2,1)S(1)}, bf16[3,144,128]{2,1,0:T(8,128)(2,1)S(1)}, u32[]{:S(2)}, u32[]{:S(2)}) %collective-permute-start.15) | collective-permute-done | bytes 110624 | tf_op jit(solution)/shard_map/ppermute | solution.py:324
  87.4 1.6 %collective-permute-done.16.refs_2_ = bf16[3,144,128]{2,1,0:T(8,128)(2,1)S(1)} collective-permute-done((bf16[3,144,128]{2,1,0:T(8,128)(2,1)S(1)}, bf16[3,144,128]{2,1,0:T(8,128)(2,1)S(1)}, u32[]{:S(2)}, u32[]{:S(2)}) %collective-permute-start.16) | collective-permute-done | bytes 110624 | tf_op jit(solution)/shard_map/ppermute | solution.py:324
  89.0 1.2 %collective-permute-done.17.refs_3_ = bf16[3,144,128]{2,1,0:T(8,128)(2,1)S(1)} collective-permute-done((bf16[3,144,128]{2,1,0:T(8,128)(2,1)S(1)}, bf16[3,144,128]{2,1,0:T(8,128)(2,1)S(1)}, u32[]{:S(2)}, u32[]{:S(2)}) %collective-permute-start.17) | collective-permute-done | bytes 110624 | tf_op jit(solution)/shard_map/ppermute | solution.py:324
  90.2 1.2 %merge.1 = f32[256,256]{1,0:T(8,128)S(1)} custom-call(s32[2,2,1]{2,1,0:T(2,128)S(1)} %copy-done.6, bf16[3,144,128]{2,1,0:T(8,128)(2,1)S(1)} %get-tuple-element.42.refs_0_, bf16[3,144,128]{2,1,0:T(8,128)(2,1)S(1)} %collective-permute-done.15.refs_1_, bf16[3,144,128]{2,1,0:T(8,128)(2,1)S(1)} %collective-permute-done.16.refs_2_, ...), custom_call_target="tpu_custom_call" | custom-call | tf_op jit(solution)/shard_map/merge/pallas_call | solution.py:412
  91.4 0.9 copy.21
  (48 shorter events, 3.3 us)
Async XLA Ops:
  0.0 2.1 %collective-permute-start = (bf16[4,128,512]{2,1,0:T(8,128)(2,1)}, bf16[4,128,512]{2,1,0:T(8,128)(2,1)S(1)}, u32[]{:S(2)}, u32[]{:S(2)}) collective-permute-start(bf16[4,128,512]{2,1,0:T(8,128)(2,1)} %param.15), channel_id=1, source_target_pairs={{0,4},{4,0},{8,12},{12,8},{16,20},{20,16},{24,28},{28,24},{32,36},... | collective-permute-start | bytes 1572872 | tf_op jit(solution)/shard_map/ppermute | solution.py:324
  2.2 18.7 %collective-permute-start.3 = (bf16[8,128,512]{2,1,0:T(8,128)(2,1)S(1)}, bf16[8,128,512]{2,1,0:T(8,128)(2,1)S(1)}, u32[]{:S(2)}, u32[]{:S(2)}) collective-permute-start(bf16[8,128,512]{2,1,0:T(8,128)(2,1)S(1)} %constant_dynamic-update-slice_fusion.refs_4_), channel_id=1, source_target_pairs={{0,32},{4,228},{8,40},{12,236},{16,48},{20,244},{24,56},{28,252},{... | collective-permute-start | bytes 3145736 | tf_op jit(solution)/shard_map/ppermute | solution.py:324
  4.9 30.4 %copy-start.5 = (s32[2,2,1]{2,1,0:T(2,128)}, s32[2,2,1]{2,1,0:T(2,128)S(1)}, u32[]{:S(2)}) copy-start(s32[2,2,1]{2,1,0:T(2,128)S(1)} %copy.18.act_ref) | copy-start | bytes 52
  4.9 1.0 %copy-start.1 = (f32[8,8,4,256]{3,2,1,0:T(4,128)S(1)}, f32[8,8,4,256]{3,2,1,0:T(4,128)}, u32[]{:S(2)}) copy-start(f32[8,8,4,256]{3,2,1,0:T(4,128)} %latent_ref.1) | copy-start | bytes 786436
  5.9 0.7 copy-start.8
  6.6 0.7 copy-start.9
  7.2 0.7 copy-start.10
  8.8 0.7 copy-start
  10.1 7.6 %collective-permute-start.2 = (bf16[4,8,256]{2,1,0:T(8,128)(2,1)S(1)}, bf16[4,8,256]{2,1,0:T(8,128)(2,1)S(1)}, u32[]{:S(2)}, u32[]{:S(2)}) collective-permute-start(bf16[4,8,256]{2,1,0:T(8,128)(2,1)S(1)} %get-tuple-element.29), channel_id=1, source_target_pairs={{4,0},{8,4},{12,8},{16,12},{20,16},{24,20},{28,24},{32,28},{36,32}... | collective-permute-start | bytes 49160 | tf_op jit(solution)/shard_map/ppermute | solution.py:312
  11.4 7.2 %collective-permute-start.1 = (bf16[4,8,256]{2,1,0:T(8,128)(2,1)S(1)}, bf16[4,8,256]{2,1,0:T(8,128)(2,1)S(1)}, u32[]{:S(2)}, u32[]{:S(2)}) collective-permute-start(bf16[4,8,256]{2,1,0:T(8,128)(2,1)S(1)} %get-tuple-element.28), channel_id=1, source_target_pairs={{0,4},{4,8},{8,12},{12,16},{16,20},{20,24},{24,28},{28,32},{32,36}... | collective-permute-start | bytes 49160 | tf_op jit(solution)/shard_map/ppermute | solution.py:312
  17.7 17.6 %copy-start.11 = (bf16[4,8,256]{2,1,0:T(8,128)(2,1)}, bf16[4,8,256]{2,1,0:T(8,128)(2,1)S(1)}, u32[]{:S(2)}) copy-start(bf16[4,8,256]{2,1,0:T(8,128)(2,1)S(1)} %collective-permute-done.2.xhi_ref) | copy-start | bytes 49156
  18.5 16.8 %copy-start.12 = (bf16[4,8,256]{2,1,0:T(8,128)(2,1)}, bf16[4,8,256]{2,1,0:T(8,128)(2,1)S(1)}, u32[]{:S(2)}) copy-start(bf16[4,8,256]{2,1,0:T(8,128)(2,1)S(1)} %collective-permute-done.1.xlo_ref) | copy-start | bytes 49156
  20.9 20.8 %collective-permute-start.6 = (bf16[8,128,512]{2,1,0:T(8,128)(2,1)S(1)}, bf16[8,128,512]{2,1,0:T(8,128)(2,1)S(1)}, u32[]{:S(2)}, u32[]{:S(2)}) collective-permute-start(bf16[8,128,512]{2,1,0:T(8,128)(2,1)S(1)} %collective-permute-done.3.refs_5_), channel_id=1, source_target_pairs={{0,32},{4,228},{8,40},{12,236},{16,48},{20,244},{24,56},{28,252},{... | collective-permute-start | bytes 3145736 | tf_op jit(solution)/shard_map/ppermute | solution.py:324
  27.2 5.9 %collective-permute-start.5 = (bf16[40,256]{1,0:T(8,128)(2,1)S(1)}, bf16[40,256]{1,0:T(8,128)(2,1)S(1)}, u32[]{:S(2)}, u32[]{:S(2)}) collective-permute-start(bf16[40,256]{1,0:T(8,128)(2,1)S(1)} %reshape.25), channel_id=1, source_target_pairs={{1,0},{2,1},{3,2},{5,4},{6,5},{7,6},{9,8},{10,9},{11,10},{13,12},{... | collective-permute-start | bytes 61448 | tf_op jit(solution)/shard_map/ppermute | solution.py:312
  29.6 5.7 %collective-permute-start.4 = (bf16[40,256]{1,0:T(8,128)(2,1)S(1)}, bf16[40,256]{1,0:T(8,128)(2,1)S(1)}, u32[]{:S(2)}, u32[]{:S(2)}) collective-permute-start(bf16[40,256]{1,0:T(8,128)(2,1)S(1)} %reshape.24), channel_id=1, source_target_pairs={{0,1},{1,2},{2,3},{4,5},{5,6},{6,7},{8,9},{9,10},{10,11},{12,13},{... | collective-permute-start | bytes 61448 | tf_op jit(solution)/shard_map/ppermute | solution.py:312
  33.0 2.3 %copy-start.13 = (bf16[40,256]{1,0:T(8,128)(2,1)}, bf16[40,256]{1,0:T(8,128)(2,1)S(1)}, u32[]{:S(2)}) copy-start(bf16[40,256]{1,0:T(8,128)(2,1)S(1)} %collective-permute-done.5.yhi_ref) | copy-start | bytes 61444
  35.3 0.6 copy-start.14
  41.7 16.2 %collective-permute-start.10 = (bf16[8,128,512]{2,1,0:T(8,128)(2,1)S(1)}, bf16[8,128,512]{2,1,0:T(8,128)(2,1)}, u32[]{:S(2)}, u32[]{:S(2)}) collective-permute-start(bf16[8,128,512]{2,1,0:T(8,128)(2,1)S(1)} %collective-permute-done.6.refs_6_), channel_id=1, source_target_pairs={{0,32},{4,228},{8,40},{12,236},{16,48},{20,244},{24,56},{28,252},{... | collective-permute-start | bytes 3145736 | tf_op jit(solution)/shard_map/ppermute | solution.py:324
  42.1 5.0 %collective-permute-start.9 = (bf16[3,144,128]{2,1,0:T(8,128)(2,1)}, bf16[3,144,128]{2,1,0:T(8,128)(2,1)S(1)}, u32[]{:S(2)}, u32[]{:S(2)}) collective-permute-start(bf16[3,144,128]{2,1,0:T(8,128)(2,1)} %get-tuple-element.37.refs_0_), channel_id=1, source_target_pairs={{0,24},{4,28},{8,0},{12,4},{16,8},{20,12},{24,16},{28,20},{32,56},... | collective-permute-start | bytes 331784 | tf_op jit(solution)/shard_map/ppermute | solution.py:324
  42.1 6.5 %collective-permute-start.8 = (bf16[3,144,128]{2,1,0:T(8,128)(2,1)}, bf16[3,144,128]{2,1,0:T(8,128)(2,1)S(1)}, u32[]{:S(2)}, u32[]{:S(2)}) collective-permute-start(bf16[3,144,128]{2,1,0:T(8,128)(2,1)} %get-tuple-element.37.refs_0_), channel_id=1, source_target_pairs={{0,16},{4,20},{8,24},{12,28},{16,0},{20,4},{24,8},{28,12},{32,48},... | collective-permute-start | bytes 331784 | tf_op jit(solution)/shard_map/ppermute | solution.py:324
  42.1 7.7 %collective-permute-start.7 = (bf16[3,144,128]{2,1,0:T(8,128)(2,1)}, bf16[3,144,128]{2,1,0:T(8,128)(2,1)S(1)}, u32[]{:S(2)}, u32[]{:S(2)}) collective-permute-start(bf16[3,144,128]{2,1,0:T(8,128)(2,1)} %get-tuple-element.37.refs_0_), channel_id=1, source_target_pairs={{0,8},{4,12},{8,16},{12,20},{16,24},{20,28},{24,0},{28,4},{32,40},... | collective-permute-start | bytes 331784 | tf_op jit(solution)/shard_map/ppermute | solution.py:324
  49.8 8.1 %collective-permute-start.12 = (bf16[8,128,512]{2,1,0:T(8,128)(2,1)S(1)}, bf16[8,128,512]{2,1,0:T(8,128)(2,1)}, u32[]{:S(2)}, u32[]{:S(2)}) collective-permute-start(bf16[8,128,512]{2,1,0:T(8,128)(2,1)S(1)} %collective-permute-done.3.refs_5_), channel_id=1, source_target_pairs={{0,4},{4,0},{8,12},{12,8},{16,20},{20,16},{24,28},{28,24},{32,36},... | collective-permute-start | bytes 3145736 | tf_op jit(solution)/shard_map/ppermute | solution.py:324
  49.8 8.1 %collective-permute-start.13 = (bf16[8,128,512]{2,1,0:T(8,128)(2,1)S(1)}, bf16[8,128,512]{2,1,0:T(8,128)(2,1)}, u32[]{:S(2)}, u32[]{:S(2)}) collective-permute-start(bf16[8,128,512]{2,1,0:T(8,128)(2,1)S(1)} %collective-permute-done.6.refs_6_), channel_id=1, source_target_pairs={{0,4},{4,0},{8,12},{12,8},{16,20},{20,16},{24,28},{28,24},{32,36},... | collective-permute-start | bytes 3145736 | tf_op jit(solution)/shard_map/ppermute | solution.py:324
  57.9 16.3 %collective-permute-start.11 = (bf16[8,128,512]{2,1,0:T(8,128)(2,1)}, bf16[8,128,512]{2,1,0:T(8,128)(2,1)}, u32[]{:S(2)}, u32[]{:S(2)}) collective-permute-start(bf16[8,128,512]{2,1,0:T(8,128)(2,1)} %collective-permute-done.10.refs_7_), channel_id=1, source_target_pairs={{0,32},{4,228},{8,40},{12,236},{16,48},{20,244},{24,56},{28,252},{... | collective-permute-start | bytes 3145736 | tf_op jit(solution)/shard_map/ppermute | solution.py:324
  57.9 16.3 %collective-permute-start.14 = (bf16[8,128,512]{2,1,0:T(8,128)(2,1)}, bf16[8,128,512]{2,1,0:T(8,128)(2,1)}, u32[]{:S(2)}, u32[]{:S(2)}) collective-permute-start(bf16[8,128,512]{2,1,0:T(8,128)(2,1)} %collective-permute-done.10.refs_7_), channel_id=1, source_target_pairs={{0,4},{4,0},{8,12},{12,8},{16,20},{20,16},{24,28},{28,24},{32,36},... | collective-permute-start | bytes 3145736 | tf_op jit(solution)/shard_map/ppermute | solution.py:324
  74.2 0.9 copy-start.4
  75.1 15.1 %copy-start.2 = (f32[256,256]{1,0:T(8,128)S(1)}, f32[256,256]{1,0:T(8,128)}, u32[]{:S(2)}) copy-start(f32[256,256]{1,0:T(8,128)} %get-tuple-element.46.refs_4_) | copy-start | bytes 786436
  75.1 15.1 %copy-start.3 = (bf16[256,256]{1,0:T(8,128)(2,1)S(1)}, bf16[256,256]{1,0:T(8,128)(2,1)}, u32[]{:S(2)}) copy-start(bf16[256,256]{1,0:T(8,128)(2,1)} %refs_5_.1) | copy-start | bytes 393220
  75.1 15.1 %copy-start.6 = (s32[2,2,1]{2,1,0:T(2,128)S(1)}, s32[2,2,1]{2,1,0:T(2,128)}, u32[]{:S(2)}) copy-start(s32[2,2,1]{2,1,0:T(2,128)} %copy-done.5) | copy-start | bytes 52
  82.4 5.0 %collective-permute-start.15 = (bf16[3,144,128]{2,1,0:T(8,128)(2,1)S(1)}, bf16[3,144,128]{2,1,0:T(8,128)(2,1)S(1)}, u32[]{:S(2)}, u32[]{:S(2)}) collective-permute-start(bf16[3,144,128]{2,1,0:T(8,128)(2,1)S(1)} %get-tuple-element.43), channel_id=1, source_target_pairs={{0,24},{4,28},{8,0},{12,4},{16,8},{20,12},{24,16},{28,20},{32,56},... | collective-permute-start | bytes 331784 | tf_op jit(solution)/shard_map/ppermute | solution.py:324
  82.7 6.4 %collective-permute-start.16 = (bf16[3,144,128]{2,1,0:T(8,128)(2,1)S(1)}, bf16[3,144,128]{2,1,0:T(8,128)(2,1)S(1)}, u32[]{:S(2)}, u32[]{:S(2)}) collective-permute-start(bf16[3,144,128]{2,1,0:T(8,128)(2,1)S(1)} %get-tuple-element.44), channel_id=1, source_target_pairs={{0,16},{4,20},{8,24},{12,28},{16,0},{20,4},{24,8},{28,12},{32,48},... | collective-permute-start | bytes 331784 | tf_op jit(solution)/shard_map/ppermute | solution.py:324
  82.8 7.4 %collective-permute-start.17 = (bf16[3,144,128]{2,1,0:T(8,128)(2,1)S(1)}, bf16[3,144,128]{2,1,0:T(8,128)(2,1)S(1)}, u32[]{:S(2)}, u32[]{:S(2)}) collective-permute-start(bf16[3,144,128]{2,1,0:T(8,128)(2,1)S(1)} %get-tuple-element.45), channel_id=1, source_target_pairs={{0,8},{4,12},{8,16},{12,20},{16,24},{20,28},{24,0},{28,4},{32,40},... | collective-permute-start | bytes 331784 | tf_op jit(solution)/shard_map/ppermute | solution.py:324
  (1 other events, 0.6 us)

commit v4 on v3

--- a/solution.py
+++ b/solution.py
@@ -21,6 +21,7 @@
 PACK = 144
 SLOTS = 4
 CHIP = 2 * SLOTS
+ARRAYS = 16
 RING, LINE, CORES = 8, 4, 2
 PAIRS = LINE * ACT_MAX * PARENTS
 GROUP = 4
@@ -150,8 +151,8 @@
 
 
 def attend_kernel(here_ref, *refs):
-    query_refs, kv_refs, out_refs = refs[:LINE], refs[LINE : LINE + RING], refs[LINE + RING : 2 * LINE + RING]
-    codes, code_ref, list_ref, held, blocks, values, levels, sems, code_sem = refs[2 * LINE + RING :]
+    query_refs, kv_refs, out_refs = refs[:LINE], refs[LINE : LINE + ARRAYS], refs[LINE + ARRAYS : 2 * LINE + ARRAYS]
+    codes, code_ref, list_ref, match_ref, held, blocks, values, levels, sems, code_sem = refs[2 * LINE + ARRAYS :]
     here = here_ref[0]
     ring, line, core = here >> 3, (here >> 1) & 3, here & 1
     for source in range(LINE):
@@ -173,29 +174,41 @@
                 blocks[w, 64 * j : 64 * j + 64, beside] = none
     listing.wait()
 
-    def owned(n):
-        code = code_ref[n // PARENTS, 0, n % PARENTS]
-        owner = code >> 2
-        return (code >= 0) & (((owner >> 1) & 3) == line), ((owner >> 3) - ring) & 7, owner & 1, code & 3
-
-    def begin(n, count):
-        mine, ahead, owner_core, slot = owned(n)
-        below = (ahead > 4) | ((ahead == 4) & (core == 0))
-        steps = jnp.where(below, RING - ahead, ahead)
-        bearer = jnp.where(ahead == 0, core, jnp.where(below, 0, 1))
-        array = jnp.where((ahead == 0) | (bearer == core), steps, 4 + steps)
-        index = jnp.where(owner_core == bearer, 0, SLOTS) + slot
-
-        @pl.when(mine)
-        def _():
-            list_ref[count] = n
-            for k in range(RING):
-                @pl.when(array == k)
-                def _(k=k):
-                    pltpu.make_async_copy(kv_refs[k].at[index], held.at[count], sems.at[count]).start()
-        return count + mine.astype(jnp.int32)
-
-    count = lax.fori_loop(0, PAIRS, begin, jnp.int32(0))
+    def fetch(w, count):
+        def parents(count):
+            for p in range(PARENTS):
+                code = code_ref[w, 0, p]
+                owner = code >> 2
+                mine = ((owner >> 1) & 3) == line
+                ahead, owner_core, slot = ((owner >> 3) - ring) & 7, owner & 1, code & 3
+                below = ahead > 4
+                steps = jnp.where(below, RING - ahead, ahead)
+                brought = (ahead == 0) | (ahead == 4) | (below == (core == 0))
+                own = owner_core == core
+                array = jnp.where(
+                    brought,
+                    jnp.where(own, steps, jnp.where(ahead == 4, 12, 5 + steps)),
+                    jnp.where(own, 12 + steps, 8 + steps),
+                )
+
+                @pl.when(mine)
+                def _(count=count, array=array, slot=slot):
+                    list_ref[count] = w
+                    for quarter in range(0, ARRAYS, 4):
+                        @pl.when((array >> 2) == quarter // 4)
+                        def _(quarter=quarter):
+                            for k in range(quarter, quarter + 4):
+                                @pl.when(array == k)
+                                def _(k=k):
+                                    pltpu.make_async_copy(kv_refs[k].at[slot], held.at[count], sems.at[count]).start()
+                count = count + mine.astype(jnp.int32)
+            return count
+
+        after = lax.cond(code_ref[w, 0, 0] >= 0, parents, lambda count: count, count)
+        match_ref[w] = after - count
+        return after
+
+    count = lax.fori_loop(0, LINE * ACT_MAX, fetch, jnp.int32(0))
 
     def attend(at, w):
         for g in range(2):
@@ -222,7 +235,7 @@
             @pl.when(at < count)
             def _(at=at):
                 pltpu.make_async_copy(kv_refs[0].at[0], held.at[at], sems.at[at]).wait()
-        window = [list_ref[jnp.minimum(i * GROUP + u, count - 1)] // PARENTS for u in range(GROUP)]
+        window = [list_ref[jnp.minimum(i * GROUP + u, count - 1)] for u in range(GROUP)]
         for u in range(GROUP):
             attend(i * GROUP + u, window[u])
         return carry
@@ -234,9 +247,7 @@
         out_ref = out_refs[source]
         for s in range(ACT_MAX):
             w = source * ACT_MAX + s
-            matches = jnp.int32(0)
-            for p in range(PARENTS):
-                matches = matches + owned(w * PARENTS + p)[0].astype(jnp.int32)
+            matches = match_ref[w]
 
             @pl.when(matches == 0)
             def _(s=s, out_ref=out_ref):
@@ -334,8 +345,8 @@
     def ringed(block):
         return move(block, lambda ring, line, core: (ring + 1 - 2 * core, line, core))
 
-    chip = jnp.concatenate([coarse_kv, swapped(coarse_kv)], axis=0)
-    first = ringed(chip)
+    a0, a1, b0 = coarse_kv, ringed(coarse_kv), swapped(coarse_kv)
+    b1 = ringed(b0)
 
     face = jax.ShapeDtypeStruct((VZ, VX, CH), BF16)
     x_first, x_last, y_first, y_last, extra, turned = pl.pallas_call(
@@ -346,17 +357,19 @@
         ],
         in_specs=[SMEM] * 3 + [VMEM] * 2,
         out_specs=[VMEM] * 6,
-        compiler_params=pltpu.CompilerParams(vmem_limit_bytes=6 << 20),
+        compiler_params=pltpu.CompilerParams(vmem_limit_bytes=56 << 20),
         name="faces",
     )(active, parent_owner, parent_slot, latent, norm_gain.reshape(1, CH))
-    x_last = after(x_last, chip)
+    x_last = after(x_last, b0)
     x_low, x_high = shift(x_last, "gx", 1), shift(x_first, "gx", -1)
-    second = ringed(after(first, x_low, x_high))
-    y_first, y_last = after(y_first, first), after(y_last, first)
+    a2, b2 = ringed(after(a1, x_low)), ringed(after(b1, x_high))
+    y_first, y_last = after(y_first, a1, b1), after(y_last, a1, b1)
     y_first = jnp.concatenate([x_low[:, :1], y_first, x_high[:, :1]], axis=1).reshape(-1, CH)
     y_last = jnp.concatenate([x_low[:, -1:], y_last, x_high[:, -1:]], axis=1).reshape(-1, CH)
     y_low, y_high = shift(y_last, "gy", 1), shift(y_first, "gy", -1)
 
+    a3, b3 = ringed(after(a2, y_low, y_high)), ringed(after(b2, y_low, y_high))
+    extra = after(extra, a2, b2)
     hidden, query = pl.pallas_call(
         conv_kernel,
         out_shape=(
@@ -382,21 +395,22 @@
         return move(block, lambda ring, line, core: (ring, line + step, core))
 
     here = lax.axis_index("gx").astype(jnp.int32).reshape(1)
-    third = ringed(after(second, query))
-    query = after(query, second)
-    queries = [query] + [along(query, d) for d in range(1, LINE)]
-    fourth = ringed(after(third, *queries))
-    kv_all = [chip, first, second, third, fourth]
-    kv_all = kv_all + [swapped(after(first, *queries)), swapped(after(second, *queries)), swapped(third)]
+    a4 = ringed(after(a3, query))
+    query = after(query, a3)
+    queries = [query, along(query, 1), along(query, 2), along(after(query, b3), 3)]
+    kv_all = [a0, a1, a2, a3, a4, b0, b1, b2, b3]
+    kv_all += [swapped(after(block, *queries)) for block in (a1, a2, a3)] + [swapped(a4)]
+    kv_all += [swapped(after(block, *queries)) for block in (b1, b2, b3)]
     parts = pl.pallas_call(
         attend_kernel,
         out_shape=[jax.ShapeDtypeStruct((ACT_MAX, PACK, LANES), BF16)] * LINE,
-        in_specs=[SMEM] + [VMEM] * LINE + [ANY] * RING,
+        in_specs=[SMEM] + [VMEM] * LINE + [ANY] * ARRAYS,
         out_specs=[VMEM] * LINE,
         scratch_shapes=[
             pltpu.VMEM((LINE * ACT_MAX, PACK - LANES, LANES), jnp.int32),
             pltpu.SMEM((LINE * ACT_MAX, PACK - LANES, LANES), jnp.int32),
             pltpu.SMEM((PAIRS,), jnp.int32),
+            pltpu.SMEM((LINE * ACT_MAX,), jnp.int32),
             pltpu.VMEM((PAIRS, TOK, 2 * CH), BF16),
             pltpu.VMEM((LINE * ACT_MAX, CH, CH), BF16),
             pltpu.VMEM((PAIRS, LANES, LANES), F32),
@@ -404,7 +418,7 @@
             pltpu.SemaphoreType.DMA((PAIRS,)),
             pltpu.SemaphoreType.DMA,
         ],
-        compiler_params=pltpu.CompilerParams(vmem_limit_bytes=18 << 20),
+        compiler_params=pltpu.CompilerParams(vmem_limit_bytes=56 << 20),
         name="attend",
     )(here, *queries, *kv_all)
 

time: 93.6 us -> 81.2 us (0.87)
  waiting for transfers between devices: 41.5 us -> 22.4 us
  starting transfers between devices: 26.9 us -> 36.4 us
  local copies, waits for them, and re-layouts: 8.59 us -> 3.89 us
  other arithmetic: 0.04 us -> 1.47 us
    ppermute x14 -> x21, waiting for transfers between devices: 38.4 us -> 20.2 us  [move(): return lax.ppermute(block, 'gx', pairs)]
    ppermute x14 -> x21, starting transfers between devices: 13.4 us -> 23.5 us  [move(): return lax.ppermute(block, 'gx', pairs)]
    unnamed x32 -> x41, local copies, waits for them, and re-layouts: 7.63 us -> 2.96 us
    pallas_call x1, Pallas kernels: 0.85 us -> 1.88 us  [per_device(): pl.pallas_call(face_kernel, out_shape=[face] * 4 + [jax.ShapeDtypeStruct(...]
  transfers between devices with their start and end apart: 18 -> 25, of which waited for: 12 -> 14; matrix products, arithmetic and copies ran while one was open for 2% -> 4% of each run, Pallas kernels for 7% -> 10%
where the time goes in v4:
time: 81.2 us; the launch traced here: 80.4 us
  starting transfers between devices  36.4 us (45%)
  waiting for transfers between devices  22.4 us (28%)
  Pallas kernels  15.9 us (20%)
  local copies, waits for them, and re-layouts  3.89 us (5%)
  other arithmetic  1.47 us (2%)
    ppermute x21, starting transfers between devices, move(): return lax.ppermute(block, 'gx', pairs)  23.5 us
    ppermute x21, waiting for transfers between devices, move(): return lax.ppermute(block, 'gx', pairs)  20.2 us
    ppermute x4, starting transfers between devices, shift(): lax.ppermute(block, axis, [(i, i + step) for i in range(count) if 0 <= i...  12.9 us
    pallas_call x1, Pallas kernels, per_device(): pl.pallas_call(attend_kernel, out_shape=[jax.ShapeDtypeStruct((ACT_MAX, P...  7.03 us
    pallas_call x1, Pallas kernels, per_device(): pl.pallas_call(conv_kernel, out_shape=(jax.ShapeDtypeStruct((ROWS, CH), F...  5.77 us
    unnamed x41, local copies, waits for them, and re-layouts  2.96 us
    ppermute x4, waiting for transfers between devices, shift(): lax.ppermute(block, axis, [(i, i + step) for i in range(count) if 0 <= i...  2.24 us
    pallas_call x1, Pallas kernels, per_device(): pl.pallas_call(face_kernel, out_shape=[face] * 4 + [jax.ShapeDtypeStruct(...  1.88 us
  transfers between devices with their start and end apart: 25, of which 14 were waited for; matrix products, arithmetic and copies ran while one was open for 4% of the time, Pallas kernels for 10%

profile of v4, /device:TPU:2, one launch (start us, length us, event | category | flops | bytes accessed | tf_op | source)
XLA Modules:
  0.0 80.4 jit_solution(17813749568697964562)
XLA Ops:
  0.0 1.9 %collective-permute-start.3 = (bf16[4,128,512]{2,1,0:T(8,128)(2,1)}, bf16[4,128,512]{2,1,0:T(8,128)(2,1)S(1)}, u32[]{:S(2)}, u32[]{:S(2)}) collective-permute-start(bf16[4,128,512]{2,1,0:T(8,128)(2,1)} %refs_4_.1), channel_id=1, source_target_pairs={{0,32},{4,228},{8,40},{12,236},{16,48},{20,244},{24,56},{28,252},{... | collective-permute-start | bytes 1572872 | tf_op jit(solution)/shard_map/ppermute | solution.py:335
  2.1 1.9 %collective-permute-start.4 = (bf16[4,128,512]{2,1,0:T(8,128)(2,1)S(1)}, bf16[4,128,512]{2,1,0:T(8,128)(2,1)S(1)}, u32[]{:S(2)}, u32[]{:S(2)}) collective-permute-start(bf16[4,128,512]{2,1,0:T(8,128)(2,1)S(1)} %collective-permute-done.refs_9_), channel_id=1, source_target_pairs={{0,32},{4,228},{8,40},{12,236},{16,48},{20,244},{24,56},{28,252},{... | collective-permute-start | bytes 1572872 | tf_op jit(solution)/shard_map/ppermute | solution.py:335
  4.0 1.3 %copy.18.act_ref = s32[2,2,1]{2,1,0:T(2,128)} copy(s32[2,2,1]{1,2,0:T(1,128)} %param.12) | data formatting | bytes 32 | tf_op args[1]
  5.4 1.9 %faces.1 = (bf16[4,8,256]{2,1,0:T(8,128)(2,1)}, bf16[4,8,256]{2,1,0:T(8,128)(2,1)}, bf16[4,8,256]{2,1,0:T(8,128)(2,1)}, bf16[4,8,256]{2,1,0:T(8,128)(2,1)}, bf16...) custom-call(s32[2,2,1]{2,1,0:T(2,128)} %copy.18.act_ref, s32[1,1,4,4]{3,2,1,0:T(4,128)} %owner_ref.1, ...), custom_call_target="tpu_custom_call" | custom-call | tf_op jit(solution)/shard_map/faces/pallas_call | solution.py:352
  7.2 5.7 %collective-permute-start.1 = (bf16[4,8,256]{2,1,0:T(8,128)(2,1)}, bf16[4,8,256]{2,1,0:T(8,128)(2,1)S(1)}, u32[]{:S(2)}, u32[]{:S(2)}) collective-permute-start(bf16[4,8,256]{2,1,0:T(8,128)(2,1)} %get-tuple-element.36), channel_id=1, source_target_pairs={{0,4},{4,8},{8,12},{12,16},{16,20},{20,24},{24,28},{28,32},{32,36}... | collective-permute-start | bytes 49160 | tf_op jit(solution)/shard_map/ppermute | solution.py:323
  12.9 1.3 %collective-permute-start.2 = (bf16[4,8,256]{2,1,0:T(8,128)(2,1)}, bf16[4,8,256]{2,1,0:T(8,128)(2,1)S(1)}, u32[]{:S(2)}, u32[]{:S(2)}) collective-permute-start(bf16[4,8,256]{2,1,0:T(8,128)(2,1)} %get-tuple-element.37), channel_id=1, source_target_pairs={{4,0},{8,4},{12,8},{16,12},{20,16},{24,20},{28,24},{32,28},{36,32}... | collective-permute-start | bytes 49160 | tf_op jit(solution)/shard_map/ppermute | solution.py:323
  14.3 4.8 %collective-permute-start.7 = (bf16[4,128,512]{2,1,0:T(8,128)(2,1)S(1)}, bf16[4,128,512]{2,1,0:T(8,128)(2,1)S(1)}, u32[]{:S(2)}, u32[]{:S(2)}) collective-permute-start(bf16[4,128,512]{2,1,0:T(8,128)(2,1)S(1)} %collective-permute-done.3.refs_5_), channel_id=1, source_target_pairs={{0,32},{4,228},{8,40},{12,236},{16,48},{20,244},{24,56},{28,252},{... | collective-permute-start | bytes 1572872 | tf_op jit(solution)/shard_map/ppermute | solution.py:335
  19.1 1.6 %collective-permute-start.8 = (bf16[4,128,512]{2,1,0:T(8,128)(2,1)S(1)}, bf16[4,128,512]{2,1,0:T(8,128)(2,1)S(1)}, u32[]{:S(2)}, u32[]{:S(2)}) collective-permute-start(bf16[4,128,512]{2,1,0:T(8,128)(2,1)S(1)} %collective-permute-done.4.refs_10_), channel_id=1, source_target_pairs={{0,32},{4,228},{8,40},{12,236},{16,48},{20,244},{24,56},{28,252},{... | collective-permute-start | bytes 1572872 | tf_op jit(solution)/shard_map/ppermute | solution.py:335
  22.3 2.5 %collective-permute-start.6 = (bf16[40,256]{1,0:T(8,128)(2,1)S(1)}, bf16[40,256]{1,0:T(8,128)(2,1)S(1)}, u32[]{:S(2)}, u32[]{:S(2)}) collective-permute-start(bf16[40,256]{1,0:T(8,128)(2,1)S(1)} %reshape.25), channel_id=1, source_target_pairs={{1,0},{2,1},{3,2},{5,4},{6,5},{7,6},{9,8},{10,9},{11,10},{13,12},{... | collective-permute-start | bytes 61448 | tf_op jit(solution)/shard_map/ppermute | solution.py:323
  24.8 3.4 %collective-permute-start.5 = (bf16[40,256]{1,0:T(8,128)(2,1)S(1)}, bf16[40,256]{1,0:T(8,128)(2,1)S(1)}, u32[]{:S(2)}, u32[]{:S(2)}) collective-permute-start(bf16[40,256]{1,0:T(8,128)(2,1)S(1)} %reshape.24), channel_id=1, source_target_pairs={{0,1},{1,2},{2,3},{4,5},{5,6},{6,7},{8,9},{9,10},{10,11},{12,13},{... | collective-permute-start | bytes 61448 | tf_op jit(solution)/shard_map/ppermute | solution.py:323
  28.2 2.2 %collective-permute-done.5.ylo_ref = bf16[40,256]{1,0:T(8,128)(2,1)S(1)} collective-permute-done((bf16[40,256]{1,0:T(8,128)(2,1)S(1)}, bf16[40,256]{1,0:T(8,128)(2,1)S(1)}, u32[]{:S(2)}, u32[]{:S(2)}) %collective-permute-start.5) | collective-permute-done | bytes 20512 | tf_op jit(solution)/shard_map/ppermute | solution.py:323
  30.5 1.3 %collective-permute-start.9 = (bf16[4,128,512]{2,1,0:T(8,128)(2,1)S(1)}, bf16[4,128,512]{2,1,0:T(8,128)(2,1)S(1)}, u32[]{:S(2)}, u32[]{:S(2)}) collective-permute-start(bf16[4,128,512]{2,1,0:T(8,128)(2,1)S(1)} %collective-permute-done.7.refs_6_), channel_id=1, source_target_pairs={{0,32},{4,228},{8,40},{12,236},{16,48},{20,244},{24,56},{28,252},{... | collective-permute-start | bytes 1572872 | tf_op jit(solution)/shard_map/ppermute | solution.py:335
  31.8 2.2 %collective-permute-start.12 = (bf16[4,128,512]{2,1,0:T(8,128)(2,1)S(1)}, bf16[4,128,512]{2,1,0:T(8,128)(2,1)}, u32[]{:S(2)}, u32[]{:S(2)}) collective-permute-start(bf16[4,128,512]{2,1,0:T(8,128)(2,1)S(1)} %collective-permute-done.8.refs_11_), channel_id=1, source_target_pairs={{0,32},{4,228},{8,40},{12,236},{16,48},{20,244},{24,56},{28,252},{... | collective-permute-start | bytes 1572872 | tf_op jit(solution)/shard_map/ppermute | solution.py:335
  34.0 5.8 %conv.1 = (f32[256,256]{1,0:T(8,128)}, bf16[3,144,128]{2,1,0:T(8,128)(2,1)}) custom-call(s32[2,2,1]{2,1,0:T(2,128)} %copy.18.act_ref, f32[4,8,8,256]{3,2,1,0:T(8,128)} %get-tuple-element.34.latent_ref, bf16[4,8,256]{2,1,0:T(8,128)(2,1)} %copy-done.16, bf16[4,8,256]{2,1,0:T(8,128)(2,1)} %copy-done.17, bf16[40,256]{1,0:T(8,128)(2,1)} %copy-done.19, ...), custom_call_target="tpu_custom_call" | custom-call | flops 905969664 | bytes 5242880 | tf_op jit(solution)/shard_map/conv/pallas_call | solution.py:373
  39.8 1.0 %collective-permute-done.9.refs_7_ = bf16[4,128,512]{2,1,0:T(8,128)(2,1)S(1)} collective-permute-done((bf16[4,128,512]{2,1,0:T(8,128)(2,1)S(1)}, bf16[4,128,512]{2,1,0:T(8,128)(2,1)S(1)}, u32[]{:S(2)}, u32[]{:S(2)}) %collective-permute-start.9) | collective-permute-done | bytes 524320 | tf_op jit(solution)/shard_map/ppermute | solution.py:335
  40.9 1.0 %collective-permute-start.14 = (bf16[4,128,512]{2,1,0:T(8,128)(2,1)S(1)}, bf16[4,128,512]{2,1,0:T(8,128)(2,1)S(1)}, u32[]{:S(2)}, u32[]{:S(2)}) collective-permute-start(bf16[4,128,512]{2,1,0:T(8,128)(2,1)S(1)} %collective-permute-done.9.refs_7_), channel_id=1, source_target_pairs={{0,32},{4,228},{8,40},{12,236},{16,48},{20,244},{24,56},{28,252},{... | collective-permute-start | bytes 1572872 | tf_op jit(solution)/shard_map/ppermute | solution.py:335
  41.8 2.0 %collective-permute-start.11 = (bf16[3,144,128]{2,1,0:T(8,128)(2,1)}, bf16[3,144,128]{2,1,0:T(8,128)(2,1)S(1)}, u32[]{:S(2)}, u32[]{:S(2)}) collective-permute-start(bf16[3,144,128]{2,1,0:T(8,128)(2,1)} %get-tuple-element.50.refs_0_), channel_id=1, source_target_pairs={{0,16},{4,20},{8,24},{12,28},{16,0},{20,4},{24,8},{28,12},{32,48},... | collective-permute-start | bytes 331784 | tf_op jit(solution)/shard_map/ppermute | solution.py:335
  43.9 0.9 %collective-permute-start.10 = (bf16[3,144,128]{2,1,0:T(8,128)(2,1)}, bf16[3,144,128]{2,1,0:T(8,128)(2,1)S(1)}, u32[]{:S(2)}, u32[]{:S(2)}) collective-permute-start(bf16[3,144,128]{2,1,0:T(8,128)(2,1)} %get-tuple-element.50.refs_0_), channel_id=1, source_target_pairs={{0,8},{4,12},{8,16},{12,20},{16,24},{20,28},{24,0},{28,4},{32,40},... | collective-permute-start | bytes 331784 | tf_op jit(solution)/shard_map/ppermute | solution.py:335
  44.7 1.9 %collective-permute-done.12.refs_12_ = bf16[4,128,512]{2,1,0:T(8,128)(2,1)} collective-permute-done((bf16[4,128,512]{2,1,0:T(8,128)(2,1)S(1)}, bf16[4,128,512]{2,1,0:T(8,128)(2,1)}, u32[]{:S(2)}, u32[]{:S(2)}) %collective-permute-start.12) | collective-permute-done | bytes 524320 | tf_op jit(solution)/shard_map/ppermute | solution.py:335
  46.6 1.1 %collective-permute-start.13 = (bf16[3,144,128]{2,1,0:T(8,128)(2,1)}, bf16[3,144,128]{2,1,0:T(8,128)(2,1)S(1)}, u32[]{:S(2)}, u32[]{:S(2)}) collective-permute-start(bf16[3,144,128]{2,1,0:T(8,128)(2,1)} %get-tuple-element.50.refs_0_), channel_id=1, source_target_pairs={{0,24},{4,28},{8,0},{12,4},{16,8},{20,12},{24,16},{28,20},{32,56},... | collective-permute-start | bytes 331784 | tf_op jit(solution)/shard_map/ppermute | solution.py:335
  47.6 4.4 %collective-permute-done.14.refs_8_ = bf16[4,128,512]{2,1,0:T(8,128)(2,1)S(1)} collective-permute-done((bf16[4,128,512]{2,1,0:T(8,128)(2,1)S(1)}, bf16[4,128,512]{2,1,0:T(8,128)(2,1)S(1)}, u32[]{:S(2)}, u32[]{:S(2)}) %collective-permute-start.14) | collective-permute-done | bytes 524320 | tf_op jit(solution)/shard_map/ppermute | solution.py:335
  54.1 1.4 %collective-permute-done.15.refs_13_ = bf16[4,128,512]{2,1,0:T(8,128)(2,1)S(1)} collective-permute-done((bf16[4,128,512]{2,1,0:T(8,128)(2,1)S(1)}, bf16[4,128,512]{2,1,0:T(8,128)(2,1)S(1)}, u32[]{:S(2)}, u32[]{:S(2)}) %collective-permute-start.15) | collective-permute-done | bytes 524320 | tf_op jit(solution)/shard_map/ppermute | solution.py:335
  56.4 0.7 collective-permute-done.19.refs_17_
  57.1 1.5 %collective-permute-done.20.refs_18_ = bf16[4,128,512]{2,1,0:T(8,128)(2,1)} collective-permute-done((bf16[4,128,512]{2,1,0:T(8,128)(2,1)S(1)}, bf16[4,128,512]{2,1,0:T(8,128)(2,1)}, u32[]{:S(2)}, u32[]{:S(2)}) %collective-permute-start.20) | collective-permute-done | bytes 524320 | tf_op jit(solution)/shard_map/ppermute | solution.py:335
  58.9 7.0 %attend.1 = (bf16[3,144,128]{2,1,0:T(8,128)(2,1)}, bf16[3,144,128]{2,1,0:T(8,128)(2,1)}, bf16[3,144,128]{2,1,0:T(8,128)(2,1)}, bf16[3,144,128]{2,1,0:T(8,128)(2,1)}) custom-call(s32[1]{0:T(128)} %bitcast.here_ref, bf16[3,144,128]{2,1,0:T(8,128)(2,1)} %get-tuple-element.50.refs_0_, bf16[3,144,128]{2,1,0:T(8,128)(2,1)} %copy-done.14, ...), custom_call_target="tpu_custom_call" | custom-call | tf_op jit(solution)/shard_map/attend/pallas_call | solution.py:404
  66.0 2.2 %collective-permute-start.22 = (bf16[3,144,128]{2,1,0:T(8,128)(2,1)}, bf16[3,144,128]{2,1,0:T(8,128)(2,1)S(1)}, u32[]{:S(2)}, u32[]{:S(2)}) collective-permute-start(bf16[3,144,128]{2,1,0:T(8,128)(2,1)} %get-tuple-element.59), channel_id=1, source_target_pairs={{0,24},{4,28},{8,0},{12,4},{16,8},{20,12},{24,16},{28,20},{32,56},... | collective-permute-start | bytes 331784 | tf_op jit(solution)/shard_map/ppermute | solution.py:335
  69.2 5.0 %collective-permute-done.22.refs_1_ = bf16[3,144,128]{2,1,0:T(8,128)(2,1)S(1)} collective-permute-done((bf16[3,144,128]{2,1,0:T(8,128)(2,1)}, bf16[3,144,128]{2,1,0:T(8,128)(2,1)S(1)}, u32[]{:S(2)}, u32[]{:S(2)}) %collective-permute-start.22) | collective-permute-done | bytes 110624 | tf_op jit(solution)/shard_map/ppermute | solution.py:335
  74.1 1.7 %collective-permute-done.23.refs_2_ = bf16[3,144,128]{2,1,0:T(8,128)(2,1)S(1)} collective-permute-done((bf16[3,144,128]{2,1,0:T(8,128)(2,1)}, bf16[3,144,128]{2,1,0:T(8,128)(2,1)S(1)}, u32[]{:S(2)}, u32[]{:S(2)}) %collective-permute-start.23) | collective-permute-done | bytes 110624 | tf_op jit(solution)/shard_map/ppermute | solution.py:335
  75.8 1.6 %collective-permute-done.24.refs_3_ = bf16[3,144,128]{2,1,0:T(8,128)(2,1)S(1)} collective-permute-done((bf16[3,144,128]{2,1,0:T(8,128)(2,1)}, bf16[3,144,128]{2,1,0:T(8,128)(2,1)S(1)}, u32[]{:S(2)}, u32[]{:S(2)}) %collective-permute-start.24) | collective-permute-done | bytes 110624 | tf_op jit(solution)/shard_map/ppermute | solution.py:335
  77.4 0.9 %copy-done.2 = bf16[3,144,128]{2,1,0:T(8,128)(2,1)S(1)} copy-done((bf16[3,144,128]{2,1,0:T(8,128)(2,1)S(1)}, bf16[3,144,128]{2,1,0:T(8,128)(2,1)}, u32[]{:S(2)}) %copy-start.2) | copy-done | bytes 110616
  78.3 1.2 %merge.1 = f32[256,256]{1,0:T(8,128)S(1)} custom-call(s32[2,2,1]{2,1,0:T(2,128)S(1)} %copy-done.3, bf16[3,144,128]{2,1,0:T(8,128)(2,1)S(1)} %copy-done.2, bf16[3,144,128]{2,1,0:T(8,128)(2,1)S(1)} %collective-permute-done.22.refs_1_, bf16[3,144,128]{2,1,0:T(8,128)(2,1)S(1)} %collective-permute-done.23.refs_2_, ...), custom_call_target="tpu_custom_call" | custom-call | tf_op jit(solution)/shard_map/merge/pallas_call | solution.py:426
  79.5 0.9 %copy.21 = f32[4,8,8,256]{3,0,2,1:T(4,128)} copy(f32[4,8,8,256]{3,2,1,0:T(8,128)S(1)} %bitcast.8) | data formatting | bytes 524288 | tf_op jit(solution)/shard_map/reshape | solution.py:438
  (70 shorter events, 5.9 us)
Async XLA Ops:
  0.0 2.1 %collective-permute-start = (bf16[4,128,512]{2,1,0:T(8,128)(2,1)}, bf16[4,128,512]{2,1,0:T(8,128)(2,1)S(1)}, u32[]{:S(2)}, u32[]{:S(2)}) collective-permute-start(bf16[4,128,512]{2,1,0:T(8,128)(2,1)} %refs_4_.1), channel_id=1, source_target_pairs={{0,4},{4,0},{8,12},{12,8},{16,20},{20,16},{24,28},{28,24},{32,36},... | collective-permute-start | bytes 1572872 | tf_op jit(solution)/shard_map/ppermute | solution.py:335
  0.0 14.2 %collective-permute-start.3 = (bf16[4,128,512]{2,1,0:T(8,128)(2,1)}, bf16[4,128,512]{2,1,0:T(8,128)(2,1)S(1)}, u32[]{:S(2)}, u32[]{:S(2)}) collective-permute-start(bf16[4,128,512]{2,1,0:T(8,128)(2,1)} %refs_4_.1), channel_id=1, source_target_pairs={{0,32},{4,228},{8,40},{12,236},{16,48},{20,244},{24,56},{28,252},{... | collective-permute-start | bytes 1572872 | tf_op jit(solution)/shard_map/ppermute | solution.py:335
  2.1 56.7 %copy-start.4 = (bf16[4,128,512]{2,1,0:T(8,128)(2,1)}, bf16[4,128,512]{2,1,0:T(8,128)(2,1)S(1)}, u32[]{:S(2)}) copy-start(bf16[4,128,512]{2,1,0:T(8,128)(2,1)S(1)} %collective-permute-done.refs_9_) | copy-start | bytes 1572868
  2.1 17.0 %collective-permute-start.4 = (bf16[4,128,512]{2,1,0:T(8,128)(2,1)S(1)}, bf16[4,128,512]{2,1,0:T(8,128)(2,1)S(1)}, u32[]{:S(2)}, u32[]{:S(2)}) collective-permute-start(bf16[4,128,512]{2,1,0:T(8,128)(2,1)S(1)} %collective-permute-done.refs_9_), channel_id=1, source_target_pairs={{0,32},{4,228},{8,40},{12,236},{16,48},{20,244},{24,56},{28,252},{... | collective-permute-start | bytes 1572872 | tf_op jit(solution)/shard_map/ppermute | solution.py:335
  7.2 7.0 %collective-permute-start.1 = (bf16[4,8,256]{2,1,0:T(8,128)(2,1)}, bf16[4,8,256]{2,1,0:T(8,128)(2,1)S(1)}, u32[]{:S(2)}, u32[]{:S(2)}) collective-permute-start(bf16[4,8,256]{2,1,0:T(8,128)(2,1)} %get-tuple-element.36), channel_id=1, source_target_pairs={{0,4},{4,8},{8,12},{12,16},{16,20},{20,24},{24,28},{28,32},{32,36}... | collective-permute-start | bytes 49160 | tf_op jit(solution)/shard_map/ppermute | solution.py:323
  12.9 6.1 %collective-permute-start.2 = (bf16[4,8,256]{2,1,0:T(8,128)(2,1)}, bf16[4,8,256]{2,1,0:T(8,128)(2,1)S(1)}, u32[]{:S(2)}, u32[]{:S(2)}) collective-permute-start(bf16[4,8,256]{2,1,0:T(8,128)(2,1)} %get-tuple-element.37), channel_id=1, source_target_pairs={{4,0},{8,4},{12,8},{16,12},{20,16},{24,20},{28,24},{32,28},{36,32}... | collective-permute-start | bytes 49160 | tf_op jit(solution)/shard_map/ppermute | solution.py:323
  14.3 44.6 %copy-start.5 = (bf16[4,128,512]{2,1,0:T(8,128)(2,1)}, bf16[4,128,512]{2,1,0:T(8,128)(2,1)S(1)}, u32[]{:S(2)}) copy-start(bf16[4,128,512]{2,1,0:T(8,128)(2,1)S(1)} %collective-permute-done.3.refs_5_) | copy-start | bytes 1572868
  14.3 19.8 %copy-start.16 = (bf16[4,8,256]{2,1,0:T(8,128)(2,1)}, bf16[4,8,256]{2,1,0:T(8,128)(2,1)S(1)}, u32[]{:S(2)}) copy-start(bf16[4,8,256]{2,1,0:T(8,128)(2,1)S(1)} %collective-permute-done.1.xlo_ref) | copy-start | bytes 49156
  14.3 13.9 %collective-permute-start.7 = (bf16[4,128,512]{2,1,0:T(8,128)(2,1)S(1)}, bf16[4,128,512]{2,1,0:T(8,128)(2,1)S(1)}, u32[]{:S(2)}, u32[]{:S(2)}) collective-permute-start(bf16[4,128,512]{2,1,0:T(8,128)(2,1)S(1)} %collective-permute-done.3.refs_5_), channel_id=1, source_target_pairs={{0,32},{4,228},{8,40},{12,236},{16,48},{20,244},{24,56},{28,252},{... | collective-permute-start | bytes 1572872 | tf_op jit(solution)/shard_map/ppermute | solution.py:335
  19.1 39.7 %copy-start.6 = (bf16[4,128,512]{2,1,0:T(8,128)(2,1)}, bf16[4,128,512]{2,1,0:T(8,128)(2,1)S(1)}, u32[]{:S(2)}) copy-start(bf16[4,128,512]{2,1,0:T(8,128)(2,1)S(1)} %collective-permute-done.4.refs_10_) | copy-start | bytes 1572868
  19.1 12.7 %collective-permute-start.8 = (bf16[4,128,512]{2,1,0:T(8,128)(2,1)S(1)}, bf16[4,128,512]{2,1,0:T(8,128)(2,1)S(1)}, u32[]{:S(2)}, u32[]{:S(2)}) collective-permute-start(bf16[4,128,512]{2,1,0:T(8,128)(2,1)S(1)} %collective-permute-done.4.refs_10_), channel_id=1, source_target_pairs={{0,32},{4,228},{8,40},{12,236},{16,48},{20,244},{24,56},{28,252},{... | collective-permute-start | bytes 1572872 | tf_op jit(solution)/shard_map/ppermute | solution.py:335
  22.3 5.9 %collective-permute-start.6 = (bf16[40,256]{1,0:T(8,128)(2,1)S(1)}, bf16[40,256]{1,0:T(8,128)(2,1)S(1)}, u32[]{:S(2)}, u32[]{:S(2)}) collective-permute-start(bf16[40,256]{1,0:T(8,128)(2,1)S(1)} %reshape.25), channel_id=1, source_target_pairs={{1,0},{2,1},{3,2},{5,4},{6,5},{7,6},{9,8},{10,9},{11,10},{13,12},{... | collective-permute-start | bytes 61448 | tf_op jit(solution)/shard_map/ppermute | solution.py:323
  24.8 5.7 %collective-permute-start.5 = (bf16[40,256]{1,0:T(8,128)(2,1)S(1)}, bf16[40,256]{1,0:T(8,128)(2,1)S(1)}, u32[]{:S(2)}, u32[]{:S(2)}) collective-permute-start(bf16[40,256]{1,0:T(8,128)(2,1)S(1)} %reshape.24), channel_id=1, source_target_pairs={{0,1},{1,2},{2,3},{4,5},{5,6},{6,7},{8,9},{9,10},{10,11},{12,13},{... | collective-permute-start | bytes 61448 | tf_op jit(solution)/shard_map/ppermute | solution.py:323
  28.2 30.7 %copy-start.7 = (bf16[4,128,512]{2,1,0:T(8,128)(2,1)}, bf16[4,128,512]{2,1,0:T(8,128)(2,1)S(1)}, u32[]{:S(2)}) copy-start(bf16[4,128,512]{2,1,0:T(8,128)(2,1)S(1)} %collective-permute-done.7.refs_6_) | copy-start | bytes 1572868
  30.5 10.4 %collective-permute-start.9 = (bf16[4,128,512]{2,1,0:T(8,128)(2,1)S(1)}, bf16[4,128,512]{2,1,0:T(8,128)(2,1)S(1)}, u32[]{:S(2)}, u32[]{:S(2)}) collective-permute-start(bf16[4,128,512]{2,1,0:T(8,128)(2,1)S(1)} %collective-permute-done.7.refs_6_), channel_id=1, source_target_pairs={{0,32},{4,228},{8,40},{12,236},{16,48},{20,244},{24,56},{28,252},{... | collective-permute-start | bytes 1572872 | tf_op jit(solution)/shard_map/ppermute | solution.py:335
  31.8 27.0 %copy-start.8 = (bf16[4,128,512]{2,1,0:T(8,128)(2,1)}, bf16[4,128,512]{2,1,0:T(8,128)(2,1)S(1)}, u32[]{:S(2)}) copy-start(bf16[4,128,512]{2,1,0:T(8,128)(2,1)S(1)} %collective-permute-done.8.refs_11_) | copy-start | bytes 1572868
  31.8 14.7 %collective-permute-start.12 = (bf16[4,128,512]{2,1,0:T(8,128)(2,1)S(1)}, bf16[4,128,512]{2,1,0:T(8,128)(2,1)}, u32[]{:S(2)}, u32[]{:S(2)}) collective-permute-start(bf16[4,128,512]{2,1,0:T(8,128)(2,1)S(1)} %collective-permute-done.8.refs_11_), channel_id=1, source_target_pairs={{0,32},{4,228},{8,40},{12,236},{16,48},{20,244},{24,56},{28,252},{... | collective-permute-start | bytes 1572872 | tf_op jit(solution)/shard_map/ppermute | solution.py:335
  40.9 11.2 %collective-permute-start.14 = (bf16[4,128,512]{2,1,0:T(8,128)(2,1)S(1)}, bf16[4,128,512]{2,1,0:T(8,128)(2,1)S(1)}, u32[]{:S(2)}, u32[]{:S(2)}) collective-permute-start(bf16[4,128,512]{2,1,0:T(8,128)(2,1)S(1)} %collective-permute-done.9.refs_7_), channel_id=1, source_target_pairs={{0,32},{4,228},{8,40},{12,236},{16,48},{20,244},{24,56},{28,252},{... | collective-permute-start | bytes 1572872 | tf_op jit(solution)/shard_map/ppermute | solution.py:335
  41.8 10.3 %collective-permute-start.11 = (bf16[3,144,128]{2,1,0:T(8,128)(2,1)}, bf16[3,144,128]{2,1,0:T(8,128)(2,1)S(1)}, u32[]{:S(2)}, u32[]{:S(2)}) collective-permute-start(bf16[3,144,128]{2,1,0:T(8,128)(2,1)} %get-tuple-element.50.refs_0_), channel_id=1, source_target_pairs={{0,16},{4,20},{8,24},{12,28},{16,0},{20,4},{24,8},{28,12},{32,48},... | collective-permute-start | bytes 331784 | tf_op jit(solution)/shard_map/ppermute | solution.py:335
  43.9 8.3 %collective-permute-start.10 = (bf16[3,144,128]{2,1,0:T(8,128)(2,1)}, bf16[3,144,128]{2,1,0:T(8,128)(2,1)S(1)}, u32[]{:S(2)}, u32[]{:S(2)}) collective-permute-start(bf16[3,144,128]{2,1,0:T(8,128)(2,1)} %get-tuple-element.50.refs_0_), channel_id=1, source_target_pairs={{0,8},{4,12},{8,16},{12,20},{16,24},{20,28},{24,0},{28,4},{32,40},... | collective-permute-start | bytes 331784 | tf_op jit(solution)/shard_map/ppermute | solution.py:335
  46.6 5.6 %collective-permute-start.13 = (bf16[3,144,128]{2,1,0:T(8,128)(2,1)}, bf16[3,144,128]{2,1,0:T(8,128)(2,1)S(1)}, u32[]{:S(2)}, u32[]{:S(2)}) collective-permute-start(bf16[3,144,128]{2,1,0:T(8,128)(2,1)} %get-tuple-element.50.refs_0_), channel_id=1, source_target_pairs={{0,24},{4,28},{8,0},{12,4},{16,8},{20,12},{24,16},{28,20},{32,56},... | collective-permute-start | bytes 331784 | tf_op jit(solution)/shard_map/ppermute | solution.py:335
  52.1 1.9 %collective-permute-start.18 = (bf16[4,128,512]{2,1,0:T(8,128)(2,1)S(1)}, bf16[4,128,512]{2,1,0:T(8,128)(2,1)S(1)}, u32[]{:S(2)}, u32[]{:S(2)}) collective-permute-start(bf16[4,128,512]{2,1,0:T(8,128)(2,1)S(1)} %collective-permute-done.14.refs_8_), channel_id=1, source_target_pairs={{0,4},{4,0},{8,12},{12,8},{16,20},{20,16},{24,28},{28,24},{32,36},... | collective-permute-start | bytes 1572872 | tf_op jit(solution)/shard_map/ppermute | solution.py:335
  52.1 3.3 %collective-permute-start.15 = (bf16[4,128,512]{2,1,0:T(8,128)(2,1)S(1)}, bf16[4,128,512]{2,1,0:T(8,128)(2,1)S(1)}, u32[]{:S(2)}, u32[]{:S(2)}) collective-permute-start(bf16[4,128,512]{2,1,0:T(8,128)(2,1)S(1)} %collective-permute-done.3.refs_5_), channel_id=1, source_target_pairs={{0,4},{4,0},{8,12},{12,8},{16,20},{20,16},{24,28},{28,24},{32,36},... | collective-permute-start | bytes 1572872 | tf_op jit(solution)/shard_map/ppermute | solution.py:335
  52.7 3.6 %collective-permute-start.16 = (bf16[4,128,512]{2,1,0:T(8,128)(2,1)S(1)}, bf16[4,128,512]{2,1,0:T(8,128)(2,1)}, u32[]{:S(2)}, u32[]{:S(2)}) collective-permute-start(bf16[4,128,512]{2,1,0:T(8,128)(2,1)S(1)} %collective-permute-done.7.refs_6_), channel_id=1, source_target_pairs={{0,4},{4,0},{8,12},{12,8},{16,20},{20,16},{24,28},{28,24},{32,36},... | collective-permute-start | bytes 1572872 | tf_op jit(solution)/shard_map/ppermute | solution.py:335
  53.0 3.4 %collective-permute-start.17 = (bf16[4,128,512]{2,1,0:T(8,128)(2,1)S(1)}, bf16[4,128,512]{2,1,0:T(8,128)(2,1)}, u32[]{:S(2)}, u32[]{:S(2)}) collective-permute-start(bf16[4,128,512]{2,1,0:T(8,128)(2,1)S(1)} %collective-permute-done.9.refs_7_), channel_id=1, source_target_pairs={{0,4},{4,0},{8,12},{12,8},{16,20},{20,16},{24,28},{28,24},{32,36},... | collective-permute-start | bytes 1572872 | tf_op jit(solution)/shard_map/ppermute | solution.py:335
  53.2 3.9 %collective-permute-start.19 = (bf16[4,128,512]{2,1,0:T(8,128)(2,1)S(1)}, bf16[4,128,512]{2,1,0:T(8,128)(2,1)}, u32[]{:S(2)}, u32[]{:S(2)}) collective-permute-start(bf16[4,128,512]{2,1,0:T(8,128)(2,1)S(1)} %collective-permute-done.4.refs_10_), channel_id=1, source_target_pairs={{0,4},{4,0},{8,12},{12,8},{16,20},{20,16},{24,28},{28,24},{32,36},... | collective-permute-start | bytes 1572872 | tf_op jit(solution)/shard_map/ppermute | solution.py:335
  54.0 4.6 %collective-permute-start.20 = (bf16[4,128,512]{2,1,0:T(8,128)(2,1)S(1)}, bf16[4,128,512]{2,1,0:T(8,128)(2,1)}, u32[]{:S(2)}, u32[]{:S(2)}) collective-permute-start(bf16[4,128,512]{2,1,0:T(8,128)(2,1)S(1)} %collective-permute-done.8.refs_11_), channel_id=1, source_target_pairs={{0,4},{4,0},{8,12},{12,8},{16,20},{20,16},{24,28},{28,24},{32,36},... | collective-permute-start | bytes 1572872 | tf_op jit(solution)/shard_map/ppermute | solution.py:335
  55.5 3.3 %collective-permute-start.21 = (bf16[4,128,512]{2,1,0:T(8,128)(2,1)}, bf16[4,128,512]{2,1,0:T(8,128)(2,1)}, u32[]{:S(2)}, u32[]{:S(2)}) collective-permute-start(bf16[4,128,512]{2,1,0:T(8,128)(2,1)} %collective-permute-done.12.refs_12_), channel_id=1, source_target_pairs={{0,4},{4,0},{8,12},{12,8},{16,20},{20,16},{24,28},{28,24},{32,36},... | collective-permute-start | bytes 1572872 | tf_op jit(solution)/shard_map/ppermute | solution.py:335
  58.9 18.5 %copy-start = (f32[256,256]{1,0:T(8,128)S(1)}, f32[256,256]{1,0:T(8,128)}, u32[]{:S(2)}) copy-start(f32[256,256]{1,0:T(8,128)} %get-tuple-element.62.refs_4_) | copy-start | bytes 786436
  66.0 8.1 %collective-permute-start.22 = (bf16[3,144,128]{2,1,0:T(8,128)(2,1)}, bf16[3,144,128]{2,1,0:T(8,128)(2,1)S(1)}, u32[]{:S(2)}, u32[]{:S(2)}) collective-permute-start(bf16[3,144,128]{2,1,0:T(8,128)(2,1)} %get-tuple-element.59), channel_id=1, source_target_pairs={{0,24},{4,28},{8,0},{12,4},{16,8},{20,12},{24,16},{28,20},{32,56},... | collective-permute-start | bytes 331784 | tf_op jit(solution)/shard_map/ppermute | solution.py:335
  68.2 7.6 %collective-permute-start.23 = (bf16[3,144,128]{2,1,0:T(8,128)(2,1)}, bf16[3,144,128]{2,1,0:T(8,128)(2,1)S(1)}, u32[]{:S(2)}, u32[]{:S(2)}) collective-permute-start(bf16[3,144,128]{2,1,0:T(8,128)(2,1)} %get-tuple-element.60), channel_id=1, source_target_pairs={{0,16},{4,20},{8,24},{12,28},{16,0},{20,4},{24,8},{28,12},{32,48},... | collective-permute-start | bytes 331784 | tf_op jit(solution)/shard_map/ppermute | solution.py:335
  68.8 8.6 %collective-permute-start.24 = (bf16[3,144,128]{2,1,0:T(8,128)(2,1)}, bf16[3,144,128]{2,1,0:T(8,128)(2,1)S(1)}, u32[]{:S(2)}, u32[]{:S(2)}) collective-permute-start(bf16[3,144,128]{2,1,0:T(8,128)(2,1)} %get-tuple-element.61), channel_id=1, source_target_pairs={{0,8},{4,12},{8,16},{12,20},{16,24},{20,28},{24,0},{28,4},{32,40},... | collective-permute-start | bytes 331784 | tf_op jit(solution)/shard_map/ppermute | solution.py:335
  (13 other events, 106.4 us)

commit v5 on v4

--- a/solution.py
+++ b/solution.py
@@ -59,23 +59,8 @@
     return query == (lane & 63), ((row >> 5) & 1) * 2 + ((row >> 2) & 1), lane
 
 
-def face_kernel(
-    act_ref, owner_ref, slot_ref, latent_ref, gain_ref, xa_ref, xb_ref, ya_ref, yb_ref, extra_ref, turned_ref
-):
-    for z in range(VZ):
-        for x in range(VX):
-            turned_ref[z, x] = latent_ref[x, :, z, :]
-    mask = row_mask(act_ref)
-    gain = gain_ref[...].reshape(1, 1, CH)
-
-    def normed(values, flags):
-        scale = lax.rsqrt(jnp.mean(values * values, axis=-1, keepdims=True) + 1e-06)
-        return (flags * values * scale * gain).astype(BF16)
-
-    for side, ref in ((0, xa_ref), (VX - 1, xb_ref)):
-        ref[...] = normed(turned_ref[:, side], mask[side][None])
-    for side, ref in ((0, ya_ref), (VY - 1, yb_ref)):
-        ref[...] = normed(turned_ref[:, :, side, :], mask[:, side, :][None])
+def table_kernel(act_ref, owner_ref, slot_ref, *refs):
+    extra_ref = refs[-1]
     row = lax.broadcasted_iota(jnp.int32, (16, LANES), 0)
     lane = lax.broadcasted_iota(jnp.int32, (16, LANES), 1)
     for s in range(ACT_MAX):
@@ -89,13 +74,41 @@
         extra_ref[s] = extra.astype(BF16)
 
 
+def face_kernel(
+    act_ref, latent_ref, gain_ref, xa_ref, xb_ref, ya_ref, yb_ref, turned_ref
+):
+    for z in range(VZ):
+        for x in range(VX):
+            turned_ref[z, x] = latent_ref[x, :, z, :]
+    mask = row_mask(act_ref)
+    gain = gain_ref[...].reshape(1, 1, CH)
+
+    def normed(values, flags):
+        scale = lax.rsqrt(jnp.mean(values * values, axis=-1, keepdims=True) + 1e-06)
+        return (flags * values * scale * gain).astype(BF16)
+
+    for side, ref in ((0, xa_ref), (VX - 1, xb_ref)):
+        ref[...] = normed(turned_ref[:, side], mask[side][None])
+    for side, ref in ((0, ya_ref), (VY - 1, yb_ref)):
+        ref[...] = normed(turned_ref[:, :, side, :], mask[:, side, :][None])
+
+
+def edge_kernel(xlo_ref, xhi_ref, ya_ref, yb_ref, outa_ref, outb_ref):
+    for side, face_ref, out_ref in ((0, ya_ref, outa_ref), (VY - 1, yb_ref, outb_ref)):
+        for z in range(VZ):
+            low = xlo_ref[z].astype(F32)[side : side + 1]
+            high = xhi_ref[z].astype(F32)[side : side + 1]
+            line = jnp.concatenate([low, face_ref[z].astype(F32), high, jnp.zeros((6, CH), F32)], axis=0)
+            out_ref[z] = line.astype(BF16)
+
+
 def conv_kernel(
     act_ref, latent_ref, xlo_ref, xhi_ref, ylo_ref, yhi_ref, ngain_ref, bias_ref,
     again_ref, weight_ref, qw_ref, extra_ref, hidden_ref, query_ref,
-    frame, weights, sems,
+    frame, weights, wide, sems,
 ):
     copies = [
-        pltpu.make_async_copy(weight_ref.at[pl.ds(3 * ab, 3)], weights.at[pl.ds(3 * ab, 3)], sems.at[ab])
+        pltpu.make_async_copy(weight_ref.at[pl.ds(3 * ab, 3)], weights.at[:, ab], sems.at[ab])
         for ab in range(9)
     ]
     for copy in copies:
@@ -113,20 +126,20 @@
     last = lax.broadcasted_iota(jnp.int32, (VY, CH), 0) == VY - 1
     for z in range(VZ):
         for x in range(VX + 2):
-            r = z * (VX + 2) + x
             here = frame[1, z, x]
-            frame[0, z, x] = jnp.where(first, ylo[r : r + 1, :], pltpu.roll(here, 1, 0))
-            frame[2, z, x] = jnp.where(last, yhi[r : r + 1, :], pltpu.roll(here, VY - 1, 0))
-    mid = jnp.zeros((ROWS, CH), F32)
-    up = jnp.zeros((ROWS - 64, CH), F32)
-    down = jnp.zeros((ROWS - 64, CH), F32)
-    for ab in range(9):
-        copies[ab].wait()
-        a, b = ab // 3, ab % 3
-        slab = frame[b, :, a : a + VX].reshape(ROWS, CH).astype(BF16)
-        up = up + jnp.dot(slab[: ROWS - 64], weights[3 * ab], preferred_element_type=F32)
-        mid = mid + jnp.dot(slab, weights[3 * ab + 1], preferred_element_type=F32)
-        down = down + jnp.dot(slab[64:], weights[3 * ab + 2], preferred_element_type=F32)
+            frame[0, z, x] = jnp.where(first, ylo[z, x : x + 1, :], pltpu.roll(here, 1, 0))
+            frame[2, z, x] = jnp.where(last, yhi[z, x : x + 1, :], pltpu.roll(here, VY - 1, 0))
+    conv = []
+    for a in range(3):
+        for b in range(3):
+            wide[:, CH * b : CH * b + CH] = frame[b, :, a : a + VX].reshape(ROWS, CH).astype(BF16)
+            copies[3 * a + b].wait()
+        rows = (slice(0, ROWS - 64), slice(0, ROWS), slice(64, ROWS))
+        for c in range(3):
+            weight = weights[c, 3 * a : 3 * a + 3].reshape(3 * CH, CH)
+            part = jnp.dot(wide[rows[c], :], weight, preferred_element_type=F32)
+            conv.append(part)
+    up, mid, down = (conv[c] + conv[3 + c] + conv[6 + c] for c in range(3))
     gap = jnp.zeros((64, CH), F32)
     conv = mid + jnp.concatenate([gap, up], 0) + jnp.concatenate([down, gap], 0) + bias_ref[...]
     flat_mask = jnp.broadcast_to(mask, (VZ, VX, VY, CH)).reshape(ROWS, CH)
@@ -315,7 +328,10 @@
         weight = jnp.concatenate([ow_ref[64 * j + 32 * side : 64 * j + 32 * side + 32, :] for j in range(4)], axis=0)
         projected = projected + jnp.dot(attended[side].astype(BF16), weight, preferred_element_type=F32)
     mask = jnp.broadcast_to(row_mask(act_ref)[None], (VZ, VX, VY, CH)).reshape(ROWS, CH)
-    out_ref[...] = mask * (hidden_ref[...] + projected)
+    result = (mask * (hidden_ref[...] + projected)).reshape(VZ, VX, VY, CH)
+    for z in range(VZ):
+        for x in range(VX):
+            out_ref[x, :, z, :] = result[z, x]
 
 
 def shift(block, axis, step):
@@ -346,61 +362,77 @@
         return move(block, lambda ring, line, core: (ring + 1 - 2 * core, line, core))
 
     a0, a1, b0 = coarse_kv, ringed(coarse_kv), swapped(coarse_kv)
-    b1 = ringed(b0)
 
     face = jax.ShapeDtypeStruct((VZ, VX, CH), BF16)
-    x_first, x_last, y_first, y_last, extra, turned = pl.pallas_call(
+    vectors = [one.reshape(1, CH) for one in (norm_gain, conv_bias, attn_gain)]
+    extra = pl.pallas_call(
+        table_kernel,
+        out_shape=jax.ShapeDtypeStruct((ACT_MAX, PACK - LANES, LANES), BF16),
+        in_specs=[SMEM] * 3 + [ANY] * 6,
+        out_specs=VMEM,
+        compiler_params=pltpu.CompilerParams(vmem_limit_bytes=60 << 20),
+        name="tables",
+    )(active, parent_owner, parent_slot, *vectors, conv_weight, q_weight, latent)
+    vectors[0] = after(vectors[0], extra)
+    x_first, x_last, y_first, y_last, turned = pl.pallas_call(
         face_kernel,
         out_shape=[face] * 4 + [
-            jax.ShapeDtypeStruct((ACT_MAX, PACK - LANES, LANES), BF16),
             jax.ShapeDtypeStruct((VZ, VX, VY, CH), F32),
         ],
-        in_specs=[SMEM] * 3 + [VMEM] * 2,
-        out_specs=[VMEM] * 6,
-        compiler_params=pltpu.CompilerParams(vmem_limit_bytes=56 << 20),
+        in_specs=[SMEM] + [VMEM] * 2,
+        out_specs=[VMEM] * 5,
+        compiler_params=pltpu.CompilerParams(vmem_limit_bytes=6 << 20),
         name="faces",
-    )(active, parent_owner, parent_slot, latent, norm_gain.reshape(1, CH))
-    x_last = after(x_last, b0)
+    )(active, latent, vectors[0])
+    b1 = ringed(after(b0, x_first, x_last))
     x_low, x_high = shift(x_last, "gx", 1), shift(x_first, "gx", -1)
-    a2, b2 = ringed(after(a1, x_low)), ringed(after(b1, x_high))
+    a2, b2 = ringed(after(a1, x_low, x_high)), ringed(after(b1, x_low, x_high))
     y_first, y_last = after(y_first, a1, b1), after(y_last, a1, b1)
-    y_first = jnp.concatenate([x_low[:, :1], y_first, x_high[:, :1]], axis=1).reshape(-1, CH)
-    y_last = jnp.concatenate([x_low[:, -1:], y_last, x_high[:, -1:]], axis=1).reshape(-1, CH)
+    y_first, y_last = pl.pallas_call(
+        edge_kernel,
+        out_shape=[jax.ShapeDtypeStruct((VZ, 16, CH), BF16)] * 2,
+        in_specs=[VMEM] * 4,
+        out_specs=[VMEM] * 2,
+        compiler_params=pltpu.CompilerParams(vmem_limit_bytes=6 << 20),
+        name="edges",
+    )(x_low, x_high, y_first, y_last)
     y_low, y_high = shift(y_last, "gy", 1), shift(y_first, "gy", -1)
 
-    a3, b3 = ringed(after(a2, y_low, y_high)), ringed(after(b2, y_low, y_high))
-    extra = after(extra, a2, b2)
+    a3 = ringed(after(a2, y_low, y_high))
+    extra = after(extra, a2)
     hidden, query = pl.pallas_call(
         conv_kernel,
         out_shape=(
             jax.ShapeDtypeStruct((ROWS, CH), F32),
             jax.ShapeDtypeStruct((ACT_MAX, PACK, LANES), BF16),
         ),
-        in_specs=[SMEM] + [VMEM] * 8 + [HBM] + [VMEM] * 2,
+        in_specs=[SMEM] + [VMEM] * 8 + [ANY] + [VMEM] * 2,
         out_specs=(VMEM, VMEM),
         scratch_shapes=[
             pltpu.VMEM((3, VZ, VX + 2, VY, CH), F32),
-            pltpu.VMEM((27, CH, CH), BF16),
+            pltpu.VMEM((3, 9, CH, CH), BF16),
+            pltpu.VMEM((ROWS, 3 * CH), BF16),
             pltpu.SemaphoreType.DMA((9,)),
         ],
-        compiler_params=pltpu.CompilerParams(vmem_limit_bytes=56 << 20),
+        compiler_params=pltpu.CompilerParams(vmem_limit_bytes=16 << 20),
         cost_estimate=pl.CostEstimate(flops=2 * 27 * ROWS * CH * CH, bytes_accessed=5 << 20, transcendentals=ROWS * CH),
         name="conv",
     )(
-        active, turned, x_low, x_high, y_low, y_high, norm_gain.reshape(1, CH),
-        conv_bias.reshape(1, CH), attn_gain.reshape(1, CH), conv_weight, q_weight, extra,
+        active, turned, x_low, x_high, y_low, y_high, vectors[0],
+        vectors[1], vectors[2], conv_weight, q_weight, extra,
     )
 
     def along(block, step):
         return move(block, lambda ring, line, core: (ring, line + step, core))
 
     here = lax.axis_index("gx").astype(jnp.int32).reshape(1)
+    query = after(query, b2)
+    b3 = ringed(after(b2, query))
+    queries = [query] + [along(query, d) for d in range(1, LINE)]
     a4 = ringed(after(a3, query))
-    query = after(query, a3)
-    queries = [query, along(query, 1), along(query, 2), along(after(query, b3), 3)]
-    kv_all = [a0, a1, a2, a3, a4, b0, b1, b2, b3]
-    kv_all += [swapped(after(block, *queries)) for block in (a1, a2, a3)] + [swapped(a4)]
-    kv_all += [swapped(after(block, *queries)) for block in (b1, b2, b3)]
+    xa1, xb1, xa2, xb2, xa3, xb3 = (swapped(after(block, *queries, b3)) for block in (a1, b1, a2, b2, a3, b3))
+    xa4 = swapped(after(a4, *queries))
+    kv_all = [a0, a1, a2, a3, a4, b0, b1, b2, b3, xa1, xa2, xa3, xa4, xb1, xb2, xb3]
     parts = pl.pallas_call(
         attend_kernel,
         out_shape=[jax.ShapeDtypeStruct((ACT_MAX, PACK, LANES), BF16)] * LINE,
@@ -423,9 +455,9 @@
     )(here, *queries, *kv_all)
 
     merged = [parts[0]] + [along(parts[d], -d) for d in range(1, LINE)]
-    out = pl.pallas_call(
+    return pl.pallas_call(
         merge_kernel,
-        out_shape=jax.ShapeDtypeStruct((ROWS, CH), F32),
+        out_shape=jax.ShapeDtypeStruct((VX, VY, VZ, CH), F32),
         in_specs=[SMEM] + [VMEM] * (LINE + 2),
         out_specs=VMEM,
         scratch_shapes=[
@@ -435,7 +467,6 @@
         compiler_params=pltpu.CompilerParams(vmem_limit_bytes=8 << 20),
         name="merge",
     )(active, *merged, hidden, out_weight)
-    return out.reshape(VZ, VX, VY, CH).transpose(1, 2, 0, 3)
 
 
 def solution(mesh):

time: 81.2 us -> 79.4 us (0.978)
  starting transfers between devices: 36.4 us -> 34.9 us
  other arithmetic: 1.47 us -> 0 us
    ppermute x4, waiting for transfers between devices: 2.24 us -> 5.1 us  [shift(): lax.ppermute(block, axis, [(i, i + step) for i in range(count) if 0 <= i...]
    pallas_call x1 -> x3, Pallas kernels: 1.19 us -> 3.69 us  [the longest x1 2.12 us: per_device(): pl.pallas_call(merge_kernel, out_shape=jax.ShapeDtypeStruct((VX, VY, VZ,...]
    ppermute x21, waiting for transfers between devices: 20.2 us -> 17.8 us  [move(): return lax.ppermute(block, 'gx', pairs)]
    pallas_call x1, Pallas kernels: 5.77 us -> 3.44 us  [per_device(): pl.pallas_call(conv_kernel, out_shape=(jax.ShapeDtypeStruct((ROWS, CH), F...]
    concatenate x2 -> x0, other arithmetic: 1.47 us -> none  [the longest x1 0.74 us: per_device(): jnp.concatenate([x_low[:, :1], y_first, x_high[:, :1]], axis=1)]
    pallas_call x1, Pallas kernels: 1.88 us -> 0.8 us  [per_device(): pl.pallas_call(face_kernel, out_shape=[face] * 4 + [jax.ShapeDtypeStruct(...]
    pallas_call x1, Pallas kernels: 7.03 us -> 8.05 us  [per_device(): pl.pallas_call(attend_kernel, out_shape=[jax.ShapeDtypeStruct((ACT_MAX, P...]
    ppermute x4, starting transfers between devices: 12.9 us -> 11.9 us  [shift(): lax.ppermute(block, axis, [(i, i + step) for i in range(count) if 0 <= i...]
  transfers between devices with their start and end apart: 25 -> 25, of which waited for: 14 -> 13; matrix products, arithmetic and copies ran while one was open for 4% -> 2% of each run, Pallas kernels for 10% -> 7%
where the time goes in v5:
time: 79.4 us; the launch traced here: 77.9 us
  starting transfers between devices  34.9 us (44%)
  waiting for transfers between devices  22.9 us (29%)
  Pallas kernels  16 us (20%)
  local copies, waits for them, and re-layouts  3.74 us (5%)
    ppermute x21, starting transfers between devices, move(): return lax.ppermute(block, 'gx', pairs)  23 us
    ppermute x21, waiting for transfers between devices, move(): return lax.ppermute(block, 'gx', pairs)  17.8 us
    ppermute x4, starting transfers between devices, shift(): lax.ppermute(block, axis, [(i, i + step) for i in range(count) if 0 <= i...  11.9 us
    pallas_call x1, Pallas kernels, per_device(): pl.pallas_call(attend_kernel, out_shape=[jax.ShapeDtypeStruct((ACT_MAX, P...  8.05 us
    ppermute x4, waiting for transfers between devices, shift(): lax.ppermute(block, axis, [(i, i + step) for i in range(count) if 0 <= i...  5.1 us
    unnamed x47, local copies, waits for them, and re-layouts  3.74 us
    pallas_call x1, Pallas kernels, per_device(): pl.pallas_call(conv_kernel, out_shape=(jax.ShapeDtypeStruct((ROWS, CH), F...  3.44 us
    pallas_call x1, Pallas kernels, per_device(): pl.pallas_call(merge_kernel, out_shape=jax.ShapeDtypeStruct((VX, VY, VZ,...  2.12 us
  transfers between devices with their start and end apart: 25, of which 13 were waited for; matrix products, arithmetic and copies ran while one was open for 2% of the time, Pallas kernels for 7%

profile of v5, /device:TPU:2, one launch (start us, length us, event | category | flops | bytes accessed | tf_op | source)
XLA Modules:
  0.0 77.9 jit_solution(4310284117894898446)
XLA Ops:
  0.1 2.0 %collective-permute-start.2 = (bf16[4,128,512]{2,1,0:T(8,128)(2,1)}, bf16[4,128,512]{2,1,0:T(8,128)(2,1)}, u32[]{:S(2)}, u32[]{:S(2)}) collective-permute-start(bf16[4,128,512]{2,1,0:T(8,128)(2,1)} %refs_4_.3), channel_id=1, source_target_pairs={{0,32},{4,228},{8,40},{12,236},{16,48},{20,244},{24,56},{28,252},{... | collective-permute-start | bytes 1572872 | tf_op jit(solution)/shard_map/ppermute | solution.py:351
  2.1 1.4 %copy.15.act_ref = s32[2,2,1]{2,1,0:T(2,128)} copy(s32[2,2,1]{1,2,0:T(1,128)} %param.12) | data formatting | bytes 32 | tf_op args[1]
  3.5 1.6 %tables.1.extra_ref = bf16[3,16,128]{2,1,0:T(8,128)(2,1)} custom-call(s32[2,2,1]{2,1,0:T(2,128)} %copy.15.act_ref, s32[1,1,4,4]{3,2,1,0:T(4,128)} %owner_ref.1, s32[1,1,4,4]{3,2,1,0:T(4,128)} %slot_ref.1, f32[1,256]{1,0:T(1,128)} %bitcast.4, f32[1,256]{1,0:T(1,128)} %bitcast.7, f32[1,256]{1,0:T(1,128)} %bitcast.9, bf16[27,256,256]{2,1,0:T(8,128)(2,1)} %weight_ref.1, ...), custom_call_target="tpu_custom_call" | custom-call | tf_op jit(solution)/shard_map/tables/pallas_call | solution.py:368
  5.0 0.8 %faces.1 = (bf16[4,8,256]{2,1,0:T(8,128)(2,1)S(1)}, bf16[4,8,256]{2,1,0:T(8,128)(2,1)S(1)}, bf16[4,8,256]{2,1,0:T(8,128)(2,1)S(1)}, bf16[4,8,256]{2,1,0:T(8,128)(2,1)S(1)}, f32[4,8,8,256]{3,2,1,0:T(8,128)S(1)}) custom-call(s32[2,2,1]{2,1,0:T(2,128)S(1)} %copy-done.8, f32[8,8,4,256]{3,2,1,0:T(4,128)S(1)} %copy-done.1, f32[1,256]{1,0:T(1,128)S(1)} %bitcast.5), custom_call_target="tpu_custom_call" | custom-call | tf_op jit(solution)/shard_map/faces/pallas_call | solution.py:377
  5.9 2.0 %collective-permute-start.4 = (bf16[4,128,512]{2,1,0:T(8,128)(2,1)}, bf16[4,128,512]{2,1,0:T(8,128)(2,1)}, u32[]{:S(2)}, u32[]{:S(2)}) collective-permute-start(bf16[4,128,512]{2,1,0:T(8,128)(2,1)} %collective-permute-done.3.refs_9_), channel_id=1, source_target_pairs={{0,32},{4,228},{8,40},{12,236},{16,48},{20,244},{24,56},{28,252},{... | collective-permute-start | bytes 1572872 | tf_op jit(solution)/shard_map/ppermute | solution.py:351
  7.9 4.8 %collective-permute-start = (bf16[4,8,256]{2,1,0:T(8,128)(2,1)S(1)}, bf16[4,8,256]{2,1,0:T(8,128)(2,1)S(1)}, u32[]{:S(2)}, u32[]{:S(2)}) collective-permute-start(bf16[4,8,256]{2,1,0:T(8,128)(2,1)S(1)} %get-tuple-element.38), channel_id=1, source_target_pairs={{0,4},{4,8},{8,12},{12,16},{16,20},{20,24},{24,28},{28,32},{32,36}... | collective-permute-start | bytes 49160 | tf_op jit(solution)/shard_map/ppermute | solution.py:339
  12.6 1.3 %collective-permute-start.1 = (bf16[4,8,256]{2,1,0:T(8,128)(2,1)S(1)}, bf16[4,8,256]{2,1,0:T(8,128)(2,1)S(1)}, u32[]{:S(2)}, u32[]{:S(2)}) collective-permute-start(bf16[4,8,256]{2,1,0:T(8,128)(2,1)S(1)} %get-tuple-element.39), channel_id=1, source_target_pairs={{4,0},{8,4},{12,8},{16,12},{20,16},{24,20},{28,24},{32,28},{36,32}... | collective-permute-start | bytes 49160 | tf_op jit(solution)/shard_map/ppermute | solution.py:339
  14.0 1.8 %collective-permute-done.1.xhi_ref = bf16[4,8,256]{2,1,0:T(8,128)(2,1)S(1)} collective-permute-done((bf16[4,8,256]{2,1,0:T(8,128)(2,1)S(1)}, bf16[4,8,256]{2,1,0:T(8,128)(2,1)S(1)}, u32[]{:S(2)}, u32[]{:S(2)}) %collective-permute-start.1) | collective-permute-done | bytes 16416 | tf_op jit(solution)/shard_map/ppermute | solution.py:339
  15.7 4.4 %collective-permute-start.7 = (bf16[4,128,512]{2,1,0:T(8,128)(2,1)}, bf16[4,128,512]{2,1,0:T(8,128)(2,1)S(1)}, u32[]{:S(2)}, u32[]{:S(2)}) collective-permute-start(bf16[4,128,512]{2,1,0:T(8,128)(2,1)} %collective-permute-done.2.refs_5_), channel_id=1, source_target_pairs={{0,32},{4,228},{8,40},{12,236},{16,48},{20,244},{24,56},{28,252},{... | collective-permute-start | bytes 1572872 | tf_op jit(solution)/shard_map/ppermute | solution.py:351
  20.1 1.9 %collective-permute-start.8 = (bf16[4,128,512]{2,1,0:T(8,128)(2,1)}, bf16[4,128,512]{2,1,0:T(8,128)(2,1)}, u32[]{:S(2)}, u32[]{:S(2)}) collective-permute-start(bf16[4,128,512]{2,1,0:T(8,128)(2,1)} %collective-permute-done.4.refs_10_), channel_id=1, source_target_pairs={{0,32},{4,228},{8,40},{12,236},{16,48},{20,244},{24,56},{28,252},{... | collective-permute-start | bytes 1572872 | tf_op jit(solution)/shard_map/ppermute | solution.py:351
  22.0 3.4 %collective-permute-start.5 = (bf16[4,16,256]{2,1,0:T(8,128)(2,1)S(1)}, bf16[4,16,256]{2,1,0:T(8,128)(2,1)S(1)}, u32[]{:S(2)}, u32[]{:S(2)}) collective-permute-start(bf16[4,16,256]{2,1,0:T(8,128)(2,1)S(1)} %get-tuple-element.45), channel_id=1, source_target_pairs={{0,1},{1,2},{2,3},{4,5},{5,6},{6,7},{8,9},{9,10},{10,11},{12,13},{... | collective-permute-start | bytes 98312 | tf_op jit(solution)/shard_map/ppermute | solution.py:339
  25.4 2.4 %collective-permute-start.6 = (bf16[4,16,256]{2,1,0:T(8,128)(2,1)S(1)}, bf16[4,16,256]{2,1,0:T(8,128)(2,1)S(1)}, u32[]{:S(2)}, u32[]{:S(2)}) collective-permute-start(bf16[4,16,256]{2,1,0:T(8,128)(2,1)S(1)} %get-tuple-element.46), channel_id=1, source_target_pairs={{1,0},{2,1},{3,2},{5,4},{6,5},{7,6},{9,8},{10,9},{11,10},{13,12},{... | collective-permute-start | bytes 98312 | tf_op jit(solution)/shard_map/ppermute | solution.py:339
  27.9 3.3 %collective-permute-done.6.yhi_ref = bf16[4,16,256]{2,1,0:T(8,128)(2,1)S(1)} collective-permute-done((bf16[4,16,256]{2,1,0:T(8,128)(2,1)S(1)}, bf16[4,16,256]{2,1,0:T(8,128)(2,1)S(1)}, u32[]{:S(2)}, u32[]{:S(2)}) %collective-permute-start.6) | collective-permute-done | bytes 32800 | tf_op jit(solution)/shard_map/ppermute | solution.py:339
  31.3 1.0 %collective-permute-start.12 = (bf16[4,128,512]{2,1,0:T(8,128)(2,1)S(1)}, bf16[4,128,512]{2,1,0:T(8,128)(2,1)}, u32[]{:S(2)}, u32[]{:S(2)}) collective-permute-start(bf16[4,128,512]{2,1,0:T(8,128)(2,1)S(1)} %collective-permute-done.7.refs_6_), channel_id=1, source_target_pairs={{0,32},{4,228},{8,40},{12,236},{16,48},{20,244},{24,56},{28,252},{... | collective-permute-start | bytes 1572872 | tf_op jit(solution)/shard_map/ppermute | solution.py:351
  33.0 3.4 %conv.1 = (f32[256,256]{1,0:T(8,128)S(1)}, bf16[3,144,128]{2,1,0:T(8,128)(2,1)S(1)}) custom-call(s32[2,2,1]{2,1,0:T(2,128)S(1)} %copy-done.8, f32[4,8,8,256]{3,2,1,0:T(8,128)S(1)} %get-tuple-element.37.latent_ref, bf16[4,8,256]{2,1,0:T(8,128)(2,1)S(1)} %collective-permute-done.xlo_ref, bf16[4,8,256]{2,1,0:T(8,128)(2,1)S(1)} %collective-permute-done.1.xhi_ref, ...), custom_call_target="tpu_custom_call" | custom-call | flops 905969664 | bytes 5242880 | tf_op jit(solution)/shard_map/conv/pallas_call | solution.py:403
  37.2 2.1 %collective-permute-start.14 = (bf16[4,128,512]{2,1,0:T(8,128)(2,1)}, bf16[4,128,512]{2,1,0:T(8,128)(2,1)S(1)}, u32[]{:S(2)}, u32[]{:S(2)}) collective-permute-start(bf16[4,128,512]{2,1,0:T(8,128)(2,1)} %collective-permute-done.8.refs_11_), channel_id=1, source_target_pairs={{0,32},{4,228},{8,40},{12,236},{16,48},{20,244},{24,56},{28,252},{... | collective-permute-start | bytes 1572872 | tf_op jit(solution)/shard_map/ppermute | solution.py:351
  40.0 1.2 %collective-permute-start.9 = (bf16[3,144,128]{2,1,0:T(8,128)(2,1)S(1)}, bf16[3,144,128]{2,1,0:T(8,128)(2,1)S(1)}, u32[]{:S(2)}, u32[]{:S(2)}) collective-permute-start(bf16[3,144,128]{2,1,0:T(8,128)(2,1)S(1)} %get-tuple-element.51.refs_0_), channel_id=1, source_target_pairs={{0,8},{4,12},{8,16},{12,20},{16,24},{20,28},{24,0},{28,4},{32,40},... | collective-permute-start | bytes 331784 | tf_op jit(solution)/shard_map/ppermute | solution.py:351
  41.8 2.4 %collective-permute-start.13 = (bf16[4,128,512]{2,1,0:T(8,128)(2,1)}, bf16[4,128,512]{2,1,0:T(8,128)(2,1)S(1)}, u32[]{:S(2)}, u32[]{:S(2)}) collective-permute-start(bf16[4,128,512]{2,1,0:T(8,128)(2,1)} %collective-permute-done.12.refs_7_), channel_id=1, source_target_pairs={{0,32},{4,228},{8,40},{12,236},{16,48},{20,244},{24,56},{28,252},{... | collective-permute-start | bytes 1572872 | tf_op jit(solution)/shard_map/ppermute | solution.py:351
  44.5 2.5 %collective-permute-done.10.refs_2_ = bf16[3,144,128]{2,1,0:T(8,128)(2,1)S(1)} collective-permute-done((bf16[3,144,128]{2,1,0:T(8,128)(2,1)S(1)}, bf16[3,144,128]{2,1,0:T(8,128)(2,1)S(1)}, u32[]{:S(2)}, u32[]{:S(2)}) %collective-permute-start.10) | collective-permute-done | bytes 110624 | tf_op jit(solution)/shard_map/ppermute | solution.py:351
  47.1 0.8 %collective-permute-done.9.refs_1_ = bf16[3,144,128]{2,1,0:T(8,128)(2,1)S(1)} collective-permute-done((bf16[3,144,128]{2,1,0:T(8,128)(2,1)S(1)}, bf16[3,144,128]{2,1,0:T(8,128)(2,1)S(1)}, u32[]{:S(2)}, u32[]{:S(2)}) %collective-permute-start.9) | collective-permute-done | bytes 110624 | tf_op jit(solution)/shard_map/ppermute | solution.py:351
  49.0 4.4 %collective-permute-done.13.refs_8_ = bf16[4,128,512]{2,1,0:T(8,128)(2,1)S(1)} collective-permute-done((bf16[4,128,512]{2,1,0:T(8,128)(2,1)}, bf16[4,128,512]{2,1,0:T(8,128)(2,1)S(1)}, u32[]{:S(2)}, u32[]{:S(2)}) %collective-permute-start.13) | collective-permute-done | bytes 524320 | tf_op jit(solution)/shard_map/ppermute | solution.py:351
  54.0 1.6 %collective-permute-done.20.refs_18_ = bf16[4,128,512]{2,1,0:T(8,128)(2,1)} collective-permute-done((bf16[4,128,512]{2,1,0:T(8,128)(2,1)}, bf16[4,128,512]{2,1,0:T(8,128)(2,1)}, u32[]{:S(2)}, u32[]{:S(2)}) %collective-permute-start.20) | collective-permute-done | bytes 524320 | tf_op jit(solution)/shard_map/ppermute | solution.py:351
  56.2 0.7 collective-permute-done.18.refs_16_
  57.0 8.0 %attend.1 = (bf16[3,144,128]{2,1,0:T(8,128)(2,1)}, bf16[3,144,128]{2,1,0:T(8,128)(2,1)}, bf16[3,144,128]{2,1,0:T(8,128)(2,1)}, bf16[3,144,128]{2,1,0:T(8,128)(2,1)}) custom-call(s32[1]{0:T(128)} %bitcast.here_ref, bf16[3,144,128]{2,1,0:T(8,128)(2,1)} %copy-done.6, bf16[3,144,128]{2,1,0:T(8,128)(2,1)} %copy-done.22, bf16[3,144,128]{2,1,0:T(8,128)(2,1)} %copy-done.21, ...), custom_call_target="tpu_custom_call" | custom-call | tf_op jit(solution)/shard_map/attend/pallas_call | solution.py:436
  65.1 0.8 %collective-permute-start.22 = (bf16[3,144,128]{2,1,0:T(8,128)(2,1)}, bf16[3,144,128]{2,1,0:T(8,128)(2,1)S(1)}, u32[]{:S(2)}, u32[]{:S(2)}) collective-permute-start(bf16[3,144,128]{2,1,0:T(8,128)(2,1)} %get-tuple-element.63), channel_id=1, source_target_pairs={{0,24},{4,28},{8,0},{12,4},{16,8},{20,12},{24,16},{28,20},{32,56},... | collective-permute-start | bytes 331784 | tf_op jit(solution)/shard_map/ppermute | solution.py:351
  65.9 1.6 %collective-permute-start.23 = (bf16[3,144,128]{2,1,0:T(8,128)(2,1)}, bf16[3,144,128]{2,1,0:T(8,128)(2,1)S(1)}, u32[]{:S(2)}, u32[]{:S(2)}) collective-permute-start(bf16[3,144,128]{2,1,0:T(8,128)(2,1)} %get-tuple-element.64), channel_id=1, source_target_pairs={{0,16},{4,20},{8,24},{12,28},{16,0},{20,4},{24,8},{28,12},{32,48},... | collective-permute-start | bytes 331784 | tf_op jit(solution)/shard_map/ppermute | solution.py:351
  67.5 1.0 %collective-permute-start.24 = (bf16[3,144,128]{2,1,0:T(8,128)(2,1)}, bf16[3,144,128]{2,1,0:T(8,128)(2,1)S(1)}, u32[]{:S(2)}, u32[]{:S(2)}) collective-permute-start(bf16[3,144,128]{2,1,0:T(8,128)(2,1)} %get-tuple-element.65), channel_id=1, source_target_pairs={{0,8},{4,12},{8,16},{12,20},{16,24},{20,28},{24,0},{28,4},{32,40},... | collective-permute-start | bytes 331784 | tf_op jit(solution)/shard_map/ppermute | solution.py:351
  68.5 2.6 %collective-permute-done.22.refs_1_ = bf16[3,144,128]{2,1,0:T(8,128)(2,1)S(1)} collective-permute-done((bf16[3,144,128]{2,1,0:T(8,128)(2,1)}, bf16[3,144,128]{2,1,0:T(8,128)(2,1)S(1)}, u32[]{:S(2)}, u32[]{:S(2)}) %collective-permute-start.22) | collective-permute-done | bytes 110624 | tf_op jit(solution)/shard_map/ppermute | solution.py:351
  71.2 2.1 %collective-permute-done.23.refs_2_ = bf16[3,144,128]{2,1,0:T(8,128)(2,1)S(1)} collective-permute-done((bf16[3,144,128]{2,1,0:T(8,128)(2,1)}, bf16[3,144,128]{2,1,0:T(8,128)(2,1)S(1)}, u32[]{:S(2)}, u32[]{:S(2)}) %collective-permute-start.23) | collective-permute-done | bytes 110624 | tf_op jit(solution)/shard_map/ppermute | solution.py:351
  73.3 1.6 %collective-permute-done.24.refs_3_ = bf16[3,144,128]{2,1,0:T(8,128)(2,1)S(1)} collective-permute-done((bf16[3,144,128]{2,1,0:T(8,128)(2,1)}, bf16[3,144,128]{2,1,0:T(8,128)(2,1)S(1)}, u32[]{:S(2)}, u32[]{:S(2)}) %collective-permute-start.24) | collective-permute-done | bytes 110624 | tf_op jit(solution)/shard_map/ppermute | solution.py:351
  74.9 0.9 %copy-done.7 = bf16[3,144,128]{2,1,0:T(8,128)(2,1)S(1)} copy-done((bf16[3,144,128]{2,1,0:T(8,128)(2,1)S(1)}, bf16[3,144,128]{2,1,0:T(8,128)(2,1)}, u32[]{:S(2)}) %copy-start.7) | copy-done | bytes 110616
  75.8 2.1 %merge.1 = f32[8,8,4,256]{3,2,1,0:T(4,128)} custom-call(s32[2,2,1]{2,1,0:T(2,128)S(1)} %copy-done.8, bf16[3,144,128]{2,1,0:T(8,128)(2,1)S(1)} %copy-done.7, bf16[3,144,128]{2,1,0:T(8,128)(2,1)S(1)} %collective-permute-done.22.refs_1_, bf16[3,144,128]{2,1,0:T(8,128)(2,1)S(1)} %collective-permute-done.23.refs_2_, ...), custom_call_target="tpu_custom_call" | custom-call | tf_op jit(solution)/shard_map/merge/pallas_call | solution.py:458
  (71 shorter events, 5.5 us)
Async XLA Ops:
  0.0 32.3 %copy-start = (bf16[27,256,256]{2,1,0:T(8,128)(2,1)S(1)}, bf16[27,256,256]{2,1,0:T(8,128)(2,1)}, u32[]{:S(2)}) copy-start(bf16[27,256,256]{2,1,0:T(8,128)(2,1)} %weight_ref.1) | copy-start | bytes 10616836
  0.0 32.3 %copy-start.12 = (f32[256]{0:T(256)S(1)}, f32[256]{0:T(256)}, u32[]{:S(2)}) copy-start(f32[256]{0:T(256)} %param.19) | copy-start | bytes 3076
  0.0 32.3 %copy-start.11 = (f32[256]{0:T(256)S(1)}, f32[256]{0:T(256)}, u32[]{:S(2)}) copy-start(f32[256]{0:T(256)} %param.18) | copy-start | bytes 3076
  0.0 5.8 %collective-permute-start.3 = (bf16[4,128,512]{2,1,0:T(8,128)(2,1)}, bf16[4,128,512]{2,1,0:T(8,128)(2,1)}, u32[]{:S(2)}, u32[]{:S(2)}) collective-permute-start(bf16[4,128,512]{2,1,0:T(8,128)(2,1)} %refs_4_.3), channel_id=1, source_target_pairs={{0,4},{4,0},{8,12},{12,8},{16,20},{20,16},{24,28},{28,24},{32,36},... | collective-permute-start | bytes 1572872 | tf_op jit(solution)/shard_map/ppermute | solution.py:351
  0.1 15.6 %collective-permute-start.2 = (bf16[4,128,512]{2,1,0:T(8,128)(2,1)}, bf16[4,128,512]{2,1,0:T(8,128)(2,1)}, u32[]{:S(2)}, u32[]{:S(2)}) collective-permute-start(bf16[4,128,512]{2,1,0:T(8,128)(2,1)} %refs_4_.3), channel_id=1, source_target_pairs={{0,32},{4,228},{8,40},{12,236},{16,48},{20,244},{24,56},{28,252},{... | collective-permute-start | bytes 1572872 | tf_op jit(solution)/shard_map/ppermute | solution.py:351
  3.5 28.8 %copy-start.2 = (bf16[256,256]{1,0:T(8,128)(2,1)S(1)}, bf16[256,256]{1,0:T(8,128)(2,1)}, u32[]{:S(2)}) copy-start(bf16[256,256]{1,0:T(8,128)(2,1)} %qw_ref.1) | copy-start | bytes 393220
  5.9 14.2 %collective-permute-start.4 = (bf16[4,128,512]{2,1,0:T(8,128)(2,1)}, bf16[4,128,512]{2,1,0:T(8,128)(2,1)}, u32[]{:S(2)}, u32[]{:S(2)}) collective-permute-start(bf16[4,128,512]{2,1,0:T(8,128)(2,1)} %collective-permute-done.3.refs_9_), channel_id=1, source_target_pairs={{0,32},{4,228},{8,40},{12,236},{16,48},{20,244},{24,56},{28,252},{... | collective-permute-start | bytes 1572872 | tf_op jit(solution)/shard_map/ppermute | solution.py:351
  7.9 6.1 %collective-permute-start = (bf16[4,8,256]{2,1,0:T(8,128)(2,1)S(1)}, bf16[4,8,256]{2,1,0:T(8,128)(2,1)S(1)}, u32[]{:S(2)}, u32[]{:S(2)}) collective-permute-start(bf16[4,8,256]{2,1,0:T(8,128)(2,1)S(1)} %get-tuple-element.38), channel_id=1, source_target_pairs={{0,4},{4,8},{8,12},{12,16},{16,20},{20,24},{24,28},{28,32},{32,36}... | collective-permute-start | bytes 49160 | tf_op jit(solution)/shard_map/ppermute | solution.py:339
  12.6 3.1 %collective-permute-start.1 = (bf16[4,8,256]{2,1,0:T(8,128)(2,1)S(1)}, bf16[4,8,256]{2,1,0:T(8,128)(2,1)S(1)}, u32[]{:S(2)}, u32[]{:S(2)}) collective-permute-start(bf16[4,8,256]{2,1,0:T(8,128)(2,1)S(1)} %get-tuple-element.39), channel_id=1, source_target_pairs={{4,0},{8,4},{12,8},{16,12},{20,16},{24,20},{28,24},{32,28},{36,32}... | collective-permute-start | bytes 49160 | tf_op jit(solution)/shard_map/ppermute | solution.py:339
  15.7 12.2 %collective-permute-start.7 = (bf16[4,128,512]{2,1,0:T(8,128)(2,1)}, bf16[4,128,512]{2,1,0:T(8,128)(2,1)S(1)}, u32[]{:S(2)}, u32[]{:S(2)}) collective-permute-start(bf16[4,128,512]{2,1,0:T(8,128)(2,1)} %collective-permute-done.2.refs_5_), channel_id=1, source_target_pairs={{0,32},{4,228},{8,40},{12,236},{16,48},{20,244},{24,56},{28,252},{... | collective-permute-start | bytes 1572872 | tf_op jit(solution)/shard_map/ppermute | solution.py:351
  20.1 17.1 %collective-permute-start.8 = (bf16[4,128,512]{2,1,0:T(8,128)(2,1)}, bf16[4,128,512]{2,1,0:T(8,128)(2,1)}, u32[]{:S(2)}, u32[]{:S(2)}) collective-permute-start(bf16[4,128,512]{2,1,0:T(8,128)(2,1)} %collective-permute-done.4.refs_10_), channel_id=1, source_target_pairs={{0,32},{4,228},{8,40},{12,236},{16,48},{20,244},{24,56},{28,252},{... | collective-permute-start | bytes 1572872 | tf_op jit(solution)/shard_map/ppermute | solution.py:351
  22.0 5.9 %collective-permute-start.5 = (bf16[4,16,256]{2,1,0:T(8,128)(2,1)S(1)}, bf16[4,16,256]{2,1,0:T(8,128)(2,1)S(1)}, u32[]{:S(2)}, u32[]{:S(2)}) collective-permute-start(bf16[4,16,256]{2,1,0:T(8,128)(2,1)S(1)} %get-tuple-element.45), channel_id=1, source_target_pairs={{0,1},{1,2},{2,3},{4,5},{5,6},{6,7},{8,9},{9,10},{10,11},{12,13},{... | collective-permute-start | bytes 98312 | tf_op jit(solution)/shard_map/ppermute | solution.py:339
  25.4 5.8 %collective-permute-start.6 = (bf16[4,16,256]{2,1,0:T(8,128)(2,1)S(1)}, bf16[4,16,256]{2,1,0:T(8,128)(2,1)S(1)}, u32[]{:S(2)}, u32[]{:S(2)}) collective-permute-start(bf16[4,16,256]{2,1,0:T(8,128)(2,1)S(1)} %get-tuple-element.46), channel_id=1, source_target_pairs={{1,0},{2,1},{3,2},{5,4},{6,5},{7,6},{9,8},{10,9},{11,10},{13,12},{... | collective-permute-start | bytes 98312 | tf_op jit(solution)/shard_map/ppermute | solution.py:339
  27.9 20.1 %copy-start.13 = (bf16[4,128,512]{2,1,0:T(8,128)(2,1)}, bf16[4,128,512]{2,1,0:T(8,128)(2,1)S(1)}, u32[]{:S(2)}) copy-start(bf16[4,128,512]{2,1,0:T(8,128)(2,1)S(1)} %collective-permute-done.7.refs_6_) | copy-start | bytes 1572868
  31.3 10.5 %collective-permute-start.12 = (bf16[4,128,512]{2,1,0:T(8,128)(2,1)S(1)}, bf16[4,128,512]{2,1,0:T(8,128)(2,1)}, u32[]{:S(2)}, u32[]{:S(2)}) collective-permute-start(bf16[4,128,512]{2,1,0:T(8,128)(2,1)S(1)} %collective-permute-done.7.refs_6_), channel_id=1, source_target_pairs={{0,32},{4,228},{8,40},{12,236},{16,48},{20,244},{24,56},{28,252},{... | collective-permute-start | bytes 1572872 | tf_op jit(solution)/shard_map/ppermute | solution.py:351
  37.2 10.8 %collective-permute-start.14 = (bf16[4,128,512]{2,1,0:T(8,128)(2,1)}, bf16[4,128,512]{2,1,0:T(8,128)(2,1)S(1)}, u32[]{:S(2)}, u32[]{:S(2)}) collective-permute-start(bf16[4,128,512]{2,1,0:T(8,128)(2,1)} %collective-permute-done.8.refs_11_), channel_id=1, source_target_pairs={{0,32},{4,228},{8,40},{12,236},{16,48},{20,244},{24,56},{28,252},{... | collective-permute-start | bytes 1572872 | tf_op jit(solution)/shard_map/ppermute | solution.py:351
  39.2 5.3 %collective-permute-start.11 = (bf16[3,144,128]{2,1,0:T(8,128)(2,1)S(1)}, bf16[3,144,128]{2,1,0:T(8,128)(2,1)S(1)}, u32[]{:S(2)}, u32[]{:S(2)}) collective-permute-start(bf16[3,144,128]{2,1,0:T(8,128)(2,1)S(1)} %get-tuple-element.51.refs_0_), channel_id=1, source_target_pairs={{0,24},{4,28},{8,0},{12,4},{16,8},{20,12},{24,16},{28,20},{32,56},... | collective-permute-start | bytes 331784 | tf_op jit(solution)/shard_map/ppermute | solution.py:351
  39.7 7.4 %collective-permute-start.10 = (bf16[3,144,128]{2,1,0:T(8,128)(2,1)S(1)}, bf16[3,144,128]{2,1,0:T(8,128)(2,1)S(1)}, u32[]{:S(2)}, u32[]{:S(2)}) collective-permute-start(bf16[3,144,128]{2,1,0:T(8,128)(2,1)S(1)} %get-tuple-element.51.refs_0_), channel_id=1, source_target_pairs={{0,16},{4,20},{8,24},{12,28},{16,0},{20,4},{24,8},{28,12},{32,48},... | collective-permute-start | bytes 331784 | tf_op jit(solution)/shard_map/ppermute | solution.py:351
  40.0 7.9 %collective-permute-start.9 = (bf16[3,144,128]{2,1,0:T(8,128)(2,1)S(1)}, bf16[3,144,128]{2,1,0:T(8,128)(2,1)S(1)}, u32[]{:S(2)}, u32[]{:S(2)}) collective-permute-start(bf16[3,144,128]{2,1,0:T(8,128)(2,1)S(1)} %get-tuple-element.51.refs_0_), channel_id=1, source_target_pairs={{0,8},{4,12},{8,16},{12,20},{16,24},{20,28},{24,0},{28,4},{32,40},... | collective-permute-start | bytes 331784 | tf_op jit(solution)/shard_map/ppermute | solution.py:351
  41.8 11.6 %collective-permute-start.13 = (bf16[4,128,512]{2,1,0:T(8,128)(2,1)}, bf16[4,128,512]{2,1,0:T(8,128)(2,1)S(1)}, u32[]{:S(2)}, u32[]{:S(2)}) collective-permute-start(bf16[4,128,512]{2,1,0:T(8,128)(2,1)} %collective-permute-done.12.refs_7_), channel_id=1, source_target_pairs={{0,32},{4,228},{8,40},{12,236},{16,48},{20,244},{24,56},{28,252},{... | collective-permute-start | bytes 1572872 | tf_op jit(solution)/shard_map/ppermute | solution.py:351
  47.9 5.5 %collective-permute-start.15 = (bf16[4,128,512]{2,1,0:T(8,128)(2,1)}, bf16[4,128,512]{2,1,0:T(8,128)(2,1)S(1)}, u32[]{:S(2)}, u32[]{:S(2)}) collective-permute-start(bf16[4,128,512]{2,1,0:T(8,128)(2,1)} %collective-permute-done.2.refs_5_), channel_id=1, source_target_pairs={{0,4},{4,0},{8,12},{12,8},{16,20},{20,16},{24,28},{28,24},{32,36},... | collective-permute-start | bytes 1572872 | tf_op jit(solution)/shard_map/ppermute | solution.py:351
  48.0 5.9 %collective-permute-start.16 = (bf16[4,128,512]{2,1,0:T(8,128)(2,1)S(1)}, bf16[4,128,512]{2,1,0:T(8,128)(2,1)S(1)}, u32[]{:S(2)}, u32[]{:S(2)}) collective-permute-start(bf16[4,128,512]{2,1,0:T(8,128)(2,1)S(1)} %collective-permute-done.7.refs_6_), channel_id=1, source_target_pairs={{0,4},{4,0},{8,12},{12,8},{16,20},{20,16},{24,28},{28,24},{32,36},... | collective-permute-start | bytes 1572872 | tf_op jit(solution)/shard_map/ppermute | solution.py:351
  48.5 5.5 %collective-permute-start.17 = (bf16[4,128,512]{2,1,0:T(8,128)(2,1)}, bf16[4,128,512]{2,1,0:T(8,128)(2,1)S(1)}, u32[]{:S(2)}, u32[]{:S(2)}) collective-permute-start(bf16[4,128,512]{2,1,0:T(8,128)(2,1)} %collective-permute-done.12.refs_7_), channel_id=1, source_target_pairs={{0,4},{4,0},{8,12},{12,8},{16,20},{20,16},{24,28},{28,24},{32,36},... | collective-permute-start | bytes 1572872 | tf_op jit(solution)/shard_map/ppermute | solution.py:351
  48.6 5.4 %collective-permute-start.19 = (bf16[4,128,512]{2,1,0:T(8,128)(2,1)}, bf16[4,128,512]{2,1,0:T(8,128)(2,1)S(1)}, u32[]{:S(2)}, u32[]{:S(2)}) collective-permute-start(bf16[4,128,512]{2,1,0:T(8,128)(2,1)} %collective-permute-done.4.refs_10_), channel_id=1, source_target_pairs={{0,4},{4,0},{8,12},{12,8},{16,20},{20,16},{24,28},{28,24},{32,36},... | collective-permute-start | bytes 1572872 | tf_op jit(solution)/shard_map/ppermute | solution.py:351
  53.4 2.3 %collective-permute-start.20 = (bf16[4,128,512]{2,1,0:T(8,128)(2,1)}, bf16[4,128,512]{2,1,0:T(8,128)(2,1)}, u32[]{:S(2)}, u32[]{:S(2)}) collective-permute-start(bf16[4,128,512]{2,1,0:T(8,128)(2,1)} %collective-permute-done.8.refs_11_), channel_id=1, source_target_pairs={{0,4},{4,0},{8,12},{12,8},{16,20},{20,16},{24,28},{28,24},{32,36},... | collective-permute-start | bytes 1572872 | tf_op jit(solution)/shard_map/ppermute | solution.py:351
  53.4 2.8 %collective-permute-start.21 = (bf16[4,128,512]{2,1,0:T(8,128)(2,1)S(1)}, bf16[4,128,512]{2,1,0:T(8,128)(2,1)}, u32[]{:S(2)}, u32[]{:S(2)}) collective-permute-start(bf16[4,128,512]{2,1,0:T(8,128)(2,1)S(1)} %collective-permute-done.14.refs_12_), channel_id=1, source_target_pairs={{0,4},{4,0},{8,12},{12,8},{16,20},{20,16},{24,28},{28,24},{32,36},... | collective-permute-start | bytes 1572872 | tf_op jit(solution)/shard_map/ppermute | solution.py:351
  53.9 3.0 %collective-permute-start.18 = (bf16[4,128,512]{2,1,0:T(8,128)(2,1)S(1)}, bf16[4,128,512]{2,1,0:T(8,128)(2,1)}, u32[]{:S(2)}, u32[]{:S(2)}) collective-permute-start(bf16[4,128,512]{2,1,0:T(8,128)(2,1)S(1)} %collective-permute-done.13.refs_8_), channel_id=1, source_target_pairs={{0,4},{4,0},{8,12},{12,8},{16,20},{20,16},{24,28},{28,24},{32,36},... | collective-permute-start | bytes 1572872 | tf_op jit(solution)/shard_map/ppermute | solution.py:351
  57.0 17.9 %copy-start.4 = (f32[256,256]{1,0:T(8,128)S(1)}, f32[256,256]{1,0:T(8,128)}, u32[]{:S(2)}) copy-start(f32[256,256]{1,0:T(8,128)} %copy-done.3) | copy-start | bytes 786436
  57.0 17.9 %copy-start.5 = (bf16[256,256]{1,0:T(8,128)(2,1)S(1)}, bf16[256,256]{1,0:T(8,128)(2,1)}, u32[]{:S(2)}) copy-start(bf16[256,256]{1,0:T(8,128)(2,1)} %refs_5_.3) | copy-start | bytes 393220
  65.1 6.1 %collective-permute-start.22 = (bf16[3,144,128]{2,1,0:T(8,128)(2,1)}, bf16[3,144,128]{2,1,0:T(8,128)(2,1)S(1)}, u32[]{:S(2)}, u32[]{:S(2)}) collective-permute-start(bf16[3,144,128]{2,1,0:T(8,128)(2,1)} %get-tuple-element.63), channel_id=1, source_target_pairs={{0,24},{4,28},{8,0},{12,4},{16,8},{20,12},{24,16},{28,20},{32,56},... | collective-permute-start | bytes 331784 | tf_op jit(solution)/shard_map/ppermute | solution.py:351
  65.9 7.4 %collective-permute-start.23 = (bf16[3,144,128]{2,1,0:T(8,128)(2,1)}, bf16[3,144,128]{2,1,0:T(8,128)(2,1)S(1)}, u32[]{:S(2)}, u32[]{:S(2)}) collective-permute-start(bf16[3,144,128]{2,1,0:T(8,128)(2,1)} %get-tuple-element.64), channel_id=1, source_target_pairs={{0,16},{4,20},{8,24},{12,28},{16,0},{20,4},{24,8},{28,12},{32,48},... | collective-permute-start | bytes 331784 | tf_op jit(solution)/shard_map/ppermute | solution.py:351
  67.5 7.3 %collective-permute-start.24 = (bf16[3,144,128]{2,1,0:T(8,128)(2,1)}, bf16[3,144,128]{2,1,0:T(8,128)(2,1)S(1)}, u32[]{:S(2)}, u32[]{:S(2)}) collective-permute-start(bf16[3,144,128]{2,1,0:T(8,128)(2,1)} %get-tuple-element.65), channel_id=1, source_target_pairs={{0,8},{4,12},{8,16},{12,20},{16,24},{20,28},{24,0},{28,4},{32,40},... | collective-permute-start | bytes 331784 | tf_op jit(solution)/shard_map/ppermute | solution.py:351
  (16 other events, 69.8 us)

commit v6 on v5

--- a/solution.py
+++ b/solution.py
@@ -59,8 +59,28 @@
     return query == (lane & 63), ((row >> 5) & 1) * 2 + ((row >> 2) & 1), lane
 
 
-def table_kernel(act_ref, owner_ref, slot_ref, *refs):
-    extra_ref = refs[-1]
+def near_kernel(*refs):
+    refs[-1][...] = jnp.zeros_like(refs[-1])
+
+
+def face_kernel(
+    act_ref, owner_ref, slot_ref, latent_ref, gain_ref, near_ref,
+    xa_ref, xb_ref, ya_ref, yb_ref, turned_ref, extra_ref,
+):
+    for z in range(VZ):
+        for x in range(VX):
+            turned_ref[z, x] = latent_ref[x, :, z, :]
+    mask = row_mask(act_ref)
+    gain = gain_ref[...].reshape(1, 1, CH)
+
+    def normed(values, flags):
+        scale = lax.rsqrt(jnp.mean(values * values, axis=-1, keepdims=True) + 1e-06)
+        return (flags * values * scale * gain).astype(BF16)
+
+    for side, ref in ((0, xa_ref), (VX - 1, xb_ref)):
+        ref[...] = normed(turned_ref[:, side], mask[side][None])
+    for side, ref in ((0, ya_ref), (VY - 1, yb_ref)):
+        ref[...] = normed(turned_ref[:, :, side, :], mask[:, side, :][None])
     row = lax.broadcasted_iota(jnp.int32, (16, LANES), 0)
     lane = lax.broadcasted_iota(jnp.int32, (16, LANES), 1)
     for s in range(ACT_MAX):
@@ -72,25 +92,6 @@
                 code = jnp.where(here, code, -1).astype(F32)
                 extra = jnp.where((row == 0) & (lane == p), jnp.maximum(extra, code), extra)
         extra_ref[s] = extra.astype(BF16)
-
-
-def face_kernel(
-    act_ref, latent_ref, gain_ref, xa_ref, xb_ref, ya_ref, yb_ref, turned_ref
-):
-    for z in range(VZ):
-        for x in range(VX):
-            turned_ref[z, x] = latent_ref[x, :, z, :]
-    mask = row_mask(act_ref)
-    gain = gain_ref[...].reshape(1, 1, CH)
-
-    def normed(values, flags):
-        scale = lax.rsqrt(jnp.mean(values * values, axis=-1, keepdims=True) + 1e-06)
-        return (flags * values * scale * gain).astype(BF16)
-
-    for side, ref in ((0, xa_ref), (VX - 1, xb_ref)):
-        ref[...] = normed(turned_ref[:, side], mask[side][None])
-    for side, ref in ((0, ya_ref), (VY - 1, yb_ref)):
-        ref[...] = normed(turned_ref[:, :, side, :], mask[:, side, :][None])
 
 
 def edge_kernel(xlo_ref, xhi_ref, ya_ref, yb_ref, outa_ref, outb_ref):
@@ -365,25 +366,25 @@
 
     face = jax.ShapeDtypeStruct((VZ, VX, CH), BF16)
     vectors = [one.reshape(1, CH) for one in (norm_gain, conv_bias, attn_gain)]
-    extra = pl.pallas_call(
-        table_kernel,
-        out_shape=jax.ShapeDtypeStruct((ACT_MAX, PACK - LANES, LANES), BF16),
-        in_specs=[SMEM] * 3 + [ANY] * 6,
+    near = pl.pallas_call(
+        near_kernel,
+        out_shape=jax.ShapeDtypeStruct((8, LANES), F32),
+        in_specs=[ANY] * 6,
         out_specs=VMEM,
         compiler_params=pltpu.CompilerParams(vmem_limit_bytes=60 << 20),
-        name="tables",
-    )(active, parent_owner, parent_slot, *vectors, conv_weight, q_weight, latent)
-    vectors[0] = after(vectors[0], extra)
-    x_first, x_last, y_first, y_last, turned = pl.pallas_call(
+        name="near",
+    )(*vectors, conv_weight, q_weight, latent)
+    x_first, x_last, y_first, y_last, turned, extra = pl.pallas_call(
         face_kernel,
         out_shape=[face] * 4 + [
             jax.ShapeDtypeStruct((VZ, VX, VY, CH), F32),
+            jax.ShapeDtypeStruct((ACT_MAX, PACK - LANES, LANES), BF16),
         ],
-        in_specs=[SMEM] + [VMEM] * 2,
-        out_specs=[VMEM] * 5,
+        in_specs=[SMEM] * 3 + [VMEM] * 2 + [ANY],
+        out_specs=[VMEM] * 6,
         compiler_params=pltpu.CompilerParams(vmem_limit_bytes=6 << 20),
         name="faces",
-    )(active, latent, vectors[0])
+    )(active, parent_owner, parent_slot, latent, vectors[0], near)
     b1 = ringed(after(b0, x_first, x_last))
     x_low, x_high = shift(x_last, "gx", 1), shift(x_first, "gx", -1)
     a2, b2 = ringed(after(a1, x_low, x_high)), ringed(after(b1, x_low, x_high))

time: 79.4 us -> 78.4 us (0.987)
  Pallas kernels: 16 us -> 14.5 us
  starting transfers between devices: 34.9 us -> 35.7 us
    pallas_call x1, Pallas kernels: 1.55 us -> 0.6 us  [per_device(): pl.pallas_call(near_kernel, out_shape=jax.ShapeDtypeStruct((8, LANES), F3...]
    unnamed x47 -> x49, local copies, waits for them, and re-layouts: 3.74 us -> 3.48 us
  transfers between devices with their start and end apart: 25 -> 25, of which waited for: 13 -> 12; matrix products, arithmetic and copies ran while one was open for 2% -> 1% of each run, Pallas kernels for 7% -> 6%
where the time goes in v6:
time: 78.4 us; the launch traced here: 77.4 us
  starting transfers between devices  35.7 us (46%)
  waiting for transfers between devices  23.5 us (30%)
  Pallas kernels  14.5 us (18%)
  local copies, waits for them, and re-layouts  3.48 us (4%)
    ppermute x21, starting transfers between devices, move(): return lax.ppermute(block, 'gx', pairs)  23.8 us
    ppermute x21, waiting for transfers between devices, move(): return lax.ppermute(block, 'gx', pairs)  18.4 us
    ppermute x4, starting transfers between devices, shift(): lax.ppermute(block, axis, [(i, i + step) for i in range(count) if 0 <= i...  11.9 us
    pallas_call x1, Pallas kernels, per_device(): pl.pallas_call(attend_kernel, out_shape=[jax.ShapeDtypeStruct((ACT_MAX, P...  7.45 us
    ppermute x4, waiting for transfers between devices, shift(): lax.ppermute(block, axis, [(i, i + step) for i in range(count) if 0 <= i...  5.1 us
    unnamed x49, local copies, waits for them, and re-layouts  3.48 us
    pallas_call x1, Pallas kernels, per_device(): pl.pallas_call(conv_kernel, out_shape=(jax.ShapeDtypeStruct((ROWS, CH), F...  3.46 us
    pallas_call x1, Pallas kernels, per_device(): pl.pallas_call(merge_kernel, out_shape=jax.ShapeDtypeStruct((VX, VY, VZ,...  2.12 us
  transfers between devices with their start and end apart: 25, of which 12 were waited for; matrix products, arithmetic and copies ran while one was open for 1% of the time, Pallas kernels for 6%

profile of v6, /device:TPU:2, one launch (start us, length us, event | category | flops | bytes accessed | tf_op | source)
XLA Modules:
  0.0 77.4 jit_solution(4969735047936228974)
XLA Ops:
  0.1 2.0 %collective-permute-start.2 = (bf16[4,128,512]{2,1,0:T(8,128)(2,1)}, bf16[4,128,512]{2,1,0:T(8,128)(2,1)}, u32[]{:S(2)}, u32[]{:S(2)}) collective-permute-start(bf16[4,128,512]{2,1,0:T(8,128)(2,1)} %refs_4_.3), channel_id=1, source_target_pairs={{0,32},{4,228},{8,40},{12,236},{16,48},{20,244},{24,56},{28,252},{... | collective-permute-start | bytes 1572872 | tf_op jit(solution)/shard_map/ppermute | solution.py:352
  2.1 0.8 copy.14.act_ref
  4.5 0.9 %faces.1 = (bf16[4,8,256]{2,1,0:T(8,128)(2,1)S(1)}, bf16[4,8,256]{2,1,0:T(8,128)(2,1)S(1)}, bf16[4,8,256]{2,1,0:T(8,128)(2,1)S(1)}, bf16[4,8,256]{2,1,0:T(8,128)...) custom-call(s32[2,2,1]{2,1,0:T(2,128)S(1)} %copy.14.act_ref, s32[1,1,4,4]{3,2,1,0:T(4,128)S(1)} %copy-done.12, ...), custom_call_target="tpu_custom_call" | custom-call | tf_op jit(solution)/shard_map/faces/pallas_call | solution.py:377
  5.4 2.0 %collective-permute-start.4 = (bf16[4,128,512]{2,1,0:T(8,128)(2,1)}, bf16[4,128,512]{2,1,0:T(8,128)(2,1)}, u32[]{:S(2)}, u32[]{:S(2)}) collective-permute-start(bf16[4,128,512]{2,1,0:T(8,128)(2,1)} %collective-permute-done.3.refs_9_), channel_id=1, source_target_pairs={{0,32},{4,228},{8,40},{12,236},{16,48},{20,244},{24,56},{28,252},{... | collective-permute-start | bytes 1572872 | tf_op jit(solution)/shard_map/ppermute | solution.py:352
  7.4 4.8 %collective-permute-start = (bf16[4,8,256]{2,1,0:T(8,128)(2,1)S(1)}, bf16[4,8,256]{2,1,0:T(8,128)(2,1)S(1)}, u32[]{:S(2)}, u32[]{:S(2)}) collective-permute-start(bf16[4,8,256]{2,1,0:T(8,128)(2,1)S(1)} %get-tuple-element.37), channel_id=1, source_target_pairs={{0,4},{4,8},{8,12},{12,16},{16,20},{20,24},{24,28},{28,32},{32,36}... | collective-permute-start | bytes 49160 | tf_op jit(solution)/shard_map/ppermute | solution.py:340
  12.2 1.3 %collective-permute-start.1 = (bf16[4,8,256]{2,1,0:T(8,128)(2,1)S(1)}, bf16[4,8,256]{2,1,0:T(8,128)(2,1)S(1)}, u32[]{:S(2)}, u32[]{:S(2)}) collective-permute-start(bf16[4,8,256]{2,1,0:T(8,128)(2,1)S(1)} %get-tuple-element.38), channel_id=1, source_target_pairs={{4,0},{8,4},{12,8},{16,12},{20,16},{24,20},{28,24},{32,28},{36,32}... | collective-permute-start | bytes 49160 | tf_op jit(solution)/shard_map/ppermute | solution.py:340
  13.5 1.8 %collective-permute-done.1.xhi_ref = bf16[4,8,256]{2,1,0:T(8,128)(2,1)S(1)} collective-permute-done((bf16[4,8,256]{2,1,0:T(8,128)(2,1)S(1)}, bf16[4,8,256]{2,1,0:T(8,128)(2,1)S(1)}, u32[]{:S(2)}, u32[]{:S(2)}) %collective-permute-start.1) | collective-permute-done | bytes 16416 | tf_op jit(solution)/shard_map/ppermute | solution.py:340
  15.3 4.4 %collective-permute-start.7 = (bf16[4,128,512]{2,1,0:T(8,128)(2,1)}, bf16[4,128,512]{2,1,0:T(8,128)(2,1)S(1)}, u32[]{:S(2)}, u32[]{:S(2)}) collective-permute-start(bf16[4,128,512]{2,1,0:T(8,128)(2,1)} %collective-permute-done.2.refs_5_), channel_id=1, source_target_pairs={{0,32},{4,228},{8,40},{12,236},{16,48},{20,244},{24,56},{28,252},{... | collective-permute-start | bytes 1572872 | tf_op jit(solution)/shard_map/ppermute | solution.py:352
  19.6 1.9 %collective-permute-start.8 = (bf16[4,128,512]{2,1,0:T(8,128)(2,1)}, bf16[4,128,512]{2,1,0:T(8,128)(2,1)}, u32[]{:S(2)}, u32[]{:S(2)}) collective-permute-start(bf16[4,128,512]{2,1,0:T(8,128)(2,1)} %collective-permute-done.4.refs_10_), channel_id=1, source_target_pairs={{0,32},{4,228},{8,40},{12,236},{16,48},{20,244},{24,56},{28,252},{... | collective-permute-start | bytes 1572872 | tf_op jit(solution)/shard_map/ppermute | solution.py:352
  21.6 3.4 %collective-permute-start.5 = (bf16[4,16,256]{2,1,0:T(8,128)(2,1)S(1)}, bf16[4,16,256]{2,1,0:T(8,128)(2,1)S(1)}, u32[]{:S(2)}, u32[]{:S(2)}) collective-permute-start(bf16[4,16,256]{2,1,0:T(8,128)(2,1)S(1)} %get-tuple-element.44), channel_id=1, source_target_pairs={{0,1},{1,2},{2,3},{4,5},{5,6},{6,7},{8,9},{9,10},{10,11},{12,13},{... | collective-permute-start | bytes 98312 | tf_op jit(solution)/shard_map/ppermute | solution.py:340
  25.0 2.4 %collective-permute-start.6 = (bf16[4,16,256]{2,1,0:T(8,128)(2,1)S(1)}, bf16[4,16,256]{2,1,0:T(8,128)(2,1)S(1)}, u32[]{:S(2)}, u32[]{:S(2)}) collective-permute-start(bf16[4,16,256]{2,1,0:T(8,128)(2,1)S(1)} %get-tuple-element.45), channel_id=1, source_target_pairs={{1,0},{2,1},{3,2},{5,4},{6,5},{7,6},{9,8},{10,9},{11,10},{13,12},{... | collective-permute-start | bytes 98312 | tf_op jit(solution)/shard_map/ppermute | solution.py:340
  27.5 3.3 %collective-permute-done.6.yhi_ref = bf16[4,16,256]{2,1,0:T(8,128)(2,1)S(1)} collective-permute-done((bf16[4,16,256]{2,1,0:T(8,128)(2,1)S(1)}, bf16[4,16,256]{2,1,0:T(8,128)(2,1)S(1)}, u32[]{:S(2)}, u32[]{:S(2)}) %collective-permute-start.6) | collective-permute-done | bytes 32800 | tf_op jit(solution)/shard_map/ppermute | solution.py:340
  30.8 1.0 %collective-permute-start.12 = (bf16[4,128,512]{2,1,0:T(8,128)(2,1)S(1)}, bf16[4,128,512]{2,1,0:T(8,128)(2,1)}, u32[]{:S(2)}, u32[]{:S(2)}) collective-permute-start(bf16[4,128,512]{2,1,0:T(8,128)(2,1)S(1)} %collective-permute-done.7.refs_6_), channel_id=1, source_target_pairs={{0,32},{4,228},{8,40},{12,236},{16,48},{20,244},{24,56},{28,252},{... | collective-permute-start | bytes 1572872 | tf_op jit(solution)/shard_map/ppermute | solution.py:352
  31.8 3.5 %conv.1 = (f32[256,256]{1,0:T(8,128)S(1)}, bf16[3,144,128]{2,1,0:T(8,128)(2,1)S(1)}) custom-call(s32[2,2,1]{2,1,0:T(2,128)S(1)} %copy.14.act_ref, f32[4,8,8,256]{3,2,1,0:T(8,128)S(1)} %get-tuple-element.36.latent_ref, bf16[4,8,256]{2,1,0:T(8,128)(2,1)S(1)} %collective-permute-done.xlo_ref, bf16[4,8,256]{2,1,0:T(8,128)(2,1)S(1)} %collective-permute-done.1.xhi_ref, ...), custom_call_target="tpu_custom_call" | custom-call | flops 905969664 | bytes 5242880 | tf_op jit(solution)/shard_map/conv/pallas_call | solution.py:404
  36.0 2.4 %collective-permute-start.14 = (bf16[4,128,512]{2,1,0:T(8,128)(2,1)}, bf16[4,128,512]{2,1,0:T(8,128)(2,1)S(1)}, u32[]{:S(2)}, u32[]{:S(2)}) collective-permute-start(bf16[4,128,512]{2,1,0:T(8,128)(2,1)} %collective-permute-done.8.refs_11_), channel_id=1, source_target_pairs={{0,32},{4,228},{8,40},{12,236},{16,48},{20,244},{24,56},{28,252},{... | collective-permute-start | bytes 1572872 | tf_op jit(solution)/shard_map/ppermute | solution.py:352
  39.0 1.4 %collective-permute-start.9 = (bf16[3,144,128]{2,1,0:T(8,128)(2,1)S(1)}, bf16[3,144,128]{2,1,0:T(8,128)(2,1)S(1)}, u32[]{:S(2)}, u32[]{:S(2)}) collective-permute-start(bf16[3,144,128]{2,1,0:T(8,128)(2,1)S(1)} %get-tuple-element.51.refs_0_), channel_id=1, source_target_pairs={{0,8},{4,12},{8,16},{12,20},{16,24},{20,28},{24,0},{28,4},{32,40},... | collective-permute-start | bytes 331784 | tf_op jit(solution)/shard_map/ppermute | solution.py:352
  40.4 0.9 %collective-permute-done.12.refs_7_ = bf16[4,128,512]{2,1,0:T(8,128)(2,1)} collective-permute-done((bf16[4,128,512]{2,1,0:T(8,128)(2,1)S(1)}, bf16[4,128,512]{2,1,0:T(8,128)(2,1)}, u32[]{:S(2)}, u32[]{:S(2)}) %collective-permute-start.12) | collective-permute-done | bytes 524320 | tf_op jit(solution)/shard_map/ppermute | solution.py:352
  41.3 2.0 %collective-permute-start.13 = (bf16[4,128,512]{2,1,0:T(8,128)(2,1)}, bf16[4,128,512]{2,1,0:T(8,128)(2,1)S(1)}, u32[]{:S(2)}, u32[]{:S(2)}) collective-permute-start(bf16[4,128,512]{2,1,0:T(8,128)(2,1)} %collective-permute-done.12.refs_7_), channel_id=1, source_target_pairs={{0,32},{4,228},{8,40},{12,236},{16,48},{20,244},{24,56},{28,252},{... | collective-permute-start | bytes 1572872 | tf_op jit(solution)/shard_map/ppermute | solution.py:352
  43.3 2.6 %collective-permute-done.10.refs_2_ = bf16[3,144,128]{2,1,0:T(8,128)(2,1)S(1)} collective-permute-done((bf16[3,144,128]{2,1,0:T(8,128)(2,1)S(1)}, bf16[3,144,128]{2,1,0:T(8,128)(2,1)S(1)}, u32[]{:S(2)}, u32[]{:S(2)}) %collective-permute-start.10) | collective-permute-done | bytes 110624 | tf_op jit(solution)/shard_map/ppermute | solution.py:352
  45.9 0.8 %collective-permute-done.9.refs_1_ = bf16[3,144,128]{2,1,0:T(8,128)(2,1)S(1)} collective-permute-done((bf16[3,144,128]{2,1,0:T(8,128)(2,1)S(1)}, bf16[3,144,128]{2,1,0:T(8,128)(2,1)S(1)}, u32[]{:S(2)}, u32[]{:S(2)}) %collective-permute-start.9) | collective-permute-done | bytes 110624 | tf_op jit(solution)/shard_map/ppermute | solution.py:352
  47.9 4.6 %collective-permute-done.13.refs_8_ = bf16[4,128,512]{2,1,0:T(8,128)(2,1)S(1)} collective-permute-done((bf16[4,128,512]{2,1,0:T(8,128)(2,1)}, bf16[4,128,512]{2,1,0:T(8,128)(2,1)S(1)}, u32[]{:S(2)}, u32[]{:S(2)}) %collective-permute-start.13) | collective-permute-done | bytes 524320 | tf_op jit(solution)/shard_map/ppermute | solution.py:352
  53.1 1.6 %collective-permute-done.20.refs_18_ = bf16[4,128,512]{2,1,0:T(8,128)(2,1)} collective-permute-done((bf16[4,128,512]{2,1,0:T(8,128)(2,1)}, bf16[4,128,512]{2,1,0:T(8,128)(2,1)}, u32[]{:S(2)}, u32[]{:S(2)}) %collective-permute-start.20) | collective-permute-done | bytes 524320 | tf_op jit(solution)/shard_map/ppermute | solution.py:352
  55.2 0.7 collective-permute-done.18.refs_16_
  56.1 7.4 %attend.1 = (bf16[3,144,128]{2,1,0:T(8,128)(2,1)}, bf16[3,144,128]{2,1,0:T(8,128)(2,1)}, bf16[3,144,128]{2,1,0:T(8,128)(2,1)}, bf16[3,144,128]{2,1,0:T(8,128)(2,1)}) custom-call(s32[1]{0:T(128)} %bitcast.here_ref, bf16[3,144,128]{2,1,0:T(8,128)(2,1)} %copy-done.6, bf16[3,144,128]{2,1,0:T(8,128)(2,1)} %copy-done.23, bf16[3,144,128]{2,1,0:T(8,128)(2,1)} %copy-done.22, ...), custom_call_target="tpu_custom_call" | custom-call | tf_op jit(solution)/shard_map/attend/pallas_call | solution.py:437
  63.5 2.0 %collective-permute-start.22 = (bf16[3,144,128]{2,1,0:T(8,128)(2,1)}, bf16[3,144,128]{2,1,0:T(8,128)(2,1)S(1)}, u32[]{:S(2)}, u32[]{:S(2)}) collective-permute-start(bf16[3,144,128]{2,1,0:T(8,128)(2,1)} %get-tuple-element.63), channel_id=1, source_target_pairs={{0,24},{4,28},{8,0},{12,4},{16,8},{20,12},{24,16},{28,20},{32,56},... | collective-permute-start | bytes 331784 | tf_op jit(solution)/shard_map/ppermute | solution.py:352
  65.6 1.1 %collective-permute-start.23 = (bf16[3,144,128]{2,1,0:T(8,128)(2,1)}, bf16[3,144,128]{2,1,0:T(8,128)(2,1)S(1)}, u32[]{:S(2)}, u32[]{:S(2)}) collective-permute-start(bf16[3,144,128]{2,1,0:T(8,128)(2,1)} %get-tuple-element.64), channel_id=1, source_target_pairs={{0,16},{4,20},{8,24},{12,28},{16,0},{20,4},{24,8},{28,12},{32,48},... | collective-permute-start | bytes 331784 | tf_op jit(solution)/shard_map/ppermute | solution.py:352
  66.7 1.1 %collective-permute-start.24 = (bf16[3,144,128]{2,1,0:T(8,128)(2,1)}, bf16[3,144,128]{2,1,0:T(8,128)(2,1)S(1)}, u32[]{:S(2)}, u32[]{:S(2)}) collective-permute-start(bf16[3,144,128]{2,1,0:T(8,128)(2,1)} %get-tuple-element.65), channel_id=1, source_target_pairs={{0,8},{4,12},{8,16},{12,20},{16,24},{20,28},{24,0},{28,4},{32,40},... | collective-permute-start | bytes 331784 | tf_op jit(solution)/shard_map/ppermute | solution.py:352
  67.8 1.0 %collective-permute-done.22.refs_1_ = bf16[3,144,128]{2,1,0:T(8,128)(2,1)S(1)} collective-permute-done((bf16[3,144,128]{2,1,0:T(8,128)(2,1)}, bf16[3,144,128]{2,1,0:T(8,128)(2,1)S(1)}, u32[]{:S(2)}, u32[]{:S(2)}) %collective-permute-start.22) | collective-permute-done | bytes 110624 | tf_op jit(solution)/shard_map/ppermute | solution.py:352
  68.8 4.1 %collective-permute-done.23.refs_2_ = bf16[3,144,128]{2,1,0:T(8,128)(2,1)S(1)} collective-permute-done((bf16[3,144,128]{2,1,0:T(8,128)(2,1)}, bf16[3,144,128]{2,1,0:T(8,128)(2,1)S(1)}, u32[]{:S(2)}, u32[]{:S(2)}) %collective-permute-start.23) | collective-permute-done | bytes 110624 | tf_op jit(solution)/shard_map/ppermute | solution.py:352
  72.9 1.5 %collective-permute-done.24.refs_3_ = bf16[3,144,128]{2,1,0:T(8,128)(2,1)S(1)} collective-permute-done((bf16[3,144,128]{2,1,0:T(8,128)(2,1)}, bf16[3,144,128]{2,1,0:T(8,128)(2,1)S(1)}, u32[]{:S(2)}, u32[]{:S(2)}) %collective-permute-start.24) | collective-permute-done | bytes 110624 | tf_op jit(solution)/shard_map/ppermute | solution.py:352
  74.4 0.9 %copy-done.7 = bf16[3,144,128]{2,1,0:T(8,128)(2,1)S(1)} copy-done((bf16[3,144,128]{2,1,0:T(8,128)(2,1)S(1)}, bf16[3,144,128]{2,1,0:T(8,128)(2,1)}, u32[]{:S(2)}) %copy-start.7) | copy-done | bytes 110616
  75.3 2.1 %merge.1 = f32[8,8,4,256]{3,2,1,0:T(4,128)} custom-call(s32[2,2,1]{2,1,0:T(2,128)S(1)} %copy.14.act_ref, bf16[3,144,128]{2,1,0:T(8,128)(2,1)S(1)} %copy-done.7, bf16[3,144,128]{2,1,0:T(8,128)(2,1)S(1)} %collective-permute-done.22.refs_1_, bf16[3,144,128]{2,1,0:T(8,128)(2,1)S(1)} %collective-permute-done.23.refs_2_, ...), custom_call_target="tpu_custom_call" | custom-call | tf_op jit(solution)/shard_map/merge/pallas_call | solution.py:459
  (73 shorter events, 5.4 us)
Async XLA Ops:
  0.0 31.8 %copy-start = (bf16[27,256,256]{2,1,0:T(8,128)(2,1)S(1)}, bf16[27,256,256]{2,1,0:T(8,128)(2,1)}, u32[]{:S(2)}) copy-start(bf16[27,256,256]{2,1,0:T(8,128)(2,1)} %weight_ref.1) | copy-start | bytes 10616836
  0.0 31.8 %copy-start.11 = (f32[256]{0:T(256)S(1)}, f32[256]{0:T(256)}, u32[]{:S(2)}) copy-start(f32[256]{0:T(256)} %param.19) | copy-start | bytes 3076
  0.0 31.8 %copy-start.10 = (f32[256]{0:T(256)S(1)}, f32[256]{0:T(256)}, u32[]{:S(2)}) copy-start(f32[256]{0:T(256)} %param.18) | copy-start | bytes 3076
  0.0 5.4 %collective-permute-start.3 = (bf16[4,128,512]{2,1,0:T(8,128)(2,1)}, bf16[4,128,512]{2,1,0:T(8,128)(2,1)}, u32[]{:S(2)}, u32[]{:S(2)}) collective-permute-start(bf16[4,128,512]{2,1,0:T(8,128)(2,1)} %refs_4_.3), channel_id=1, source_target_pairs={{0,4},{4,0},{8,12},{12,8},{16,20},{20,16},{24,28},{28,24},{32,36},... | collective-permute-start | bytes 1572872 | tf_op jit(solution)/shard_map/ppermute | solution.py:352
  0.1 15.1 %collective-permute-start.2 = (bf16[4,128,512]{2,1,0:T(8,128)(2,1)}, bf16[4,128,512]{2,1,0:T(8,128)(2,1)}, u32[]{:S(2)}, u32[]{:S(2)}) collective-permute-start(bf16[4,128,512]{2,1,0:T(8,128)(2,1)} %refs_4_.3), channel_id=1, source_target_pairs={{0,32},{4,228},{8,40},{12,236},{16,48},{20,244},{24,56},{28,252},{... | collective-permute-start | bytes 1572872 | tf_op jit(solution)/shard_map/ppermute | solution.py:352
  2.9 28.9 %copy-start.2 = (bf16[256,256]{1,0:T(8,128)(2,1)S(1)}, bf16[256,256]{1,0:T(8,128)(2,1)}, u32[]{:S(2)}) copy-start(bf16[256,256]{1,0:T(8,128)(2,1)} %qw_ref.1) | copy-start | bytes 393220
  5.4 14.2 %collective-permute-start.4 = (bf16[4,128,512]{2,1,0:T(8,128)(2,1)}, bf16[4,128,512]{2,1,0:T(8,128)(2,1)}, u32[]{:S(2)}, u32[]{:S(2)}) collective-permute-start(bf16[4,128,512]{2,1,0:T(8,128)(2,1)} %collective-permute-done.3.refs_9_), channel_id=1, source_target_pairs={{0,32},{4,228},{8,40},{12,236},{16,48},{20,244},{24,56},{28,252},{... | collective-permute-start | bytes 1572872 | tf_op jit(solution)/shard_map/ppermute | solution.py:352
  7.4 6.1 %collective-permute-start = (bf16[4,8,256]{2,1,0:T(8,128)(2,1)S(1)}, bf16[4,8,256]{2,1,0:T(8,128)(2,1)S(1)}, u32[]{:S(2)}, u32[]{:S(2)}) collective-permute-start(bf16[4,8,256]{2,1,0:T(8,128)(2,1)S(1)} %get-tuple-element.37), channel_id=1, source_target_pairs={{0,4},{4,8},{8,12},{12,16},{16,20},{20,24},{24,28},{28,32},{32,36}... | collective-permute-start | bytes 49160 | tf_op jit(solution)/shard_map/ppermute | solution.py:340
  12.2 3.1 %collective-permute-start.1 = (bf16[4,8,256]{2,1,0:T(8,128)(2,1)S(1)}, bf16[4,8,256]{2,1,0:T(8,128)(2,1)S(1)}, u32[]{:S(2)}, u32[]{:S(2)}) collective-permute-start(bf16[4,8,256]{2,1,0:T(8,128)(2,1)S(1)} %get-tuple-element.38), channel_id=1, source_target_pairs={{4,0},{8,4},{12,8},{16,12},{20,16},{24,20},{28,24},{32,28},{36,32}... | collective-permute-start | bytes 49160 | tf_op jit(solution)/shard_map/ppermute | solution.py:340
  15.3 12.2 %collective-permute-start.7 = (bf16[4,128,512]{2,1,0:T(8,128)(2,1)}, bf16[4,128,512]{2,1,0:T(8,128)(2,1)S(1)}, u32[]{:S(2)}, u32[]{:S(2)}) collective-permute-start(bf16[4,128,512]{2,1,0:T(8,128)(2,1)} %collective-permute-done.2.refs_5_), channel_id=1, source_target_pairs={{0,32},{4,228},{8,40},{12,236},{16,48},{20,244},{24,56},{28,252},{... | collective-permute-start | bytes 1572872 | tf_op jit(solution)/shard_map/ppermute | solution.py:352
  19.6 16.4 %collective-permute-start.8 = (bf16[4,128,512]{2,1,0:T(8,128)(2,1)}, bf16[4,128,512]{2,1,0:T(8,128)(2,1)}, u32[]{:S(2)}, u32[]{:S(2)}) collective-permute-start(bf16[4,128,512]{2,1,0:T(8,128)(2,1)} %collective-permute-done.4.refs_10_), channel_id=1, source_target_pairs={{0,32},{4,228},{8,40},{12,236},{16,48},{20,244},{24,56},{28,252},{... | collective-permute-start | bytes 1572872 | tf_op jit(solution)/shard_map/ppermute | solution.py:352
  21.6 5.9 %collective-permute-start.5 = (bf16[4,16,256]{2,1,0:T(8,128)(2,1)S(1)}, bf16[4,16,256]{2,1,0:T(8,128)(2,1)S(1)}, u32[]{:S(2)}, u32[]{:S(2)}) collective-permute-start(bf16[4,16,256]{2,1,0:T(8,128)(2,1)S(1)} %get-tuple-element.44), channel_id=1, source_target_pairs={{0,1},{1,2},{2,3},{4,5},{5,6},{6,7},{8,9},{9,10},{10,11},{12,13},{... | collective-permute-start | bytes 98312 | tf_op jit(solution)/shard_map/ppermute | solution.py:340
  25.0 5.8 %collective-permute-start.6 = (bf16[4,16,256]{2,1,0:T(8,128)(2,1)S(1)}, bf16[4,16,256]{2,1,0:T(8,128)(2,1)S(1)}, u32[]{:S(2)}, u32[]{:S(2)}) collective-permute-start(bf16[4,16,256]{2,1,0:T(8,128)(2,1)S(1)} %get-tuple-element.45), channel_id=1, source_target_pairs={{1,0},{2,1},{3,2},{5,4},{6,5},{7,6},{9,8},{10,9},{11,10},{13,12},{... | collective-permute-start | bytes 98312 | tf_op jit(solution)/shard_map/ppermute | solution.py:340
  27.4 19.4 %copy-start.14 = (bf16[4,128,512]{2,1,0:T(8,128)(2,1)}, bf16[4,128,512]{2,1,0:T(8,128)(2,1)S(1)}, u32[]{:S(2)}) copy-start(bf16[4,128,512]{2,1,0:T(8,128)(2,1)S(1)} %collective-permute-done.7.refs_6_) | copy-start | bytes 1572868
  30.8 10.5 %collective-permute-start.12 = (bf16[4,128,512]{2,1,0:T(8,128)(2,1)S(1)}, bf16[4,128,512]{2,1,0:T(8,128)(2,1)}, u32[]{:S(2)}, u32[]{:S(2)}) collective-permute-start(bf16[4,128,512]{2,1,0:T(8,128)(2,1)S(1)} %collective-permute-done.7.refs_6_), channel_id=1, source_target_pairs={{0,32},{4,228},{8,40},{12,236},{16,48},{20,244},{24,56},{28,252},{... | collective-permute-start | bytes 1572872 | tf_op jit(solution)/shard_map/ppermute | solution.py:352
  36.0 10.8 %collective-permute-start.14 = (bf16[4,128,512]{2,1,0:T(8,128)(2,1)}, bf16[4,128,512]{2,1,0:T(8,128)(2,1)S(1)}, u32[]{:S(2)}, u32[]{:S(2)}) collective-permute-start(bf16[4,128,512]{2,1,0:T(8,128)(2,1)} %collective-permute-done.8.refs_11_), channel_id=1, source_target_pairs={{0,32},{4,228},{8,40},{12,236},{16,48},{20,244},{24,56},{28,252},{... | collective-permute-start | bytes 1572872 | tf_op jit(solution)/shard_map/ppermute | solution.py:352
  38.4 4.9 %collective-permute-start.11 = (bf16[3,144,128]{2,1,0:T(8,128)(2,1)S(1)}, bf16[3,144,128]{2,1,0:T(8,128)(2,1)S(1)}, u32[]{:S(2)}, u32[]{:S(2)}) collective-permute-start(bf16[3,144,128]{2,1,0:T(8,128)(2,1)S(1)} %get-tuple-element.51.refs_0_), channel_id=1, source_target_pairs={{0,24},{4,28},{8,0},{12,4},{16,8},{20,12},{24,16},{28,20},{32,56},... | collective-permute-start | bytes 331784 | tf_op jit(solution)/shard_map/ppermute | solution.py:352
  38.5 7.4 %collective-permute-start.10 = (bf16[3,144,128]{2,1,0:T(8,128)(2,1)S(1)}, bf16[3,144,128]{2,1,0:T(8,128)(2,1)S(1)}, u32[]{:S(2)}, u32[]{:S(2)}) collective-permute-start(bf16[3,144,128]{2,1,0:T(8,128)(2,1)S(1)} %get-tuple-element.51.refs_0_), channel_id=1, source_target_pairs={{0,16},{4,20},{8,24},{12,28},{16,0},{20,4},{24,8},{28,12},{32,48},... | collective-permute-start | bytes 331784 | tf_op jit(solution)/shard_map/ppermute | solution.py:352
  39.0 7.7 %collective-permute-start.9 = (bf16[3,144,128]{2,1,0:T(8,128)(2,1)S(1)}, bf16[3,144,128]{2,1,0:T(8,128)(2,1)S(1)}, u32[]{:S(2)}, u32[]{:S(2)}) collective-permute-start(bf16[3,144,128]{2,1,0:T(8,128)(2,1)S(1)} %get-tuple-element.51.refs_0_), channel_id=1, source_target_pairs={{0,8},{4,12},{8,16},{12,20},{16,24},{20,28},{24,0},{28,4},{32,40},... | collective-permute-start | bytes 331784 | tf_op jit(solution)/shard_map/ppermute | solution.py:352
  41.3 11.1 %collective-permute-start.13 = (bf16[4,128,512]{2,1,0:T(8,128)(2,1)}, bf16[4,128,512]{2,1,0:T(8,128)(2,1)S(1)}, u32[]{:S(2)}, u32[]{:S(2)}) collective-permute-start(bf16[4,128,512]{2,1,0:T(8,128)(2,1)} %collective-permute-done.12.refs_7_), channel_id=1, source_target_pairs={{0,32},{4,228},{8,40},{12,236},{16,48},{20,244},{24,56},{28,252},{... | collective-permute-start | bytes 1572872 | tf_op jit(solution)/shard_map/ppermute | solution.py:352
  46.8 5.6 %collective-permute-start.15 = (bf16[4,128,512]{2,1,0:T(8,128)(2,1)}, bf16[4,128,512]{2,1,0:T(8,128)(2,1)S(1)}, u32[]{:S(2)}, u32[]{:S(2)}) collective-permute-start(bf16[4,128,512]{2,1,0:T(8,128)(2,1)} %collective-permute-done.2.refs_5_), channel_id=1, source_target_pairs={{0,4},{4,0},{8,12},{12,8},{16,20},{20,16},{24,28},{28,24},{32,36},... | collective-permute-start | bytes 1572872 | tf_op jit(solution)/shard_map/ppermute | solution.py:352
  46.9 6.1 %collective-permute-start.16 = (bf16[4,128,512]{2,1,0:T(8,128)(2,1)S(1)}, bf16[4,128,512]{2,1,0:T(8,128)(2,1)S(1)}, u32[]{:S(2)}, u32[]{:S(2)}) collective-permute-start(bf16[4,128,512]{2,1,0:T(8,128)(2,1)S(1)} %collective-permute-done.7.refs_6_), channel_id=1, source_target_pairs={{0,4},{4,0},{8,12},{12,8},{16,20},{20,16},{24,28},{28,24},{32,36},... | collective-permute-start | bytes 1572872 | tf_op jit(solution)/shard_map/ppermute | solution.py:352
  47.4 5.7 %collective-permute-start.17 = (bf16[4,128,512]{2,1,0:T(8,128)(2,1)}, bf16[4,128,512]{2,1,0:T(8,128)(2,1)S(1)}, u32[]{:S(2)}, u32[]{:S(2)}) collective-permute-start(bf16[4,128,512]{2,1,0:T(8,128)(2,1)} %collective-permute-done.12.refs_7_), channel_id=1, source_target_pairs={{0,4},{4,0},{8,12},{12,8},{16,20},{20,16},{24,28},{28,24},{32,36},... | collective-permute-start | bytes 1572872 | tf_op jit(solution)/shard_map/ppermute | solution.py:352
  47.5 5.6 %collective-permute-start.19 = (bf16[4,128,512]{2,1,0:T(8,128)(2,1)}, bf16[4,128,512]{2,1,0:T(8,128)(2,1)S(1)}, u32[]{:S(2)}, u32[]{:S(2)}) collective-permute-start(bf16[4,128,512]{2,1,0:T(8,128)(2,1)} %collective-permute-done.4.refs_10_), channel_id=1, source_target_pairs={{0,4},{4,0},{8,12},{12,8},{16,20},{20,16},{24,28},{28,24},{32,36},... | collective-permute-start | bytes 1572872 | tf_op jit(solution)/shard_map/ppermute | solution.py:352
  52.4 2.3 %collective-permute-start.20 = (bf16[4,128,512]{2,1,0:T(8,128)(2,1)}, bf16[4,128,512]{2,1,0:T(8,128)(2,1)}, u32[]{:S(2)}, u32[]{:S(2)}) collective-permute-start(bf16[4,128,512]{2,1,0:T(8,128)(2,1)} %collective-permute-done.8.refs_11_), channel_id=1, source_target_pairs={{0,4},{4,0},{8,12},{12,8},{16,20},{20,16},{24,28},{28,24},{32,36},... | collective-permute-start | bytes 1572872 | tf_op jit(solution)/shard_map/ppermute | solution.py:352
  52.4 2.8 %collective-permute-start.21 = (bf16[4,128,512]{2,1,0:T(8,128)(2,1)S(1)}, bf16[4,128,512]{2,1,0:T(8,128)(2,1)}, u32[]{:S(2)}, u32[]{:S(2)}) collective-permute-start(bf16[4,128,512]{2,1,0:T(8,128)(2,1)S(1)} %collective-permute-done.14.refs_12_), channel_id=1, source_target_pairs={{0,4},{4,0},{8,12},{12,8},{16,20},{20,16},{24,28},{28,24},{32,36},... | collective-permute-start | bytes 1572872 | tf_op jit(solution)/shard_map/ppermute | solution.py:352
  52.9 3.0 %collective-permute-start.18 = (bf16[4,128,512]{2,1,0:T(8,128)(2,1)S(1)}, bf16[4,128,512]{2,1,0:T(8,128)(2,1)}, u32[]{:S(2)}, u32[]{:S(2)}) collective-permute-start(bf16[4,128,512]{2,1,0:T(8,128)(2,1)S(1)} %collective-permute-done.13.refs_8_), channel_id=1, source_target_pairs={{0,4},{4,0},{8,12},{12,8},{16,20},{20,16},{24,28},{28,24},{32,36},... | collective-permute-start | bytes 1572872 | tf_op jit(solution)/shard_map/ppermute | solution.py:352
  56.0 18.4 %copy-start.4 = (f32[256,256]{1,0:T(8,128)S(1)}, f32[256,256]{1,0:T(8,128)}, u32[]{:S(2)}) copy-start(f32[256,256]{1,0:T(8,128)} %copy-done.3) | copy-start | bytes 786436
  56.0 18.4 %copy-start.5 = (bf16[256,256]{1,0:T(8,128)(2,1)S(1)}, bf16[256,256]{1,0:T(8,128)(2,1)}, u32[]{:S(2)}) copy-start(bf16[256,256]{1,0:T(8,128)(2,1)} %refs_5_.3) | copy-start | bytes 393220
  63.5 5.3 %collective-permute-start.22 = (bf16[3,144,128]{2,1,0:T(8,128)(2,1)}, bf16[3,144,128]{2,1,0:T(8,128)(2,1)S(1)}, u32[]{:S(2)}, u32[]{:S(2)}) collective-permute-start(bf16[3,144,128]{2,1,0:T(8,128)(2,1)} %get-tuple-element.63), channel_id=1, source_target_pairs={{0,24},{4,28},{8,0},{12,4},{16,8},{20,12},{24,16},{28,20},{32,56},... | collective-permute-start | bytes 331784 | tf_op jit(solution)/shard_map/ppermute | solution.py:352
  65.6 7.4 %collective-permute-start.23 = (bf16[3,144,128]{2,1,0:T(8,128)(2,1)}, bf16[3,144,128]{2,1,0:T(8,128)(2,1)S(1)}, u32[]{:S(2)}, u32[]{:S(2)}) collective-permute-start(bf16[3,144,128]{2,1,0:T(8,128)(2,1)} %get-tuple-element.64), channel_id=1, source_target_pairs={{0,16},{4,20},{8,24},{12,28},{16,0},{20,4},{24,8},{28,12},{32,48},... | collective-permute-start | bytes 331784 | tf_op jit(solution)/shard_map/ppermute | solution.py:352
  66.7 7.7 %collective-permute-start.24 = (bf16[3,144,128]{2,1,0:T(8,128)(2,1)}, bf16[3,144,128]{2,1,0:T(8,128)(2,1)S(1)}, u32[]{:S(2)}, u32[]{:S(2)}) collective-permute-start(bf16[3,144,128]{2,1,0:T(8,128)(2,1)} %get-tuple-element.65), channel_id=1, source_target_pairs={{0,8},{4,12},{8,16},{12,20},{16,24},{20,28},{24,0},{28,4},{32,40},... | collective-permute-start | bytes 331784 | tf_op jit(solution)/shard_map/ppermute | solution.py:352
  (17 other events, 68.9 us)
